TPU v7x, 512 devices: a whole 4x4x16 slice. The times are simulated.
512 devices in a mesh: rep: 16 (over z), exp: 32 (over y, x, core).
Axes of the slice: x: 4, y: 4, z: 16, core: 2. Of those that a mesh axis runs over, the one named last changes fastest.
Arguments:
- tokens: bfloat16 [256, 512, 512], P('rep', 'exp'), may hold values from -48 to 48
- gate: float32 [256, 512], P('rep', 'exp'), may hold values from 0.25 to 1
- route: int32 [16, 32, 256, 1], P('rep', 'exp'), may hold values from 0 to 31; in each aligned block of 256 rows (0 to 255, 256 to 511, ..., all dimensions but the last counted through in order) at most 12 rows name the same one
- cotangent: bfloat16 [256, 512, 512], P('rep', 'exp'), may hold values from -6 to 6
- w_qkv: bfloat16 [512, 1536], replicated, may hold values from -1 to 1
- w_proj: bfloat16 [512, 512], replicated, may hold values from -0.25 to 0.25
- w_up: bfloat16 [32, 2048, 512], P('exp', 'rep'), may hold values from -0.25 to 0.25
- w_down: bfloat16 [32, 2048, 512], P('exp', 'rep'), may hold values from -0.125 to 0.125
Outputs:
- layer_out: bfloat16 [256, 512, 512], P('rep', 'exp')
- input_grad: bfloat16 [256, 512, 512], P('rep', 'exp')
- grad_up: float32 [32, 2048, 512], P('exp', 'rep')
- grad_down: float32 [32, 2048, 512], P('exp', 'rep')
Inputs may be any that keep to these rules, and one draw needn't show every extreme that they name: `route`: among the tokens of one tile no expert is named more than 12 times.
All inputs are finite; a program needn't handle non-finite values.
Results may differ from a plain program's by a relative error of at most 0.018.
Values may be sent and summed in bfloat16 or wider, within the bound.
No kernel may reach another device: no remote copies, remote signals or barrier semaphores. Data moves between devices by JAX's collectives and lax.ppermute only.
A program may use at most 64 MiB of HBM per device.

v0:
```python
import math

import jax
import jax.numpy as jnp
from jax import lax
from jax.sharding import PartitionSpec as P

HEADS = 16


GELU_C = math.sqrt(2.0 / math.pi)
window_side = 8
margin_cells = 4


def padded(block, sides, width):
    for axis, dim in sides:
        count = lax.axis_size(axis)
        forward = [(i, i + 1) for i in range(count - 1)]
        backward = [(target, source) for source, target in forward]
        low = lax.ppermute(
            lax.slice_in_dim(block, block.shape[dim] - width, None, axis=dim), axis, forward
        )
        high = lax.ppermute(lax.slice_in_dim(block, 0, width, axis=dim), axis, backward)
        block = jnp.concatenate([low, block, high], axis=dim)
    return block


def sent_together(arrays, axis, dim, along):
    ends, at = ([], 0)
    for a in arrays[:-1]:
        at += a.shape[along]
        ends.append(at)
    both = jnp.concatenate(arrays, axis=along)
    return tuple(jnp.split(lax.all_gather(both, axis, axis=dim, tiled=True), ends, axis=along))


def in_one_piece(arrays, axis, split_dim, concat_dim, along):
    both = jnp.concatenate(arrays, axis=along)
    result, at, finished = (
        lax.all_to_all(both, axis, split_axis=split_dim, concat_axis=concat_dim, tiled=True),
        0,
        [],
    )
    for a in arrays:
        finished.append(lax.slice_in_dim(result, at, at + a.shape[along], axis=along))
        at += a.shape[along]
    return tuple(finished)


def sent_together_2(arrays, axis, dim, along):
    ends, at = ([], 0)
    for a in arrays[:-1]:
        at += a.shape[along]
        ends.append(at)
    both = jnp.concatenate(arrays, axis=along)
    return tuple(
        jnp.split(lax.psum_scatter(both, axis, scatter_dimension=dim, tiled=True), ends, axis=along)
    )


def gelu_tanh(inputs):
    return 0.5 * inputs * (1.0 + jnp.tanh(GELU_C * (inputs + 0.044715 * inputs * inputs * inputs)))


def gelu_slope(inputs):
    inner = jnp.tanh(GELU_C * (inputs + 0.044715 * inputs * inputs * inputs))
    return 0.5 * (1.0 + inner) + 0.5 * inputs * (1.0 - inner * inner) * GELU_C * (
        1.0 + 3.0 * 0.044715 * inputs * inputs
    )


def layer_norm(values):
    average = jnp.mean(values, axis=-1, keepdims=True)
    centred = values - average
    spread = jnp.mean(centred * centred, axis=-1, keepdims=True)
    return centred * lax.rsqrt(spread + 1e-05)


def window_attend(qkv, in_grid):
    ext_rows, ext_cols, triple = qkv.shape
    feature = triple // 3
    head_size = feature // HEADS
    win_rows = ext_rows // window_side
    win_cols = ext_cols // window_side
    cells = window_side * window_side
    blocks = qkv.reshape(win_rows, window_side, win_cols, window_side, triple).transpose(
        0, 2, 1, 3, 4
    )
    blocks = blocks.reshape(win_rows * win_cols, cells, 3, HEADS, head_size)
    present = (
        in_grid.reshape(win_rows, window_side, win_cols, window_side)
        .transpose(0, 2, 1, 3)
        .reshape(win_rows * win_cols, cells)
    )
    scores = jnp.einsum(
        "wqhd,wkhd->whqk", blocks[:, :, 0], blocks[:, :, 1], preferred_element_type=jnp.float32
    ) / math.sqrt(head_size)
    scores = jnp.where(present[:, None, None, :], scores, jnp.float32(-1e30))
    peak_score = jnp.max(scores, axis=-1, keepdims=True)
    weights = jnp.exp(scores - peak_score)
    probabilities = (weights / jnp.sum(weights, axis=-1, keepdims=True)).astype(jnp.bfloat16)
    context = jnp.einsum(
        "whqk,wkhd->wqhd", probabilities, blocks[:, :, 2], preferred_element_type=jnp.float32
    ).astype(jnp.bfloat16)
    context = context.reshape(win_rows, win_cols, window_side, window_side, feature).transpose(
        0, 2, 1, 3, 4
    )
    return context.reshape(ext_rows, ext_cols, feature)


def per_device(tokens, gate, route, cotangent, w_qkv, w_proj, w_up, w_down):
    tile_rows, tile_cols, feature = tokens.shape
    tok_count = tile_rows * tile_cols
    ext_rows = tile_rows + 2 * margin_cells
    ext_cols = tile_cols + 2 * margin_cells
    extended = padded(tokens, (("rep", 0), ("exp", 1)), 4)
    qkv = jnp.dot(extended.reshape(-1, feature), w_qkv, preferred_element_type=jnp.float32).astype(
        jnp.bfloat16
    )
    qkv = qkv.reshape(ext_rows, ext_cols, 3 * feature)
    row_ids = (
        lax.axis_index("rep") * tile_rows - margin_cells + jnp.arange(ext_rows, dtype=jnp.int32)
    )
    col_ids = (
        lax.axis_index("exp") * tile_cols - margin_cells + jnp.arange(ext_cols, dtype=jnp.int32)
    )
    row_inside = (row_ids >= 0) & (row_ids < tile_rows * lax.axis_size("rep"))
    col_inside = (col_ids >= 0) & (col_ids < tile_cols * lax.axis_size("exp"))
    in_grid = row_inside[:, None] & col_inside[None, :]
    context = window_attend(qkv, in_grid)[
        margin_cells : tile_rows + margin_cells, margin_cells : tile_cols + margin_cells
    ].reshape(tok_count, feature)
    attended = jnp.dot(context, w_proj, preferred_element_type=jnp.float32)
    flat_tokens = tokens.reshape(tok_count, feature)
    mixed = (flat_tokens.astype(jnp.float32) + layer_norm(attended)).astype(jnp.bfloat16)
    experts = lax.axis_size("exp")
    capacity = max(2, 3 * tok_count // (2 * experts))
    chosen = route.reshape(tok_count)
    matches = (chosen[:, None] == jnp.arange(experts, dtype=jnp.int32)[None, :]).astype(jnp.int32)
    position = jnp.sum(matches * (jnp.cumsum(matches, axis=0) - 1), axis=1)
    target = chosen * capacity + position
    placer = (target[:, None] == jnp.arange(experts * capacity, dtype=jnp.int32)[None, :]).astype(
        jnp.bfloat16
    )
    gate_rows = gate.reshape(tok_count)
    upstream = (
        gate_rows[:, None] * cotangent.reshape(tok_count, feature).astype(jnp.float32)
    ).astype(jnp.bfloat16)

    def to_slots(values):
        placed = lax.dot_general(
            placer, values, (((0,), (0,)), ((), ())), preferred_element_type=jnp.float32
        )
        return placed.astype(jnp.bfloat16).reshape(experts, capacity, feature)

    def from_slots(slot_values):
        return jnp.dot(
            placer,
            slot_values.reshape(experts * capacity, feature),
            preferred_element_type=jnp.float32,
        )

    up_whole, down_whole = sent_together((w_up, w_down), "rep", 1, 0)
    up_mat = up_whole[0]
    down_mat = down_whole[0]

    def forward(sent_x):
        slot_rows = sent_x.reshape(-1, feature)
        pre_act = lax.dot_general(
            slot_rows, up_mat, (((1,), (1,)), ((), ())), preferred_element_type=jnp.float32
        )
        hidden = gelu_tanh(pre_act).astype(jnp.bfloat16)
        expert_out = jnp.dot(hidden, down_mat, preferred_element_type=jnp.float32).astype(
            jnp.bfloat16
        )
        return (slot_rows, pre_act, hidden, expert_out.reshape(-1, capacity, feature))

    def backward(pre_act, sent_g):
        slot_grads = sent_g.reshape(-1, feature)
        hidden_grad = lax.dot_general(
            slot_grads, down_mat, (((1,), (1,)), ((), ())), preferred_element_type=jnp.float32
        )
        pre_grad = (hidden_grad * gelu_slope(pre_act)).astype(jnp.bfloat16)
        input_slots = jnp.dot(pre_grad, up_mat, preferred_element_type=jnp.float32).astype(
            jnp.bfloat16
        )
        return (slot_grads, pre_grad, input_slots.reshape(-1, capacity, feature))

    sent_x, sent_g = in_one_piece((to_slots(mixed), to_slots(upstream)), "exp", 0, 0, 1)
    slot_rows, pre_act, hidden, expert_out = forward(sent_x)
    slot_grads, pre_grad, input_slots = backward(pre_act, sent_g)
    back_out, back_grad = in_one_piece((expert_out, input_slots), "exp", 0, 0, 1)
    layer_out = (mixed.astype(jnp.float32) + gate_rows[:, None] * from_slots(back_out)).astype(
        jnp.bfloat16
    )
    input_grad = from_slots(back_grad).astype(jnp.bfloat16)
    full_up = lax.dot_general(
        pre_grad, slot_rows, (((0,), (0,)), ((), ())), preferred_element_type=jnp.float32
    )
    full_down = lax.dot_general(
        hidden, slot_grads, (((0,), (0,)), ((), ())), preferred_element_type=jnp.float32
    )
    grad_up_rows, grad_down_rows = tuple(
        (
            part.astype(jnp.float32)
            for part in sent_together_2(
                (full_up.astype(jnp.bfloat16), full_down.astype(jnp.bfloat16)), "rep", 0, 1
            )
        )
    )
    average_factor = 1.0 / lax.axis_size("rep")
    return (
        layer_out.reshape(tile_rows, tile_cols, feature),
        input_grad.reshape(tile_rows, tile_cols, feature),
        (grad_up_rows * average_factor)[None],
        (grad_down_rows * average_factor)[None],
    )


def solution(mesh):
    placed = (
        P("rep", "exp", None),
        P("rep", "exp"),
        P("rep", "exp", None, None),
        P("rep", "exp", None),
        P(),
        P(),
        P("exp", "rep", None),
        P("exp", "rep", None),
    )
    return jax.shard_map(
        per_device,
        mesh=mesh,
        in_specs=placed,
        out_specs=(
            P("rep", "exp", None),
            P("rep", "exp", None),
            P("exp", "rep", None),
            P("exp", "rep", None),
        ),
        check_vma=False,
    )
```

profile of v0, /device:TPU:6, one launch (start us, length us, event | category | flops | bytes accessed | tf_op | source)
XLA Modules:
  0.0 203.9 jit_solution(18179986279111986893)
XLA Ops:
  7.2 1.8 pad_maximum_fusion.4
  9.1 0.9 fusion.52
  10.0 3.8 %collective-permute-start = (bf16[4,16,512]{2,1,0:T(8,128)(2,1)S(1)}, bf16[4,16,512]{2,1,0:T(8,128)(2,1)S(1)}, u32[]{:S(2)}, u32[]{:S(2)}) collective-permute-start(bf16[4,16,512]{2,1,0:T(8,128)(2,1)S(1)} %get-tuple-element.28), channel_id=1, source_target_pairs={{0,32},{32,64},{64,96},{96,128},{128,160},{160,192},{192,224},{224... | collective-permute-start | bytes 196616 | tf_op jit(solution)/shard_map/ppermute | solution.py:21
  13.8 1.3 collective-permute-start.1
  15.1 0.8 mul.107
  15.9 0.7 fusion.36
  16.6 0.6 reduce-window.6
  17.2 0.2 slice_reduce_fusion
  17.4 0.8 fusion.35
  18.2 0.7 multiply_add_fusion.2
  18.9 1.4 convolution_convert_fusion.3
  20.3 1.0 constant_dynamic-update-slice_fusion.1
  21.4 1.9 collective-permute-start.3
  23.3 2.4 %collective-permute-start.2 = (bf16[24,4,512]{2,1,0:T(4,128)(2,1)S(1)}, bf16[24,4,512]{2,1,0:T(4,128)(2,1)S(1)}, u32[]{:S(2)}, u32[]{:S(2)}) collective-permute-start(bf16[24,4,512]{2,1,0:T(4,128)(2,1)S(1)} %get-tuple-element.23), channel_id=1, source_target_pairs={{0,1},{1,2},{2,3},{3,4},{4,5},{5,6},{6,7},{7,8},{8,9},{9,10},{10,1... | collective-permute-start | bytes 294920 | tf_op jit(solution)/shard_map/ppermute | solution.py:21
  25.8 0.9 reshape.141
  26.7 0.1 and.40
  26.8 2.4 %collective-permute-done.2 = bf16[24,4,512]{2,1,0:T(4,128)(2,1)S(1)} collective-permute-done((bf16[24,4,512]{2,1,0:T(4,128)(2,1)S(1)}, bf16[24,4,512]{2,1,0:T(4,128)(2,1)S(1)}, u32[]{:S(2)}, u32[]{:S(2)}) %collective-permute-start.2) | collective-permute-done | bytes 98336 | tf_op jit(solution)/shard_map/ppermute | solution.py:21
  29.2 0.3 pad_maximum_fusion.3
  29.5 1.1 convolution_convert_fusion
  30.6 0.2 copy.46
  30.8 6.6 %reshape.134 = bf16[9,64,3,16,32]{4,3,2,1,0:T(8,128)(2,1)} reshape(bf16[3,3,8,8,1536]{4,3,2,1,0:T(8,128)(2,1)S(1)} %bitcast.79) | data formatting | bytes 3538944 | tf_op jit(solution)/shard_map/reshape | solution.py:90
  37.4 6.9 %fusion.47 = (bf16[9,64,1,16,32]{4,3,2,1,0:T(8,128)(2,1)}, bf16[9,64,1,16,32]{4,3,2,1,0:T(8,128)(2,1)}, bf16[9,64,1,16,32]{4,3,2,1,0:T(8,128)(2,1)}) fusion(bf16[9,64,3,16,32]{4,3,2,1,0:T(8,128)(2,1)} %reshape.134), kind=kLoop, calls=%fused_computation.86 | loop fusion | bytes 3538944 | tf_op jit(solution)/shard_map/slice | solution.py:104
  44.3 3.5 %copy.40 = bf16[9,64,1,16,32]{1,4,3,0,2:T(8,128)(2,1)S(1)} copy(bf16[9,64,1,16,32]{4,3,2,1,0:T(8,128)(2,1)} %get-tuple-element.18) | data formatting | bytes 1179648
  47.8 3.5 %copy.39 = bf16[9,64,1,16,32]{1,4,3,0,2:T(8,128)(2,1)S(1)} copy(bf16[9,64,1,16,32]{4,3,2,1,0:T(8,128)(2,1)} %get-tuple-element.17) | data formatting | bytes 1179648
  51.4 4.3 %copy.38 = bf16[9,64,1,16,32]{1,4,3,0,2:T(8,128)(2,1)} copy(bf16[9,64,1,16,32]{4,3,2,1,0:T(8,128)(2,1)} %get-tuple-element.16) | data formatting | bytes 1179648
  55.7 0.8 fusion.22
  56.5 2.6 %fusion.53 = (f32[9,16,64]{2,1,0:T(8,128)S(1)}, f32[9,16,64,64]{2,3,1,0:T(8,128)S(1)}) fusion(f32[9,16,64,64]{2,3,1,0:T(8,128)S(1)} %fusion.22, pred[9,64]{1,0:T(8,128)(4,1)S(1)} %and.40), kind=kOutput, calls=%fused_computation.92 | output fusion | flops 3539007 | bytes 4756032 | tf_op jit(solution)/shard_map/sub | solution.py:101
  59.1 0.8 fusion.17
  59.9 3.0 %copy.30 = bf16[9,64,16,32]{3,2,1,0:T(8,128)(2,1)} copy(bf16[9,64,16,32]{1,3,2,0:T(8,128)(2,1)S(1)} %fusion.17) | data formatting | bytes 1179648 | tf_op jit(solution)/shard_map/convert_element_type | solution.py:105
  62.9 3.8 %reshape.135 = bf16[3,3,8,8,512]{4,3,2,1,0:T(8,128)(2,1)S(1)} reshape(bf16[9,64,16,32]{3,2,1,0:T(8,128)(2,1)} %copy.30) | data formatting | bytes 1179648 | tf_op jit(solution)/shard_map/reshape | solution.py:106
  66.7 0.1 slice.61
  66.9 0.4 fusion.54
  67.2 0.2 multiply_reduce_fusion
  67.5 0.2 fusion.27
  67.6 0.4 convolution_convert_fusion.4
  68.1 0.2 pad_maximum_fusion.1
  68.4 20.9 %all_to_all.10 = bf16[32,24,512]{2,1,0:T(8,128)(2,1)S(1)} all-to-all(bf16[32,24,512]{2,1,0:T(8,128)(2,1)S(1)} %pad_maximum_fusion.1), channel_id=1, replica_groups=mesh['rep'=16,'exp'=32] {'exp'}, dimensions={0} | all-to-all | bytes 1572864 | tf_op jit(solution)/shard_map/all_to_all | solution.py:41
  89.3 0.2 fusion.49
  89.5 0.1 reshape.142
  89.6 0.1 reshape.144
  89.7 4.2 %all-gather.2.cloned.1.call-done = bf16[2,2048,512]{2,1,0:T(8,128)(2,1)} async-done(((bf16[2,128,512]{2,1,0:T(8,128)(2,1)}), bf16[2,2048,512]{2,1,0:T(8,128)(2,1)}) %all-gather.2.cloned.1.call-update) | async-done | bytes 4194320 | tf_op jit(solution)/shard_map/all_gather | solution.py:35
  93.9 2.6 %fusion.14 = f32[384,2048]{1,0:T(8,128)S(1)} fusion(bf16[384,512]{1,0:T(8,128)(2,1)S(1)} %reshape.142, bf16[2,2048,512]{2,1,0:T(8,128)(2,1)} %all-gather.2.cloned.1.call-done), kind=kOutput, calls=%fused_computation.26 | convolution fusion | flops 805306368 | bytes 5636096 | tf_op jit(solution)/shard_map/dot_general | solution.py:170
  96.5 1.6 convolution_convert_fusion.1
  98.2 1.7 copy-done.6
  99.9 2.5 %fusion.8 = bf16[384,2048]{1,0:T(8,128)(2,1)S(1)} fusion(f32[384,2048]{1,0:T(8,128)S(1)} %fusion.14, bf16[384,512]{1,0:T(8,128)(2,1)S(1)} %reshape.144, bf16[2,2048,512]{2,1,0:T(8,128)(2,1)S(1)} %copy-done.6), kind=kOutput, calls=%fused_computation.14 | convolution fusion | flops 820248576 | bytes 7208960 | tf_op jit(solution)/shard_map/dot_general | solution.py:181
  102.4 1.2 copy-done.8
  103.6 1.3 convolution_convert_fusion.2
  104.9 2.7 %pad_maximum_fusion = bf16[2048,1024]{0,1:T(8,128)(2,1)} fusion(bf16[2048,512]{0,1:T(8,128)(2,1)S(1)} %convolution_convert_fusion.1, bf16[2048,512]{0,1:T(8,128)(2,1)S(1)} %convolution_convert_fusion.2), kind=kLoop, calls=%fused_computation.6 | loop fusion | flops 8388608 | bytes 8388608 | tf_op jit(solution)/shard_map/concatenate | solution.py:56
  107.5 6.4 %copy.36 = bf16[2048,1024]{1,0:T(8,128)(2,1)} copy(bf16[2048,1024]{0,1:T(8,128)(2,1)} %pad_maximum_fusion) | data formatting | bytes 8388608
  114.0 3.0 %fusion.19 = bf16[384,512]{1,0:T(8,128)(2,1)S(1)} fusion(bf16[384,2048]{1,0:T(8,128)(2,1)} %copy-done.8, bf16[2,2048,512]{2,1,0:T(8,128)(2,1)} %all-gather.2.cloned.1.call-done), kind=kOutput, calls=%fused_computation.32 | convolution fusion | flops 805502976 | bytes 4063232 | tf_op jit(solution)/shard_map/dot_general | solution.py:185
  117.1 3.7 %fusion.18 = bf16[384,512]{1,0:T(8,128)(2,1)S(1)} fusion(bf16[2,2048,512]{2,1,0:T(8,128)(2,1)} %all-gather.2.cloned.1.call-done, f32[384,2048]{1,0:T(8,128)} %copy-done.2), kind=kOutput, calls=%fused_computation.31 | convolution fusion | flops 812580864 | bytes 5636096 | tf_op jit(solution)/shard_map/dot_general | solution.py:174
  120.9 0.2 pad_maximum_fusion.2
  121.1 19.2 %all_to_all.11 = bf16[32,24,512]{2,1,0:T(8,128)(2,1)S(1)} all-to-all(bf16[32,24,512]{2,1,0:T(8,128)(2,1)S(1)} %pad_maximum_fusion.2), channel_id=1, replica_groups=mesh['rep'=16,'exp'=32] {'exp'}, dimensions={0} | all-to-all | bytes 1572864 | tf_op jit(solution)/shard_map/all_to_all | solution.py:41
  140.3 0.2 fusion.48
  140.5 0.1 reshape.146
  140.6 0.1 reshape.148
  140.7 1.1 convolution_convert_fusion.5
  141.8 1.1 fusion.21
  142.8 51.2 %reduce-scatter.4.cloned.1.call-done = bf16[128,1024]{1,0:T(8,128)(2,1)} async-done(((bf16[2048,1024]{1,0:T(8,128)(2,1)}), bf16[128,1024]{1,0:T(8,128)(2,1)}) %reduce-scatter.4.cloned.1.call-update) | async-done | bytes 262160
  194.0 1.0 fusion.51
  195.0 0.1 copy.41
  195.2 0.8 copy.33
  196.0 0.1 copy.42
  196.2 0.8 copy.34
  (38 shorter events, 0.8 us)
Async XLA Ops:
  7.2 22.4 %copy-start = (bf16[512,1536]{1,0:T(8,128)(2,1)S(1)}, bf16[512,1536]{1,0:T(8,128)(2,1)}, u32[]{:S(2)}) copy-start(bf16[512,1536]{1,0:T(8,128)(2,1)} %param.12) | copy-start | bytes 4718596
  7.2 86.7 %all-gather.2.cloned.1.call-start = ((), (), s32[]{:S(2)}) async-start(), calls=%async_computation.3 | async-start | bytes 4456448 | tf_op jit(solution)/shard_map/all_gather | solution.py:35
  9.1 185.0 %reduce-scatter.4.cloned.1.call-start = ((), (), s32[]{:S(2)}) async-start(), calls=%async_computation.4 | async-start | bytes 4456448
  10.0 10.3 %collective-permute-start = (bf16[4,16,512]{2,1,0:T(8,128)(2,1)S(1)}, bf16[4,16,512]{2,1,0:T(8,128)(2,1)S(1)}, u32[]{:S(2)}, u32[]{:S(2)}) collective-permute-start(bf16[4,16,512]{2,1,0:T(8,128)(2,1)S(1)} %get-tuple-element.28), channel_id=1, source_target_pairs={{0,32},{32,64},{64,96},{96,128},{128,160},{160,192},{192,224},{224... | collective-permute-start | bytes 196616 | tf_op jit(solution)/shard_map/ppermute | solution.py:21
  13.8 7.4 %collective-permute-start.1 = (bf16[4,16,512]{2,1,0:T(8,128)(2,1)S(1)}, bf16[4,16,512]{2,1,0:T(8,128)(2,1)S(1)}, u32[]{:S(2)}, u32[]{:S(2)}) collective-permute-start(bf16[4,16,512]{2,1,0:T(8,128)(2,1)S(1)} %get-tuple-element.27), channel_id=1, source_target_pairs={{32,0},{64,32},{96,64},{128,96},{160,128},{192,160},{224,192},{256... | collective-permute-start | bytes 196616 | tf_op jit(solution)/shard_map/ppermute | solution.py:24
  21.4 5.4 %collective-permute-start.3 = (bf16[24,4,512]{2,1,0:T(4,128)(2,1)S(1)}, bf16[24,4,512]{2,1,0:T(4,128)(2,1)S(1)}, u32[]{:S(2)}, u32[]{:S(2)}) collective-permute-start(bf16[24,4,512]{2,1,0:T(4,128)(2,1)S(1)} %get-tuple-element.24), channel_id=1, source_target_pairs={{1,0},{2,1},{3,2},{4,3},{5,4},{6,5},{7,6},{8,7},{9,8},{10,9},{11,1... | collective-permute-start | bytes 294920 | tf_op jit(solution)/shard_map/ppermute | solution.py:24
  23.3 5.9 %collective-permute-start.2 = (bf16[24,4,512]{2,1,0:T(4,128)(2,1)S(1)}, bf16[24,4,512]{2,1,0:T(4,128)(2,1)S(1)}, u32[]{:S(2)}, u32[]{:S(2)}) collective-permute-start(bf16[24,4,512]{2,1,0:T(4,128)(2,1)S(1)} %get-tuple-element.23), channel_id=1, source_target_pairs={{0,1},{1,2},{2,3},{3,4},{4,5},{5,6},{6,7},{7,8},{8,9},{9,10},{10,1... | collective-permute-start | bytes 294920 | tf_op jit(solution)/shard_map/ppermute | solution.py:21
  56.5 2.6 %copy-start.5 = (bf16[9,64,1,16,32]{1,4,3,0,2:T(8,128)(2,1)S(1)}, bf16[9,64,1,16,32]{1,4,3,0,2:T(8,128)(2,1)}, u32[]{:S(2)}) copy-start(bf16[9,64,1,16,32]{1,4,3,0,2:T(8,128)(2,1)} %copy.38) | copy-start | bytes 1769476
  62.9 4.0 %copy-start.7 = (bf16[512,512]{1,0:T(8,128)(2,1)S(1)}, bf16[512,512]{1,0:T(8,128)(2,1)}, u32[]{:S(2)}) copy-start(bf16[512,512]{1,0:T(8,128)(2,1)} %param.13) | copy-start | bytes 1572868
  62.9 4.6 %copy-start.4 = (bf16[16,16,512]{2,1,0:T(8,128)(2,1)S(1)}, bf16[16,16,512]{2,1,0:T(8,128)(2,1)}, u32[]{:S(2)}) copy-start(bf16[16,16,512]{2,1,0:T(8,128)(2,1)} %param.8) | copy-start | bytes 786436
  66.7 1.4 copy-start.3
  96.5 1.7 copy-start.2
  96.5 3.3 %copy-start.6 = (bf16[2,2048,512]{2,1,0:T(8,128)(2,1)S(1)}, bf16[2,2048,512]{2,1,0:T(8,128)(2,1)}, u32[]{:S(2)}) copy-start(bf16[2,2048,512]{2,1,0:T(8,128)(2,1)} %all-gather.2.cloned.1.call-done) | copy-start | bytes 12582916
  102.4 1.2 copy-start.8
  140.5 56.5 %copy-start.1 = (bf16[512,1536]{1,0:T(8,128)(2,1)S(1)}, bf16[512,1536]{1,0:T(8,128)(2,1)}, u32[]{:S(2)}) copy-start(bf16[512,1536]{1,0:T(8,128)(2,1)} %param.12) | copy-start | bytes 4718596
Sparse Core Ops, SparseCore 0:
  10.7 83.1 all-gather.1
  114.1 79.9 reduce-scatter.3
where the time goes:
time: 205 us; the launch traced here: 204 us
  waiting for transfers between devices  57.9 us (28%)
  local copies, waits for them, and re-layouts  49 us (24%)
  blocking collectives  40.1 us (20%)
  matrix products  21.7 us (11%)
  between operations  14.5 us (7%)
  other arithmetic  11.1 us (5%)
  starting transfers between devices  9.52 us (5%)
    unnamed x3, waiting for transfers between devices  51.3 us
    all_to_all x2, blocking collectives, in_one_piece(): lax.all_to_all(both, axis, split_axis=split_dim, concat_axis=concat_dim,...  40.1 us
    unnamed x28, local copies, waits for them, and re-layouts  23.5 us
    slice x1, local copies, waits for them, and re-layouts, window_attend(): blocks[:, :, 2]  6.93 us
    reshape x1, local copies, waits for them, and re-layouts, window_attend(): blocks = blocks.reshape(win_rows * win_cols, cells, 3, HEADS, head_size)  6.61 us
    ppermute x2, starting transfers between devices, padded(): lax.ppermute(lax.slice_in_dim(block, block.shape[dim] - width, None, axis...  6.23 us
    all_gather x1, waiting for transfers between devices, sent_together(): lax.all_gather(both, axis, axis=dim, tiled=True)  4.22 us
  transfers between devices with their start and end apart: 6, of which 3 were waited for; matrix products, arithmetic and copies ran while one was open for 28% of the time, Pallas kernels for 0%

commit v1 on v0

--- a/solution.py
+++ b/solution.py
@@ -3,6 +3,8 @@
 import jax
 import jax.numpy as jnp
 from jax import lax
+from jax.experimental import pallas as pl
+from jax.experimental.pallas import tpu as pltpu
 from jax.sharding import PartitionSpec as P
 
 HEADS = 16
@@ -11,6 +13,9 @@
 GELU_C = math.sqrt(2.0 / math.pi)
 window_side = 8
 margin_cells = 4
+CHUNKS = 8
+
+VMEM_LIMIT = 48 * 1024 * 1024
 
 
 def padded(block, sides, width):
@@ -26,15 +31,6 @@
     return block
 
 
-def sent_together(arrays, axis, dim, along):
-    ends, at = ([], 0)
-    for a in arrays[:-1]:
-        at += a.shape[along]
-        ends.append(at)
-    both = jnp.concatenate(arrays, axis=along)
-    return tuple(jnp.split(lax.all_gather(both, axis, axis=dim, tiled=True), ends, axis=along))
-
-
 def in_one_piece(arrays, axis, split_dim, concat_dim, along):
     both = jnp.concatenate(arrays, axis=along)
     result, at, finished = (
@@ -46,28 +42,6 @@
         finished.append(lax.slice_in_dim(result, at, at + a.shape[along], axis=along))
         at += a.shape[along]
     return tuple(finished)
-
-
-def sent_together_2(arrays, axis, dim, along):
-    ends, at = ([], 0)
-    for a in arrays[:-1]:
-        at += a.shape[along]
-        ends.append(at)
-    both = jnp.concatenate(arrays, axis=along)
-    return tuple(
-        jnp.split(lax.psum_scatter(both, axis, scatter_dimension=dim, tiled=True), ends, axis=along)
-    )
-
-
-def gelu_tanh(inputs):
-    return 0.5 * inputs * (1.0 + jnp.tanh(GELU_C * (inputs + 0.044715 * inputs * inputs * inputs)))
-
-
-def gelu_slope(inputs):
-    inner = jnp.tanh(GELU_C * (inputs + 0.044715 * inputs * inputs * inputs))
-    return 0.5 * (1.0 + inner) + 0.5 * inputs * (1.0 - inner * inner) * GELU_C * (
-        1.0 + 3.0 * 0.044715 * inputs * inputs
-    )
 
 
 def layer_norm(values):
@@ -109,11 +83,125 @@
     return context.reshape(ext_rows, ext_cols, feature)
 
 
+def nt(a, b):
+    return lax.dot_general(a, b, (((1,), (1,)), ((), ())), preferred_element_type=jnp.float32)
+
+
+def tn(a, b):
+    return lax.dot_general(a, b, (((0,), (0,)), ((), ())), preferred_element_type=jnp.float32)
+
+
+def middle_kernel(w_ref, x_ref, g_ref, grads_ref, hid_ref, pg_ref):
+    shards, _, width, feature = w_ref.shape
+    up = w_ref[:, 0].reshape(shards * width, feature)
+    down = w_ref[:, 1].reshape(shards * width, feature)
+    x, g = x_ref[...], g_ref[...]
+    pre = nt(up, x)
+    square = pre * pre
+    inner = jnp.tanh(pre * (GELU_C + (GELU_C * 0.044715) * square))
+    half = 0.5 + 0.5 * inner
+    hidden = (pre * half).astype(jnp.bfloat16)
+    slope = half + (0.5 * pre) * (1.0 - inner * inner) * (
+        GELU_C + (3.0 * 0.044715 * GELU_C) * square
+    )
+    pre_grad = (nt(down, g) * slope).astype(jnp.bfloat16)
+    hid_ref[...] = hidden
+    pg_ref[...] = pre_grad
+    grad_up = jnp.dot(pre_grad, x, preferred_element_type=jnp.float32).astype(jnp.bfloat16)
+    grad_down = jnp.dot(hidden, g, preferred_element_type=jnp.float32).astype(jnp.bfloat16)
+    grads_ref[:, :width] = grad_up.reshape(shards, width, feature)
+    grads_ref[:, width:] = grad_down.reshape(shards, width, feature)
+
+
+def middle(weights, slot_x, slot_g):
+    owners, _, width, feature = weights.shape
+    rows = slot_x.shape[0]
+    step = owners // CHUNKS
+    ff = owners * width
+    return pl.pallas_call(
+        middle_kernel,
+        grid=(CHUNKS,),
+        in_specs=[
+            pl.BlockSpec((step, 2, width, feature), lambda i: (i, 0, 0, 0)),
+            pl.BlockSpec((rows, feature), lambda i: (0, 0)),
+            pl.BlockSpec((rows, feature), lambda i: (0, 0)),
+        ],
+        out_specs=[
+            pl.BlockSpec((step, 2 * width, feature), lambda i: (i, 0, 0)),
+            pl.BlockSpec((step * width, rows), lambda i: (i, 0)),
+            pl.BlockSpec((step * width, rows), lambda i: (i, 0)),
+        ],
+        out_shape=[
+            jax.ShapeDtypeStruct((owners, 2 * width, feature), jnp.bfloat16),
+            jax.ShapeDtypeStruct((ff, rows), jnp.bfloat16),
+            jax.ShapeDtypeStruct((ff, rows), jnp.bfloat16),
+        ],
+        compiler_params=pltpu.CompilerParams(vmem_limit_bytes=VMEM_LIMIT),
+        cost_estimate=pl.CostEstimate(
+            flops=8 * rows * ff * feature,
+            bytes_accessed=8 * ff * feature + 4 * ff * rows,
+            transcendentals=ff * rows,
+        ),
+        name="middle",
+    )(weights, slot_x, slot_g)
+
+
+def back_kernel(w_ref, hid_ref, pg_ref, out_ref, in_ref, out_acc, in_acc):
+    shards, _, width, feature = w_ref.shape
+    up = w_ref[:, 0].reshape(shards * width, feature)
+    down = w_ref[:, 1].reshape(shards * width, feature)
+
+    @pl.when(pl.program_id(0) == 0)
+    def _():
+        out_acc[...] = jnp.zeros_like(out_acc)
+        in_acc[...] = jnp.zeros_like(in_acc)
+
+    out_acc[...] += tn(hid_ref[...], down)
+    in_acc[...] += tn(pg_ref[...], up)
+
+    @pl.when(pl.program_id(0) == pl.num_programs(0) - 1)
+    def _():
+        out_ref[...] = out_acc[...].astype(jnp.bfloat16)
+        in_ref[...] = in_acc[...].astype(jnp.bfloat16)
+
+
+def back(weights, hidden, pre_grad):
+    owners, _, width, feature = weights.shape
+    ff, rows = hidden.shape
+    steps = 4
+    step = owners // steps
+    return pl.pallas_call(
+        back_kernel,
+        grid=(steps,),
+        in_specs=[
+            pl.BlockSpec((step, 2, width, feature), lambda i: (i, 0, 0, 0)),
+            pl.BlockSpec((step * width, rows), lambda i: (i, 0)),
+            pl.BlockSpec((step * width, rows), lambda i: (i, 0)),
+        ],
+        out_specs=[
+            pl.BlockSpec((rows, feature), lambda i: (0, 0)),
+            pl.BlockSpec((rows, feature), lambda i: (0, 0)),
+        ],
+        out_shape=[jax.ShapeDtypeStruct((rows, feature), jnp.bfloat16)] * 2,
+        scratch_shapes=[pltpu.VMEM((rows, feature), jnp.float32)] * 2,
+        compiler_params=pltpu.CompilerParams(vmem_limit_bytes=VMEM_LIMIT),
+        cost_estimate=pl.CostEstimate(
+            flops=4 * rows * ff * feature,
+            bytes_accessed=4 * ff * feature + 4 * ff * rows,
+            transcendentals=0,
+        ),
+        name="back",
+    )(weights, hidden, pre_grad)
+
+
 def per_device(tokens, gate, route, cotangent, w_qkv, w_proj, w_up, w_down):
     tile_rows, tile_cols, feature = tokens.shape
     tok_count = tile_rows * tile_cols
     ext_rows = tile_rows + 2 * margin_cells
     ext_cols = tile_cols + 2 * margin_cells
+    weights = lax.all_gather(
+        jnp.concatenate([w_up, w_down], axis=0), "rep", axis=0, tiled=False
+    )
     extended = padded(tokens, (("rep", 0), ("exp", 1)), 4)
     qkv = jnp.dot(extended.reshape(-1, feature), w_qkv, preferred_element_type=jnp.float32).astype(
         jnp.bfloat16
@@ -137,8 +225,14 @@
     experts = lax.axis_size("exp")
     capacity = max(2, 3 * tok_count // (2 * experts))
     chosen = route.reshape(tok_count)
-    matches = (chosen[:, None] == jnp.arange(experts, dtype=jnp.int32)[None, :]).astype(jnp.int32)
-    position = jnp.sum(matches * (jnp.cumsum(matches, axis=0) - 1), axis=1)
+    matches = chosen[:, None] == jnp.arange(experts, dtype=jnp.int32)[None, :]
+    earlier = jnp.arange(tok_count)[:, None] > jnp.arange(tok_count)[None, :]
+    before = jnp.dot(
+        earlier.astype(jnp.bfloat16),
+        matches.astype(jnp.bfloat16),
+        preferred_element_type=jnp.float32,
+    )
+    position = jnp.sum(jnp.where(matches, before, 0.0), axis=1).astype(jnp.int32)
     target = chosen * capacity + position
     placer = (target[:, None] == jnp.arange(experts * capacity, dtype=jnp.int32)[None, :]).astype(
         jnp.bfloat16
@@ -161,60 +255,34 @@
             preferred_element_type=jnp.float32,
         )
 
-    up_whole, down_whole = sent_together((w_up, w_down), "rep", 1, 0)
-    up_mat = up_whole[0]
-    down_mat = down_whole[0]
-
-    def forward(sent_x):
-        slot_rows = sent_x.reshape(-1, feature)
-        pre_act = lax.dot_general(
-            slot_rows, up_mat, (((1,), (1,)), ((), ())), preferred_element_type=jnp.float32
-        )
-        hidden = gelu_tanh(pre_act).astype(jnp.bfloat16)
-        expert_out = jnp.dot(hidden, down_mat, preferred_element_type=jnp.float32).astype(
-            jnp.bfloat16
-        )
-        return (slot_rows, pre_act, hidden, expert_out.reshape(-1, capacity, feature))
-
-    def backward(pre_act, sent_g):
-        slot_grads = sent_g.reshape(-1, feature)
-        hidden_grad = lax.dot_general(
-            slot_grads, down_mat, (((1,), (1,)), ((), ())), preferred_element_type=jnp.float32
-        )
-        pre_grad = (hidden_grad * gelu_slope(pre_act)).astype(jnp.bfloat16)
-        input_slots = jnp.dot(pre_grad, up_mat, preferred_element_type=jnp.float32).astype(
-            jnp.bfloat16
-        )
-        return (slot_grads, pre_grad, input_slots.reshape(-1, capacity, feature))
-
     sent_x, sent_g = in_one_piece((to_slots(mixed), to_slots(upstream)), "exp", 0, 0, 1)
-    slot_rows, pre_act, hidden, expert_out = forward(sent_x)
-    slot_grads, pre_grad, input_slots = backward(pre_act, sent_g)
-    back_out, back_grad = in_one_piece((expert_out, input_slots), "exp", 0, 0, 1)
+    slot_rows = sent_x.reshape(-1, feature)
+    slot_grads = sent_g.reshape(-1, feature)
+    grads, hidden, pre_grad = middle(weights, slot_rows, slot_grads)
+    summed = lax.psum_scatter(grads, "rep", scatter_dimension=0, tiled=True)[0]
+    expert_out, input_slots = back(weights, hidden, pre_grad)
+    back_out, back_grad = in_one_piece(
+        (
+            expert_out.reshape(-1, capacity, feature),
+            input_slots.reshape(-1, capacity, feature),
+        ),
+        "exp",
+        0,
+        0,
+        1,
+    )
     layer_out = (mixed.astype(jnp.float32) + gate_rows[:, None] * from_slots(back_out)).astype(
         jnp.bfloat16
     )
     input_grad = from_slots(back_grad).astype(jnp.bfloat16)
-    full_up = lax.dot_general(
-        pre_grad, slot_rows, (((0,), (0,)), ((), ())), preferred_element_type=jnp.float32
-    )
-    full_down = lax.dot_general(
-        hidden, slot_grads, (((0,), (0,)), ((), ())), preferred_element_type=jnp.float32
-    )
-    grad_up_rows, grad_down_rows = tuple(
-        (
-            part.astype(jnp.float32)
-            for part in sent_together_2(
-                (full_up.astype(jnp.bfloat16), full_down.astype(jnp.bfloat16)), "rep", 0, 1
-            )
-        )
-    )
     average_factor = 1.0 / lax.axis_size("rep")
+    width = w_up.shape[1]
+    total = summed.astype(jnp.float32) * average_factor
     return (
         layer_out.reshape(tile_rows, tile_cols, feature),
         input_grad.reshape(tile_rows, tile_cols, feature),
-        (grad_up_rows * average_factor)[None],
-        (grad_down_rows * average_factor)[None],
+        total[:width][None],
+        total[width:][None],
     )
 
 

time: 205 us -> 200 us (0.976)
  Pallas kernels: 0 us -> 14.5 us
  matrix products: 21.7 us -> 9.13 us
  other arithmetic: 11.1 us -> 7.31 us
  local copies, waits for them, and re-layouts: 49 us -> 45.3 us
    reduce_scatter x0 -> x1, waiting for transfers between devices: none -> 54 us  [per_device(): summed = lax.psum_scatter(grads, 'rep', scatter_dimension=0, tiled=True)[0]]
    unnamed x3 -> x2, waiting for transfers between devices: 51.3 us -> 0.03 us
    pallas_call x0 -> x2, Pallas kernels: none -> 14.5 us  [the longest x1 9.82 us: middle(): pl.pallas_call(middle_kernel, grid=(CHUNKS,), in_specs=[pl.BlockSpec((ste...]
    dot_general x6 -> x1, matrix products: 14.7 us -> 0.96 us  [per_device(): jnp.dot(earlier.astype(jnp.bfloat16), matches.astype(jnp.bfloat16), prefe...]
    unnamed x28 -> x27, local copies, waits for them, and re-layouts: 23.5 us -> 18.4 us
    all_gather x1, waiting for transfers between devices: 4.22 us -> 0.63 us  [per_device(): lax.all_gather(jnp.concatenate([w_up, w_down], axis=0), 'rep', axis=0, ti...]
    concatenate x2 -> x1, other arithmetic: 4.46 us -> 1.8 us  [per_device(): jnp.concatenate([w_up, w_down], axis=0)]
    ppermute x2, waiting for transfers between devices: 2.44 us -> 0.01 us  [padded(): lax.ppermute(lax.slice_in_dim(block, block.shape[dim] - width, None, axis...]
  transfers between devices with their start and end apart: 6 -> 6, of which waited for: 3 -> 3; matrix products, arithmetic and copies ran while one was open for 28% -> 27% of each run, Pallas kernels for 0% -> 2%
where the time goes in v1:
time: 200 us; the launch traced here: 199 us
  waiting for transfers between devices  55.9 us (28%)
  local copies, waits for them, and re-layouts  45.3 us (23%)
  blocking collectives  41.4 us (21%)
  Pallas kernels  14.5 us (7%)
  between operations  14.4 us (7%)
  starting transfers between devices  10.8 us (5%)
  matrix products  9.13 us (5%)
  other arithmetic  7.31 us (4%)
    reduce_scatter x1, waiting for transfers between devices, per_device(): summed = lax.psum_scatter(grads, 'rep', scatter_dimension=0, tiled=True)[0]  54 us
    all_to_all x2, blocking collectives, in_one_piece(): lax.all_to_all(both, axis, split_axis=split_dim, concat_axis=concat_dim,...  41.4 us
    unnamed x27, local copies, waits for them, and re-layouts  18.4 us
    pallas_call x1, Pallas kernels, middle(): pl.pallas_call(middle_kernel, grid=(CHUNKS,), in_specs=[pl.BlockSpec((ste...  9.82 us
    slice x1, local copies, waits for them, and re-layouts, window_attend(): blocks[:, :, 2]  6.88 us
    reshape x1, local copies, waits for them, and re-layouts, window_attend(): blocks = blocks.reshape(win_rows * win_cols, cells, 3, HEADS, head_size)  6.65 us
    ppermute x2, starting transfers between devices, padded(): lax.ppermute(lax.slice_in_dim(block, block.shape[dim] - width, None, axis...  5.75 us
    ppermute x2, starting transfers between devices, padded(): lax.ppermute(lax.slice_in_dim(block, 0, width, axis=dim), axis, backward)  4.93 us
  transfers between devices with their start and end apart: 6, of which 3 were waited for; matrix products, arithmetic and copies ran while one was open for 27% of the time, Pallas kernels for 2%

profile of v1, /device:TPU:6, one launch (start us, length us, event | category | flops | bytes accessed | tf_op | source)
XLA Modules:
  0.0 198.7 jit_solution(7791982540989400370)
XLA Ops:
  7.2 0.0 all-gather.3.cloned.1.call-start
  7.2 1.8 pad_maximum_fusion.3
  9.1 0.0 reduce-scatter.2.cloned.1.call-start
  9.1 0.9 fusion.39
  10.0 3.8 %collective-permute-start = (bf16[4,16,512]{2,1,0:T(8,128)(2,1)S(1)}, bf16[4,16,512]{2,1,0:T(8,128)(2,1)S(1)}, u32[]{:S(2)}, u32[]{:S(2)}) collective-permute-start(bf16[4,16,512]{2,1,0:T(8,128)(2,1)S(1)} %get-tuple-element.26), channel_id=1, source_target_pairs={{0,32},{32,64},{64,96},{96,128},{128,160},{160,192},{192,224},{224... | collective-permute-start | bytes 196616 | tf_op jit(solution)/shard_map/ppermute | solution.py:26
  13.8 1.3 collective-permute-start.1
  15.1 0.8 mul.55
  15.9 1.0 fusion.14
  16.9 0.7 convert_add_fusion.1
  17.6 1.4 convolution_convert_fusion.1
  19.0 1.0 constant_dynamic-update-slice_fusion.1
  19.9 0.0 collective-permute-done.1
  20.0 0.1 fusion.38
  20.1 1.9 collective-permute-start.2
  22.0 3.6 %collective-permute-start.3 = (bf16[24,4,512]{2,1,0:T(4,128)(2,1)S(1)}, bf16[24,4,512]{2,1,0:T(4,128)(2,1)S(1)}, u32[]{:S(2)}, u32[]{:S(2)}) collective-permute-start(bf16[24,4,512]{2,1,0:T(4,128)(2,1)S(1)} %get-tuple-element.24), channel_id=1, source_target_pairs={{1,0},{2,1},{3,2},{4,3},{5,4},{6,5},{7,6},{8,7},{9,8},{10,9},{11,1... | collective-permute-start | bytes 294920 | tf_op jit(solution)/shard_map/ppermute | solution.py:29
  25.7 0.1 broadcast_and_fusion
  25.7 0.1 and.40
  25.8 0.9 reshape.130
  26.7 1.1 collective-permute-done.3
  27.8 0.3 pad_maximum_fusion.2
  28.2 1.1 convolution_convert_fusion
  29.3 0.2 copy.32
  29.4 6.6 %reshape.124 = bf16[9,64,3,16,32]{4,3,2,1,0:T(8,128)(2,1)} reshape(bf16[3,3,8,8,1536]{4,3,2,1,0:T(8,128)(2,1)S(1)} %bitcast.41) | data formatting | bytes 3538944 | tf_op jit(solution)/shard_map/reshape | solution.py:64
  36.1 6.9 %fusion.34 = (bf16[9,64,1,16,32]{4,3,2,1,0:T(8,128)(2,1)}, bf16[9,64,1,16,32]{4,3,2,1,0:T(8,128)(2,1)}, bf16[9,64,1,16,32]{4,3,2,1,0:T(8,128)(2,1)}) fusion(bf16[9,64,3,16,32]{4,3,2,1,0:T(8,128)(2,1)} %reshape.124), kind=kLoop, calls=%fused_computation.62 | loop fusion | bytes 3538944 | tf_op jit(solution)/shard_map/slice | solution.py:78
  43.0 3.5 %copy.29 = bf16[9,64,1,16,32]{1,4,3,0,2:T(8,128)(2,1)S(1)} copy(bf16[9,64,1,16,32]{4,3,2,1,0:T(8,128)(2,1)} %get-tuple-element.15) | data formatting | bytes 1179648
  46.5 4.3 %copy.30 = bf16[9,64,1,16,32]{1,4,3,0,2:T(8,128)(2,1)} copy(bf16[9,64,1,16,32]{4,3,2,1,0:T(8,128)(2,1)} %get-tuple-element.16) | data formatting | bytes 1179648
  50.8 4.3 %copy.28 = bf16[9,64,1,16,32]{1,4,3,0,2:T(8,128)(2,1)} copy(bf16[9,64,1,16,32]{4,3,2,1,0:T(8,128)(2,1)} %get-tuple-element.14) | data formatting | bytes 1179648
  55.1 2.1 %fusion.10 = f32[9,16,64,64]{2,3,1,0:T(8,128)S(1)} fusion(bf16[9,64,1,16,32]{1,4,3,0,2:T(8,128)(2,1)} %copy.30, bf16[9,64,1,16,32]{1,4,3,0,2:T(8,128)(2,1)S(1)} %copy.29), kind=kOutput, calls=%fused_computation.19 | convolution fusion | flops 37748736 | bytes 3538944 | tf_op jit(solution)/shard_map/wqhd,wkhd->whqk/dot_general | solution.py:70
  57.2 2.6 %fusion.40 = (f32[9,16,64]{2,1,0:T(8,128)S(1)}, f32[9,16,64,64]{2,3,1,0:T(8,128)S(1)}) fusion(f32[9,16,64,64]{2,3,1,0:T(8,128)S(1)} %fusion.10, pred[9,64]{1,0:T(8,128)(4,1)S(1)} %and.40), kind=kOutput, calls=%fused_computation.68 | output fusion | flops 3539007 | bytes 4756032 | tf_op jit(solution)/shard_map/sub | solution.py:75
  59.8 0.7 fusion.7
  60.6 3.0 %copy.25 = bf16[9,64,16,32]{3,2,1,0:T(8,128)(2,1)} copy(bf16[9,64,16,32]{1,3,2,0:T(8,128)(2,1)S(1)} %fusion.7) | data formatting | bytes 1179648 | tf_op jit(solution)/shard_map/convert_element_type | solution.py:79
  63.6 3.8 %reshape.125 = bf16[3,3,8,8,512]{4,3,2,1,0:T(8,128)(2,1)S(1)} reshape(bf16[9,64,16,32]{3,2,1,0:T(8,128)(2,1)} %copy.25) | data formatting | bytes 1179648 | tf_op jit(solution)/shard_map/reshape | solution.py:80
  67.4 0.1 slice.63
  67.6 0.4 fusion.41
  68.0 0.2 multiply_reduce_fusion
  68.2 0.2 copy-done.6
  68.3 0.2 fusion.16
  68.5 0.7 copy-done.8
  69.2 0.4 convolution_convert_fusion.2
  69.6 0.1 reshape.129
  69.7 0.2 pad_maximum_fusion
  69.9 22.2 %all_to_all.10 = bf16[32,24,512]{2,1,0:T(8,128)(2,1)S(1)} all-to-all(bf16[32,24,512]{2,1,0:T(8,128)(2,1)S(1)} %pad_maximum_fusion), channel_id=1, replica_groups=mesh['rep'=16,'exp'=32] {'exp'}, dimensions={0} | all-to-all | bytes 1572864 | tf_op jit(solution)/shard_map/all_to_all | solution.py:37
  92.2 0.2 fusion.36
  92.4 0.1 reshape.131.x_ref
  92.5 0.8 reshape.132.g_ref
  93.3 0.6 all-gather.3.cloned.1.call-done
  93.9 1.0 copy-done.3
  94.9 9.8 %middle.1 = (bf16[16,256,512]{2,1,0:T(8,128)(2,1)}, bf16[2048,384]{1,0:T(8,128)(2,1)S(1)}, bf16[2048,384]{1,0:T(8,128)(2,1)S(1)}) custom-call(bf16[16,2,128,512]{3,2,1,0:T(8,128)(2,1)} %bitcast.42, bf16[384,512]{1,0:T(8,128)(2,1)S(1)} %reshape.131.x_ref, bf16[384,512]{1,0:T(8,128)(2,1)S(1)} %copy-done.3), custom_call_target="tpu_custom_call" | custom-call | flops 3221225472 | bytes 11534336 | tf_op jit(solution)/shard_map/middle/pallas_call | solution.py:121
  104.7 1.2 copy-done.1
  106.0 1.4 copy-done.2
  107.4 4.7 %back.1 = (bf16[384,512]{1,0:T(8,128)(2,1)S(1)}, bf16[384,512]{1,0:T(8,128)(2,1)S(1)}) custom-call(bf16[16,2,128,512]{3,2,1,0:T(8,128)(2,1)} %bitcast.43, bf16[2048,384]{1,0:T(8,128)(2,1)S(1)} %get-tuple-element.9.hid_ref, bf16[2048,384]{1,0:T(8,128)(2,1)S(1)} %copy-done.2), custom_call_target="tpu_custom_call" | custom-call | flops 1610612736 | bytes 7340032 | tf_op jit(solution)/shard_map/back/pallas_call | solution.py:173
  112.1 0.8 copy-done.4
  112.9 1.1 reshape.133
  113.9 0.1 reshape.134
  114.0 0.2 pad_maximum_fusion.1
  114.3 19.2 %all_to_all.11 = bf16[32,24,512]{2,1,0:T(8,128)(2,1)S(1)} all-to-all(bf16[32,24,512]{2,1,0:T(8,128)(2,1)S(1)} %pad_maximum_fusion.1), channel_id=1, replica_groups=mesh['rep'=16,'exp'=32] {'exp'}, dimensions={0} | all-to-all | bytes 1572864 | tf_op jit(solution)/shard_map/all_to_all | solution.py:37
  133.5 0.2 fusion.35
  133.7 0.1 reshape.137
  133.8 0.1 reshape.135
  133.9 1.1 convolution_convert_fusion.3
  134.9 1.1 fusion.9
  136.0 54.0 %reduce-scatter.2.cloned.1.call-done = bf16[1,256,512]{2,1,0:T(8,128)(2,1)} async-done(((bf16[16,256,512]{2,1,0:T(8,128)(2,1)}), bf16[1,256,512]{2,1,0:T(8,128)(2,1)}) %reduce-scatter.2.cloned.1.call-update) | async-done | bytes 262160 | tf_op jit(solution)/shard_map/reduce_scatter | solution.py:262
  190.0 1.0 convert_multiply_fusion.1
  191.0 0.8 fusion.37
  (26 shorter events, 0.2 us)
Async XLA Ops:
  7.2 21.0 %copy-start = (bf16[512,1536]{1,0:T(8,128)(2,1)S(1)}, bf16[512,1536]{1,0:T(8,128)(2,1)}, u32[]{:S(2)}) copy-start(bf16[512,1536]{1,0:T(8,128)(2,1)} %param.12) | copy-start | bytes 4718596
  7.2 86.7 %all-gather.3.cloned.1.call-start = ((), (), s32[]{:S(2)}) async-start(), calls=%async_computation.4 | async-start | bytes 4456448 | tf_op jit(solution)/shard_map/all_gather | solution.py:202
  9.1 181.0 %reduce-scatter.2.cloned.1.call-start = ((), (), s32[]{:S(2)}) async-start(), calls=%async_computation.3 | async-start | bytes 4456448 | tf_op jit(solution)/shard_map/reduce_scatter | solution.py:262
  10.0 9.0 %collective-permute-start = (bf16[4,16,512]{2,1,0:T(8,128)(2,1)S(1)}, bf16[4,16,512]{2,1,0:T(8,128)(2,1)S(1)}, u32[]{:S(2)}, u32[]{:S(2)}) collective-permute-start(bf16[4,16,512]{2,1,0:T(8,128)(2,1)S(1)} %get-tuple-element.26), channel_id=1, source_target_pairs={{0,32},{32,64},{64,96},{96,128},{128,160},{160,192},{192,224},{224... | collective-permute-start | bytes 196616 | tf_op jit(solution)/shard_map/ppermute | solution.py:26
  13.8 6.2 %collective-permute-start.1 = (bf16[4,16,512]{2,1,0:T(8,128)(2,1)S(1)}, bf16[4,16,512]{2,1,0:T(8,128)(2,1)S(1)}, u32[]{:S(2)}, u32[]{:S(2)}) collective-permute-start(bf16[4,16,512]{2,1,0:T(8,128)(2,1)S(1)} %get-tuple-element.25), channel_id=1, source_target_pairs={{32,0},{64,32},{96,64},{128,96},{160,128},{192,160},{224,192},{256... | collective-permute-start | bytes 196616 | tf_op jit(solution)/shard_map/ppermute | solution.py:29
  20.1 6.6 %collective-permute-start.2 = (bf16[24,4,512]{2,1,0:T(4,128)(2,1)S(1)}, bf16[24,4,512]{2,1,0:T(4,128)(2,1)S(1)}, u32[]{:S(2)}, u32[]{:S(2)}) collective-permute-start(bf16[24,4,512]{2,1,0:T(4,128)(2,1)S(1)} %get-tuple-element.23), channel_id=1, source_target_pairs={{0,1},{1,2},{2,3},{3,4},{4,5},{5,6},{6,7},{7,8},{8,9},{9,10},{10,1... | collective-permute-start | bytes 294920 | tf_op jit(solution)/shard_map/ppermute | solution.py:26
  22.0 5.8 %collective-permute-start.3 = (bf16[24,4,512]{2,1,0:T(4,128)(2,1)S(1)}, bf16[24,4,512]{2,1,0:T(4,128)(2,1)S(1)}, u32[]{:S(2)}, u32[]{:S(2)}) collective-permute-start(bf16[24,4,512]{2,1,0:T(4,128)(2,1)S(1)} %get-tuple-element.24), channel_id=1, source_target_pairs={{1,0},{2,1},{3,2},{4,3},{5,4},{6,5},{7,6},{8,7},{9,8},{10,9},{11,1... | collective-permute-start | bytes 294920 | tf_op jit(solution)/shard_map/ppermute | solution.py:29
  57.2 2.6 %copy-start.7 = (bf16[9,64,1,16,32]{1,4,3,0,2:T(8,128)(2,1)S(1)}, bf16[9,64,1,16,32]{1,4,3,0,2:T(8,128)(2,1)}, u32[]{:S(2)}) copy-start(bf16[9,64,1,16,32]{1,4,3,0,2:T(8,128)(2,1)} %copy.28) | copy-start | bytes 1769476
  63.6 4.0 %copy-start.10 = (bf16[512,512]{1,0:T(8,128)(2,1)S(1)}, bf16[512,512]{1,0:T(8,128)(2,1)}, u32[]{:S(2)}) copy-start(bf16[512,512]{1,0:T(8,128)(2,1)} %param.13) | copy-start | bytes 1572868
  67.4 1.0 copy-start.6
  67.5 2.2 %copy-start.5 = (bf16[32,12,512]{2,1,0:T(8,128)(2,1)S(1)}, bf16[32,12,512]{2,1,0:T(8,128)(2,1)}, u32[]{:S(2)}) copy-start(bf16[32,12,512]{2,1,0:T(8,128)(2,1)} %reshape.130) | copy-start | bytes 1179652
  68.5 0.7 copy-start.8
  93.9 1.0 copy-start.3
  104.7 1.2 copy-start.1
  105.9 1.4 copy-start.2
  112.1 0.8 copy-start.4
  133.5 1.5 copy-start.9
Sparse Core Ops, SparseCore 0:
  10.7 83.1 all-gather.2
  106.1 83.9 reduce-scatter.1

commit v2 on v1

v2 whole, which is shorter than its diff:
```python
import functools
import math

import jax
import jax.numpy as jnp
import numpy as np
from jax import lax
from jax.experimental import pallas as pl
from jax.experimental.pallas import tpu as pltpu
from jax.sharding import PartitionSpec as P

HEADS = 16


GELU_C = math.sqrt(2.0 / math.pi)
window_side = 8
margin_cells = 4
CHUNKS = 8

VMEM_LIMIT = 48 * 1024 * 1024


def nt(a, b):
    return lax.dot_general(a, b, (((1,), (1,)), ((), ())), preferred_element_type=jnp.float32)


def tn(a, b):
    return lax.dot_general(a, b, (((0,), (0,)), ((), ())), preferred_element_type=jnp.float32)


def middle_kernel(w_ref, x_ref, g_ref, grads_ref, hid_ref, pg_ref):
    shards, _, width, feature = w_ref.shape
    up = w_ref[:, 0].reshape(shards * width, feature)
    down = w_ref[:, 1].reshape(shards * width, feature)
    x, g = x_ref[...], g_ref[...]
    pre = nt(up, x)
    square = pre * pre
    inner = jnp.tanh(pre * (GELU_C + (GELU_C * 0.044715) * square))
    half = 0.5 + 0.5 * inner
    hidden = (pre * half).astype(jnp.bfloat16)
    slope = half + (0.5 * pre) * (1.0 - inner * inner) * (
        GELU_C + (3.0 * 0.044715 * GELU_C) * square
    )
    pre_grad = (nt(down, g) * slope).astype(jnp.bfloat16)
    hid_ref[...] = hidden
    pg_ref[...] = pre_grad
    grad_up = jnp.dot(pre_grad, x, preferred_element_type=jnp.float32).astype(jnp.bfloat16)
    grad_down = jnp.dot(hidden, g, preferred_element_type=jnp.float32).astype(jnp.bfloat16)
    grads_ref[:, :width] = grad_up.reshape(shards, width, feature)
    grads_ref[:, width:] = grad_down.reshape(shards, width, feature)


def middle(weights, slot_x, slot_g):
    owners, _, width, feature = weights.shape
    rows = slot_x.shape[0]
    step = owners // CHUNKS
    ff = owners * width
    return pl.pallas_call(
        middle_kernel,
        grid=(CHUNKS,),
        in_specs=[
            pl.BlockSpec((step, 2, width, feature), lambda i: (i, 0, 0, 0)),
            pl.BlockSpec((rows, feature), lambda i: (0, 0)),
            pl.BlockSpec((rows, feature), lambda i: (0, 0)),
        ],
        out_specs=[
            pl.BlockSpec((step, 2 * width, feature), lambda i: (i, 0, 0)),
            pl.BlockSpec((step * width, rows), lambda i: (i, 0)),
            pl.BlockSpec((step * width, rows), lambda i: (i, 0)),
        ],
        out_shape=[
            jax.ShapeDtypeStruct((owners, 2 * width, feature), jnp.bfloat16),
            jax.ShapeDtypeStruct((ff, rows), jnp.bfloat16),
            jax.ShapeDtypeStruct((ff, rows), jnp.bfloat16),
        ],
        compiler_params=pltpu.CompilerParams(vmem_limit_bytes=VMEM_LIMIT),
        cost_estimate=pl.CostEstimate(
            flops=8 * rows * ff * feature,
            bytes_accessed=8 * ff * feature + 4 * ff * rows,
            transcendentals=ff * rows,
        ),
        name="middle",
    )(weights, slot_x, slot_g)


def back_kernel(w_ref, hid_ref, pg_ref, out_ref, in_ref, out_acc, in_acc):
    shards, _, width, feature = w_ref.shape
    up = w_ref[:, 0].reshape(shards * width, feature)
    down = w_ref[:, 1].reshape(shards * width, feature)

    @pl.when(pl.program_id(0) == 0)
    def _():
        out_acc[...] = jnp.zeros_like(out_acc)
        in_acc[...] = jnp.zeros_like(in_acc)

    out_acc[...] += tn(hid_ref[...], down)
    in_acc[...] += tn(pg_ref[...], up)

    @pl.when(pl.program_id(0) == pl.num_programs(0) - 1)
    def _():
        out_ref[...] = out_acc[...].astype(jnp.bfloat16)
        in_ref[...] = in_acc[...].astype(jnp.bfloat16)


def back(weights, hidden, pre_grad):
    owners, _, width, feature = weights.shape
    ff, rows = hidden.shape
    steps = 4
    step = owners // steps
    return pl.pallas_call(
        back_kernel,
        grid=(steps,),
        in_specs=[
            pl.BlockSpec((step, 2, width, feature), lambda i: (i, 0, 0, 0)),
            pl.BlockSpec((step * width, rows), lambda i: (i, 0)),
            pl.BlockSpec((step * width, rows), lambda i: (i, 0)),
        ],
        out_specs=[
            pl.BlockSpec((rows, feature), lambda i: (0, 0)),
            pl.BlockSpec((rows, feature), lambda i: (0, 0)),
        ],
        out_shape=[jax.ShapeDtypeStruct((rows, feature), jnp.bfloat16)] * 2,
        scratch_shapes=[pltpu.VMEM((rows, feature), jnp.float32)] * 2,
        compiler_params=pltpu.CompilerParams(vmem_limit_bytes=VMEM_LIMIT),
        cost_estimate=pl.CostEstimate(
            flops=4 * rows * ff * feature,
            bytes_accessed=4 * ff * feature + 4 * ff * rows,
            transcendentals=0,
        ),
        name="back",
    )(weights, hidden, pre_grad)


def window_rows(side, margin, tile):
    ext = tile + 2 * margin
    wins = ext // side
    edge, strip = margin * tile, ext * margin
    into = np.zeros((ext * ext, ext * ext), np.float32)
    outof = np.zeros((tile * tile, ext * ext), np.float32)
    for r in range(ext):
        for c in range(ext):
            at = ((r // side) * wins + c // side) * side * side + (r % side) * side + c % side
            base = tile * tile
            if c < margin:
                piece = base + 2 * edge + r * margin + c
            elif c >= tile + margin:
                piece = base + 2 * edge + strip + r * margin + c - tile - margin
            elif r < margin:
                piece = base + r * tile + c - margin
            elif r >= tile + margin:
                piece = base + edge + (r - tile - margin) * tile + c - margin
            else:
                piece = (r - margin) * tile + c - margin
                outof[piece, at] = 1.0
            into[at, piece] = 1.0
    return into.astype(jnp.bfloat16), outof.astype(jnp.bfloat16)


def placers(target, slots, capacity):
    rows = lax.broadcasted_iota(jnp.int32, (2 * slots, target.shape[1]), 0)
    return rows == target, rows == target + capacity


def front_kernel(
    experts, capacity, at_ref, tok_ref, low_ref, high_ref, left_ref, right_ref, into_ref, outof_ref,
    wqkv_ref, wproj_ref, route_ref, gate_ref, cot_ref, mixed_ref, slots_ref, target_ref, qkv_ref, ctx_ref,
):
    bf16, f32 = jnp.bfloat16, jnp.float32
    tokens = tok_ref[...]
    count, feature = tokens.shape
    cells = window_side * window_side
    head = feature // HEADS
    group = 128 // head
    pieces = jnp.concatenate(
        [tokens, low_ref[...], high_ref[...], left_ref[...], right_ref[...]], axis=0
    )
    placed = jnp.dot(into_ref[...], pieces, preferred_element_type=f32).astype(bf16)
    qkv_ref[...] = jnp.dot(placed, wqkv_ref[...], preferred_element_type=f32).astype(bf16)
    first_row, last_row = at_ref[0] == 0, at_ref[0] == at_ref[1] - 1
    first_col, last_col = at_ref[2] == 0, at_ref[2] == at_ref[3] - 1
    lane = lax.broadcasted_iota(jnp.int32, (1, 128), 1)
    own = [
        ((lane >= h * head) & (lane < (h + 1) * head)).astype(f32) for h in range(group)
    ]
    own16 = [o.astype(bf16) for o in own]
    key = lax.broadcasted_iota(jnp.int32, (cells, 128), 0)
    key_row, key_col = key // window_side, key % window_side
    half = window_side // 2
    low_bias = jnp.float32(-1e30)
    edge_bias = {
        (0, 0): jnp.where(key_row < half, jnp.where(first_row, low_bias, 0.0), 0.0),
        (0, 2): jnp.where(key_row >= half, jnp.where(last_row, low_bias, 0.0), 0.0),
        (1, 0): jnp.where(key_col < half, jnp.where(first_col, low_bias, 0.0), 0.0),
        (1, 2): jnp.where(key_col >= half, jnp.where(last_col, low_bias, 0.0), 0.0),
    }
    scale = 1.0 / math.sqrt(head)
    for window in range(9):
        wi, wj = window // 3, window % 3
        bias = None
        if wi != 1:
            bias = edge_bias[0, wi]
        if wj != 1:
            bias = edge_bias[1, wj] if bias is None else bias + edge_bias[1, wj]
        if bias is not None:
            bias = jnp.concatenate([bias] * (group * cells // 128), axis=1)
        rows = slice(window * cells, (window + 1) * cells)
        for g in range(feature // 128):
            q = qkv_ref[rows, g * 128 : (g + 1) * 128]
            k = qkv_ref[rows, feature + g * 128 : feature + (g + 1) * 128]
            v = qkv_ref[rows, 2 * feature + g * 128 : 2 * feature + (g + 1) * 128]
            spread = jnp.concatenate([q * o for o in own16], axis=0)
            scores = nt(k, spread)
            if bias is not None:
                scores = scores + bias
            peak = jnp.max(scores, axis=0, keepdims=True)
            weights = jnp.exp((scores - peak) * scale)
            probs = (weights * (1.0 / jnp.sum(weights, axis=0, keepdims=True))).astype(bf16)
            wide = tn(probs, v)
            mine = wide[:cells] * own[0]
            for h in range(1, group):
                mine = mine + wide[h * cells : (h + 1) * cells] * own[h]
            ctx_ref[rows, g * 128 : (g + 1) * 128] = mine.astype(bf16)
    context = jnp.dot(outof_ref[...], ctx_ref[...], preferred_element_type=f32).astype(bf16)
    attended = jnp.dot(context, wproj_ref[...], preferred_element_type=f32)
    centred = attended - jnp.mean(attended, axis=-1, keepdims=True)
    spread_of = jnp.mean(centred * centred, axis=-1, keepdims=True)
    mixed = (tokens.astype(f32) + centred * lax.rsqrt(spread_of + 1e-05)).astype(bf16)
    mixed_ref[...] = mixed
    route = route_ref[...]
    matches = lax.broadcasted_iota(jnp.int32, (experts, count), 0) == route
    matches = matches.astype(f32)
    earlier = lax.broadcasted_iota(jnp.int32, (count, count), 0) < lax.broadcasted_iota(
        jnp.int32, (count, count), 1
    )
    before = jnp.dot(
        matches.astype(bf16), earlier.astype(f32).astype(bf16), preferred_element_type=f32
    )
    position = jnp.sum(matches * before, axis=0, keepdims=True).astype(jnp.int32)
    target = route * (2 * capacity) + position
    target_ref[...] = target
    upstream = (gate_ref[...] * cot_ref[...].astype(f32)).astype(bf16)
    place_x, place_g = placers(target, experts * capacity, capacity)
    slots = jnp.dot(place_x.astype(f32).astype(bf16), mixed, preferred_element_type=f32)
    slots = slots + jnp.dot(
        place_g.astype(f32).astype(bf16), upstream, preferred_element_type=f32
    )
    slots_ref[...] = slots.astype(bf16)


def front(at, tokens, low, high, left, right, w_qkv, w_proj, route, gate, cotangent, experts, capacity):
    count, feature = tokens.shape
    into, outof = window_rows(window_side, margin_cells, math.isqrt(count))
    ext = into.shape[0]
    vmem = pl.BlockSpec(memory_space=pltpu.VMEM)
    return pl.pallas_call(
        functools.partial(front_kernel, experts, capacity),
        in_specs=[pl.BlockSpec(memory_space=pltpu.SMEM)] + [vmem] * 12,
        out_specs=[vmem] * 3,
        out_shape=[
            jax.ShapeDtypeStruct((count, feature), jnp.bfloat16),
            jax.ShapeDtypeStruct((2 * experts * capacity, feature), jnp.bfloat16),
            jax.ShapeDtypeStruct((1, count), jnp.int32),
        ],
        scratch_shapes=[
            pltpu.VMEM((ext, 3 * feature), jnp.bfloat16),
            pltpu.VMEM((ext, feature), jnp.bfloat16),
        ],
        compiler_params=pltpu.CompilerParams(vmem_limit_bytes=VMEM_LIMIT),
        cost_estimate=pl.CostEstimate(
            flops=5_000_000_000, bytes_accessed=8_000_000, transcendentals=600_000
        ),
        name="front",
    )(
        at, tokens, low, high, left, right, jnp.asarray(into), jnp.asarray(outof),
        w_qkv, w_proj, route, gate, cotangent,
    )


def combine_kernel(capacity, back_ref, target_ref, mixed_ref, gate_ref, out_ref, grad_ref):
    f32 = jnp.float32
    back_rows = back_ref[...]
    place_x, place_g = placers(target_ref[...], back_rows.shape[0] // 2, capacity)
    token_out = tn(place_x.astype(f32).astype(jnp.bfloat16), back_rows)
    out_ref[...] = (mixed_ref[...].astype(f32) + gate_ref[...] * token_out).astype(jnp.bfloat16)
    grad_ref[...] = tn(place_g.astype(f32).astype(jnp.bfloat16), back_rows).astype(jnp.bfloat16)


def combine(returned, target, mixed, gate, capacity):
    vmem = pl.BlockSpec(memory_space=pltpu.VMEM)
    return pl.pallas_call(
        functools.partial(combine_kernel, capacity),
        in_specs=[vmem] * 4,
        out_specs=[vmem] * 2,
        out_shape=[jax.ShapeDtypeStruct(mixed.shape, jnp.bfloat16)] * 2,
        compiler_params=pltpu.CompilerParams(vmem_limit_bytes=VMEM_LIMIT),
        cost_estimate=pl.CostEstimate(
            flops=800_000_000, bytes_accessed=2_000_000, transcendentals=0
        ),
        name="combine",
    )(returned, target, mixed, gate)


def shifts(axis):
    count = lax.axis_size(axis)
    forward = [(i, i + 1) for i in range(count - 1)]
    return forward, [(target, source) for source, target in forward]


def per_device(tokens, gate, route, cotangent, w_qkv, w_proj, w_up, w_down):
    tile_rows, tile_cols, feature = tokens.shape
    tok_count = tile_rows * tile_cols
    margin = margin_cells
    experts = lax.axis_size("exp")
    capacity = max(2, 3 * tok_count // (2 * experts))
    weights = lax.all_gather(
        jnp.concatenate([w_up, w_down], axis=0), "rep", axis=0, tiled=False
    )
    forward, backward = shifts("rep")
    low = lax.ppermute(tokens[tile_rows - margin :], "rep", forward)
    high = lax.ppermute(tokens[:margin], "rep", backward)
    forward, backward = shifts("exp")

    def strip(cols):
        parts = [low[:, cols], tokens[:, cols], high[:, cols]]
        return jnp.concatenate(parts, axis=0).reshape(-1, feature)

    left = lax.ppermute(strip(slice(tile_cols - margin, tile_cols)), "exp", forward)
    right = lax.ppermute(strip(slice(0, margin)), "exp", backward)
    at = jnp.stack(
        [
            lax.axis_index("rep"),
            jnp.int32(lax.axis_size("rep")),
            lax.axis_index("exp"),
            jnp.int32(experts),
        ]
    ).astype(jnp.int32)
    gate_rows = gate.reshape(tok_count, 1)
    mixed, slots, target = front(
        at,
        tokens.reshape(tok_count, feature),
        low.reshape(-1, feature),
        high.reshape(-1, feature),
        left,
        right,
        w_qkv,
        w_proj,
        route.reshape(1, tok_count),
        gate_rows,
        cotangent.reshape(tok_count, feature),
        experts,
        capacity,
    )
    sent = lax.all_to_all(
        slots.reshape(experts, 2 * capacity, feature), "exp", 0, 0, tiled=True
    )
    slot_rows = sent[:, :capacity].reshape(-1, feature)
    slot_grads = sent[:, capacity:].reshape(-1, feature)
    grads, hidden, pre_grad = middle(weights, slot_rows, slot_grads)
    summed = lax.psum_scatter(grads, "rep", scatter_dimension=0, tiled=True)[0]
    expert_out, input_slots = back(weights, hidden, pre_grad)
    both = jnp.concatenate(
        [
            expert_out.reshape(experts, capacity, feature),
            input_slots.reshape(experts, capacity, feature),
        ],
        axis=1,
    )
    returned = lax.all_to_all(both, "exp", 0, 0, tiled=True).reshape(-1, feature)
    layer_out, input_grad = combine(returned, target, mixed, gate_rows, capacity)
    average_factor = 1.0 / lax.axis_size("rep")
    width = w_up.shape[1]
    total = summed.astype(jnp.float32) * average_factor
    return (
        layer_out.reshape(tile_rows, tile_cols, feature),
        input_grad.reshape(tile_rows, tile_cols, feature),
        total[:width][None],
        total[width:][None],
    )


def solution(mesh):
    placed = (
        P("rep", "exp", None),
        P("rep", "exp"),
        P("rep", "exp", None, None),
        P("rep", "exp", None),
        P(),
        P(),
        P("exp", "rep", None),
        P("exp", "rep", None),
    )
    return jax.shard_map(
        per_device,
        mesh=mesh,
        in_specs=placed,
        out_specs=(
            P("rep", "exp", None),
            P("rep", "exp", None),
            P("exp", "rep", None),
            P("exp", "rep", None),
        ),
        check_vma=False,
    )
```

time: 200 us -> 191 us (0.955)
  local copies, waits for them, and re-layouts: 45.3 us -> 10.8 us
  waiting for transfers between devices: 55.9 us -> 88.2 us
  matrix products: 9.13 us -> 0 us
  Pallas kernels: 14.5 us -> 20.7 us
  other arithmetic: 7.31 us -> 3.31 us
    all_gather x1, waiting for transfers between devices: 0.63 us -> 36.8 us  [per_device(): lax.all_gather(jnp.concatenate([w_up, w_down], axis=0), 'rep', axis=0, ti...]
    unnamed x27 -> x26, local copies, waits for them, and re-layouts: 18.4 us -> 4.82 us
    reshape x10 -> x7, local copies, waits for them, and re-layouts: 13.7 us -> 2.98 us  [the longest x1 1.08 us: per_device(): expert_out.reshape(experts, capacity, feature)]
    dot_general x9 -> x0, matrix products: 9.13 us -> none  [the longest x2 2.11 us: from_slots(): jnp.dot(placer, slot_values.reshape(experts * capacity, feature), preferr...]
    slice x6 -> x5, local copies, waits for them, and re-layouts: 8.33 us -> 2.13 us  [the longest x3 1.06 us: strip(): parts = [low[:, cols], tokens[:, cols], high[:, cols]]]
    pallas_call x0 -> x2, Pallas kernels: none -> 6.09 us  [the longest x1 4.77 us: front(): pl.pallas_call(functools.partial(front_kernel, experts, capacity), in_spe...]
    reduce_scatter x1, waiting for transfers between devices: 54 us -> 49.3 us  [per_device(): summed = lax.psum_scatter(grads, 'rep', scatter_dimension=0, tiled=True)[0]]
    convert_element_type x1 -> x0, local copies, waits for them, and re-layouts: 2.98 us -> none  [window_attend(): context = jnp.einsum('whqk,wkhd->wqhd', probabilities, blocks[:, :, 2], p...]
  transfers between devices with their start and end apart: 6 -> 6, of which waited for: 3 -> 4; matrix products, arithmetic and copies ran while one was open for 27% -> 3% of each run, Pallas kernels for 2% -> 6%
where the time goes in v2:
time: 191 us; the launch traced here: 190 us
  waiting for transfers between devices  88.2 us (46%)
  blocking collectives  41.4 us (22%)
  Pallas kernels  20.7 us (11%)
  between operations  14.3 us (7%)
  starting transfers between devices  11.5 us (6%)
  local copies, waits for them, and re-layouts  10.8 us (6%)
  other arithmetic  3.31 us (2%)
    reduce_scatter x1, waiting for transfers between devices, per_device(): summed = lax.psum_scatter(grads, 'rep', scatter_dimension=0, tiled=True)[0]  49.3 us
    all_gather x1, waiting for transfers between devices, per_device(): lax.all_gather(jnp.concatenate([w_up, w_down], axis=0), 'rep', axis=0, ti...  36.8 us
    all_to_all x1, blocking collectives, per_device(): lax.all_to_all(slots.reshape(experts, 2 * capacity, feature), 'exp', 0, 0...  22.2 us
    all_to_all x1, blocking collectives, per_device(): lax.all_to_all(both, 'exp', 0, 0, tiled=True).reshape(-1, feature)  19.2 us
    pallas_call x1, Pallas kernels, middle(): pl.pallas_call(middle_kernel, grid=(CHUNKS,), in_specs=[pl.BlockSpec((ste...  9.89 us
    unnamed x26, local copies, waits for them, and re-layouts  4.82 us
    pallas_call x1, Pallas kernels, front(): pl.pallas_call(functools.partial(front_kernel, experts, capacity), in_spe...  4.77 us
    pallas_call x1, Pallas kernels, back(): pl.pallas_call(back_kernel, grid=(steps,), in_specs=[pl.BlockSpec((step,...  4.73 us
  transfers between devices with their start and end apart: 6, of which 4 were waited for; matrix products, arithmetic and copies ran while one was open for 3% of the time, Pallas kernels for 6%

profile of v2, /device:TPU:6, one launch (start us, length us, event | category | flops | bytes accessed | tf_op | source)
XLA Modules:
  0.0 190.2 jit_solution(11009724876445651976)
XLA Ops:
  7.2 0.0 copy-start.2
  7.2 0.0 copy-start.6
  7.2 0.0 copy-start.5
  7.2 0.0 copy-start.8
  7.2 0.0 all-gather.3.cloned.1.call-start
  7.3 1.8 pad_maximum_fusion.1
  9.1 0.0 all-gather.3.cloned.1.call-update
  9.1 0.0 reduce-scatter.2.cloned.1.call-start
  9.2 0.9 fusion.3
  10.1 1.3 collective-permute-start.1
  11.4 4.5 %collective-permute-start = (bf16[4,16,512]{2,1,0:T(8,128)(2,1)S(1)}, bf16[4,16,512]{2,1,0:T(8,128)(2,1)S(1)}, u32[]{:S(2)}, u32[]{:S(2)}) collective-permute-start(bf16[4,16,512]{2,1,0:T(8,128)(2,1)S(1)} %get-tuple-element.31), channel_id=1, source_target_pairs={{0,32},{32,64},{64,96},{96,128},{128,160},{160,192},{192,224},{224... | collective-permute-start | bytes 196616 | tf_op jit(solution)/shard_map/ppermute | solution.py:319
  15.9 1.0 fusion.2
  16.9 0.8 reshape.80.gate_ref
  17.8 0.0 copy-start.3
  17.8 0.0 collective-permute-done.1
  17.8 0.0 collective-permute-done
  17.8 0.1 pad_maximum_fusion.3
  17.9 0.1 pad_maximum_fusion.2
  18.1 1.9 %collective-permute-start.2 = (bf16[96,512]{1,0:T(8,128)(2,1)S(1)}, bf16[96,512]{1,0:T(8,128)(2,1)S(1)}, u32[]{:S(2)}, u32[]{:S(2)}) collective-permute-start(bf16[96,512]{1,0:T(8,128)(2,1)S(1)} %reshape.66), channel_id=1, source_target_pairs={{0,1},{1,2},{2,3},{3,4},{4,5},{5,6},{6,7},{7,8},{8,9},{9,10},{10,1... | collective-permute-start | bytes 294920 | tf_op jit(solution)/shard_map/ppermute | solution.py:327
  20.0 3.6 %collective-permute-start.3 = (bf16[96,512]{1,0:T(8,128)(2,1)S(1)}, bf16[96,512]{1,0:T(8,128)(2,1)S(1)}, u32[]{:S(2)}, u32[]{:S(2)}) collective-permute-start(bf16[96,512]{1,0:T(8,128)(2,1)S(1)} %reshape.67), channel_id=1, source_target_pairs={{1,0},{2,1},{3,2},{4,3},{5,4},{6,5},{7,6},{8,7},{9,8},{10,9},{11,1... | collective-permute-start | bytes 294920 | tf_op jit(solution)/shard_map/ppermute | solution.py:328
  23.6 0.1 pad_add_fusion.at_ref
  23.7 0.3 collective-permute-done.2.left_ref
  24.0 1.8 collective-permute-done.3.right_ref
  25.8 0.0 copy-done.2
  25.8 0.0 copy-done.6
  25.8 0.0 copy-done.5
  25.8 0.0 copy-done.8
  25.8 0.0 copy-start.7
  25.9 0.9 copy-done.7
  26.8 0.0 copy-start.9
  26.8 1.1 copy-done.9
  27.9 0.0 copy-start.10
  27.9 1.0 copy-done.10
  28.9 4.8 %front.1 = (bf16[256,512]{1,0:T(8,128)(2,1)S(1)}, bf16[768,512]{1,0:T(8,128)(2,1)S(1)}, s32[1,256]{1,0:T(1,128)S(1)}) custom-call(s32[4]{0:T(128)S(1)} %pad_add_fusion.at_ref, bf16[256,512]{1,0:T(8,128)(2,1)S(1)} %bitcast.14, bf16[64,512]{1,0:T(8,128)(2,1)S(1)} %bitcast.16, bf16[64,512]{1,0:T(8,128)(2,1)S(1)} %bitcast.15, ...), custom_call_target="tpu_custom_call" | custom-call | flops 5000000000 | bytes 8000000 | tf_op jit(solution)/shard_map/front/pallas_call | solution.py:255
  33.7 0.0 copy-done.3
  33.7 0.0 copy-start.11
  33.7 22.2 %all_to_all.10 = bf16[32,24,512]{2,1,0:T(8,128)(2,1)S(1)} all-to-all(bf16[32,24,512]{2,1,0:T(8,128)(2,1)S(1)} %bitcast.12), channel_id=1, replica_groups=mesh['rep'=16,'exp'=32] {'exp'}, dimensions={0} | all-to-all | bytes 1572864 | tf_op jit(solution)/shard_map/all_to_all | solution.py:353
  55.9 0.2 fusion
  56.1 0.0 copy-done.11
  56.1 0.1 reshape.73.g_ref
  56.2 0.9 reshape.72.x_ref
  57.1 36.8 %all-gather.3.cloned.1.call-done = bf16[32,128,512]{2,1,0:T(8,128)(2,1)} async-done(((bf16[2,128,512]{2,1,0:T(8,128)(2,1)}), bf16[32,128,512]{2,1,0:T(8,128)(2,1)}) %all-gather.3.cloned.1.call-update) | async-done | bytes 4194320 | tf_op jit(solution)/shard_map/all_gather | solution.py:315
  93.9 0.0 copy-start
  93.9 1.0 copy-done
  94.9 9.9 %middle.1 = (bf16[16,256,512]{2,1,0:T(8,128)(2,1)}, bf16[2048,384]{1,0:T(8,128)(2,1)S(1)}, bf16[2048,384]{1,0:T(8,128)(2,1)S(1)}) custom-call(bf16[16,2,128,512]{3,2,1,0:T(8,128)(2,1)} %bitcast.19, bf16[384,512]{1,0:T(8,128)(2,1)S(1)} %copy-done, bf16[384,512]{1,0:T(8,128)(2,1)S(1)} %reshape.73.g_ref), custom_call_target="tpu_custom_call" | custom-call | flops 3221225472 | bytes 11534336 | tf_op jit(solution)/shard_map/middle/pallas_call | solution.py:58
  104.8 0.0 reduce-scatter.2.cloned.1.call-update
  104.8 4.7 %back.1 = (bf16[384,512]{1,0:T(8,128)(2,1)S(1)}, bf16[384,512]{1,0:T(8,128)(2,1)S(1)}) custom-call(bf16[16,2,128,512]{3,2,1,0:T(8,128)(2,1)} %bitcast.20, bf16[2048,384]{1,0:T(8,128)(2,1)S(1)} %get-tuple-element.15.hid_ref, bf16[2048,384]{1,0:T(8,128)(2,1)S(1)} %get-tuple-element.16.pg_ref), custom_call_target="tpu_custom_call" | custom-call | flops 1610612736 | bytes 7340032 | tf_op jit(solution)/shard_map/back/pallas_call | solution.py:110
  109.5 0.0 copy-start.1
  109.5 0.8 copy-done.1
  110.3 1.1 reshape.74
  111.4 0.1 reshape.75
  111.5 0.0 copy-start.4
  111.5 0.0 copy-start.12
  111.5 0.2 pad_maximum_fusion
  111.7 19.2 %all_to_all.11 = bf16[32,24,512]{2,1,0:T(8,128)(2,1)S(1)} all-to-all(bf16[32,24,512]{2,1,0:T(8,128)(2,1)S(1)} %pad_maximum_fusion), channel_id=1, replica_groups=mesh['rep'=16,'exp'=32] {'exp'}, dimensions={0} | all-to-all | bytes 1572864 | tf_op jit(solution)/shard_map/all_to_all | solution.py:368
  131.0 0.0 copy-done.4
  131.0 0.0 copy-done.12
  131.0 1.3 combine.1
  132.3 49.3 %reduce-scatter.2.cloned.1.call-done = bf16[1,256,512]{2,1,0:T(8,128)(2,1)} async-done(((bf16[16,256,512]{2,1,0:T(8,128)(2,1)}), bf16[1,256,512]{2,1,0:T(8,128)(2,1)}) %reduce-scatter.2.cloned.1.call-update) | async-done | bytes 262160 | tf_op jit(solution)/shard_map/reduce_scatter | solution.py:359
  181.5 1.0 convert_multiply_fusion
  182.5 0.8 fusion.1
  (4 shorter events, 0.1 us)
Async XLA Ops:
  7.2 18.7 %copy-start.2 = (bf16[16,16,512]{2,1,0:T(8,128)(2,1)S(1)}, bf16[16,16,512]{2,1,0:T(8,128)(2,1)}, u32[]{:S(2)}) copy-start(bf16[16,16,512]{2,1,0:T(8,128)(2,1)} %param.10) | copy-start | bytes 786436
  7.2 18.7 %copy-start.6 = (bf16[512,512]{1,0:T(8,128)(2,1)S(1)}, bf16[512,512]{1,0:T(8,128)(2,1)}, u32[]{:S(2)}) copy-start(bf16[512,512]{1,0:T(8,128)(2,1)} %wproj_ref.1) | copy-start | bytes 1572868
  7.2 18.7 %copy-start.5 = (bf16[512,1536]{1,0:T(8,128)(2,1)S(1)}, bf16[512,1536]{1,0:T(8,128)(2,1)}, u32[]{:S(2)}) copy-start(bf16[512,1536]{1,0:T(8,128)(2,1)} %wqkv_ref.1) | copy-start | bytes 4718596
  7.2 18.6 %copy-start.8 = (s32[1,1,256,1]{2,3,1,0:T(1,128)S(1)}, s32[1,1,256,1]{2,3,1,0:T(1,128)}, u32[]{:S(2)}) copy-start(s32[1,1,256,1]{2,3,1,0:T(1,128)} %param.12) | copy-start | bytes 3076
  7.2 86.7 %all-gather.3.cloned.1.call-start = ((), (), s32[]{:S(2)}) async-start(), calls=%async_computation.4 | async-start | bytes 4456448 | tf_op jit(solution)/shard_map/all_gather | solution.py:315
  9.1 172.4 %reduce-scatter.2.cloned.1.call-start = ((), (), s32[]{:S(2)}) async-start(), calls=%async_computation.3 | async-start | bytes 4456448 | tf_op jit(solution)/shard_map/reduce_scatter | solution.py:359
  10.1 7.7 %collective-permute-start.1 = (bf16[4,16,512]{2,1,0:T(8,128)(2,1)S(1)}, bf16[4,16,512]{2,1,0:T(8,128)(2,1)S(1)}, u32[]{:S(2)}, u32[]{:S(2)}) collective-permute-start(bf16[4,16,512]{2,1,0:T(8,128)(2,1)S(1)} %get-tuple-element.30), channel_id=1, source_target_pairs={{32,0},{64,32},{96,64},{128,96},{160,128},{192,160},{224,192},{256... | collective-permute-start | bytes 196616 | tf_op jit(solution)/shard_map/ppermute | solution.py:320
  11.4 6.4 %collective-permute-start = (bf16[4,16,512]{2,1,0:T(8,128)(2,1)S(1)}, bf16[4,16,512]{2,1,0:T(8,128)(2,1)S(1)}, u32[]{:S(2)}, u32[]{:S(2)}) collective-permute-start(bf16[4,16,512]{2,1,0:T(8,128)(2,1)S(1)} %get-tuple-element.31), channel_id=1, source_target_pairs={{0,32},{32,64},{64,96},{96,128},{128,160},{160,192},{192,224},{224... | collective-permute-start | bytes 196616 | tf_op jit(solution)/shard_map/ppermute | solution.py:319
  17.8 15.9 %copy-start.3 = (f32[256,1]{1,0:T(8,128)}, f32[256,1]{1,0:T(8,128)S(1)}, u32[]{:S(2)}) copy-start(f32[256,1]{1,0:T(8,128)S(1)} %reshape.80.gate_ref) | copy-start | bytes 3076
  18.1 5.9 %collective-permute-start.2 = (bf16[96,512]{1,0:T(8,128)(2,1)S(1)}, bf16[96,512]{1,0:T(8,128)(2,1)S(1)}, u32[]{:S(2)}, u32[]{:S(2)}) collective-permute-start(bf16[96,512]{1,0:T(8,128)(2,1)S(1)} %reshape.66), channel_id=1, source_target_pairs={{0,1},{1,2},{2,3},{3,4},{4,5},{5,6},{6,7},{7,8},{8,9},{9,10},{10,1... | collective-permute-start | bytes 294920 | tf_op jit(solution)/shard_map/ppermute | solution.py:327
  20.0 5.8 %collective-permute-start.3 = (bf16[96,512]{1,0:T(8,128)(2,1)S(1)}, bf16[96,512]{1,0:T(8,128)(2,1)S(1)}, u32[]{:S(2)}, u32[]{:S(2)}) collective-permute-start(bf16[96,512]{1,0:T(8,128)(2,1)S(1)} %reshape.67), channel_id=1, source_target_pairs={{1,0},{2,1},{3,2},{4,3},{5,4},{6,5},{7,6},{8,7},{9,8},{10,9},{11,1... | collective-permute-start | bytes 294920 | tf_op jit(solution)/shard_map/ppermute | solution.py:328
  25.8 1.0 copy-start.7
  26.8 1.1 copy-start.9
  27.9 1.0 copy-start.10
  33.7 22.4 %copy-start.11 = (bf16[256,512]{1,0:T(8,128)(2,1)}, bf16[256,512]{1,0:T(8,128)(2,1)S(1)}, u32[]{:S(2)}) copy-start(bf16[256,512]{1,0:T(8,128)(2,1)S(1)} %get-tuple-element.20.mixed_ref) | copy-start | bytes 786436
  93.9 1.0 copy-start
  109.5 0.8 copy-start.1
  111.5 19.5 %copy-start.4 = (f32[256,1]{1,0:T(8,128)S(1)}, f32[256,1]{1,0:T(8,128)}, u32[]{:S(2)}) copy-start(f32[256,1]{1,0:T(8,128)} %copy-done.3) | copy-start | bytes 3076
  111.5 19.5 %copy-start.12 = (bf16[256,512]{1,0:T(8,128)(2,1)S(1)}, bf16[256,512]{1,0:T(8,128)(2,1)}, u32[]{:S(2)}) copy-start(bf16[256,512]{1,0:T(8,128)(2,1)} %copy-done.11) | copy-start | bytes 786436
Sparse Core Ops, SparseCore 0:
  10.7 83.1 all-gather.2
  104.9 76.5 reduce-scatter.1

commit v3 on v2

--- a/solution.py
+++ b/solution.py
@@ -15,9 +15,9 @@
 GELU_C = math.sqrt(2.0 / math.pi)
 window_side = 8
 margin_cells = 4
-CHUNKS = 8
-
-VMEM_LIMIT = 48 * 1024 * 1024
+CHUNKS = 4
+
+VMEM_LIMIT = 24 * 1024 * 1024
 
 
 def nt(a, b):
@@ -28,62 +28,99 @@
     return lax.dot_general(a, b, (((0,), (0,)), ((), ())), preferred_element_type=jnp.float32)
 
 
-def middle_kernel(w_ref, x_ref, g_ref, grads_ref, hid_ref, pg_ref):
+def unpack_kernel(capacity, sent_ref, x_ref, g_ref):
+    f32, bf16 = jnp.float32, jnp.bfloat16
+    sent = sent_ref[...]
+    own = sent.shape[0] // 2
+    row = lax.broadcasted_iota(jnp.int32, (own, 2 * own), 0)
+    expert = ((row.astype(f32) + 0.5) * (1.0 / capacity)).astype(jnp.int32)
+    place = lax.broadcasted_iota(jnp.int32, (own, 2 * own), 1) - (row + capacity * expert)
+    x_ref[...] = jnp.dot(
+        (place == 0).astype(f32).astype(bf16), sent, preferred_element_type=f32
+    ).astype(bf16)
+    g_ref[...] = jnp.dot(
+        (place == capacity).astype(f32).astype(bf16), sent, preferred_element_type=f32
+    ).astype(bf16)
+
+
+def unpack(sent, capacity):
+    rows, feature = sent.shape
+    vmem = pl.BlockSpec(memory_space=pltpu.VMEM)
+    return pl.pallas_call(
+        functools.partial(unpack_kernel, capacity),
+        in_specs=[vmem],
+        out_specs=[vmem] * 2,
+        out_shape=[jax.ShapeDtypeStruct((rows // 2, feature), jnp.bfloat16)] * 2,
+        compiler_params=pltpu.CompilerParams(vmem_limit_bytes=VMEM_LIMIT),
+        cost_estimate=pl.CostEstimate(
+            flops=600_000_000, bytes_accessed=1_600_000, transcendentals=0
+        ),
+        name="unpack",
+    )(sent)
+
+
+def middle_kernel(w_ref, *refs):
+    slots, (grads_ref, hid_ref, pg_ref) = refs[:-3], refs[-3:]
     shards, _, width, feature = w_ref.shape
     up = w_ref[:, 0].reshape(shards * width, feature)
     down = w_ref[:, 1].reshape(shards * width, feature)
-    x, g = x_ref[...], g_ref[...]
-    pre = nt(up, x)
-    square = pre * pre
-    inner = jnp.tanh(pre * (GELU_C + (GELU_C * 0.044715) * square))
-    half = 0.5 + 0.5 * inner
-    hidden = (pre * half).astype(jnp.bfloat16)
-    slope = half + (0.5 * pre) * (1.0 - inner * inner) * (
-        GELU_C + (3.0 * 0.044715 * GELU_C) * square
-    )
-    pre_grad = (nt(down, g) * slope).astype(jnp.bfloat16)
-    hid_ref[...] = hidden
-    pg_ref[...] = pre_grad
-    grad_up = jnp.dot(pre_grad, x, preferred_element_type=jnp.float32).astype(jnp.bfloat16)
-    grad_down = jnp.dot(hidden, g, preferred_element_type=jnp.float32).astype(jnp.bfloat16)
-    grads_ref[:, :width] = grad_up.reshape(shards, width, feature)
-    grads_ref[:, width:] = grad_down.reshape(shards, width, feature)
-
-
-def middle(weights, slot_x, slot_g):
+    rows = slots[0].shape[0]
+    halves = len(slots) // 2
+    pres = [nt(up, slots[2 * n][...]) for n in range(halves)]
+    backs = [nt(down, slots[2 * n + 1][...]) for n in range(halves)]
+    grad_up = grad_down = None
+    for n in range(halves):
+        pre = pres[n]
+        square = pre * pre
+        inner = jnp.tanh(pre * (GELU_C + (GELU_C * 0.044715) * square))
+        half = 0.5 + 0.5 * inner
+        hidden = (pre * half).astype(jnp.bfloat16)
+        slope = half + (0.5 * pre) * (1.0 - inner * inner) * (
+            GELU_C + (3.0 * 0.044715 * GELU_C) * square
+        )
+        pre_grad = (backs[n] * slope).astype(jnp.bfloat16)
+        hid_ref[:, n * rows : (n + 1) * rows] = hidden
+        pg_ref[:, n * rows : (n + 1) * rows] = pre_grad
+        by_up = jnp.dot(pre_grad, slots[2 * n][...], preferred_element_type=jnp.float32)
+        by_down = jnp.dot(hidden, slots[2 * n + 1][...], preferred_element_type=jnp.float32)
+        grad_up = by_up if grad_up is None else grad_up + by_up
+        grad_down = by_down if grad_down is None else grad_down + by_down
+    grads_ref[:, :width] = grad_up.astype(jnp.bfloat16).reshape(shards, width, feature)
+    grads_ref[:, width:] = grad_down.astype(jnp.bfloat16).reshape(shards, width, feature)
+
+
+def middle(weights, slots):
     owners, _, width, feature = weights.shape
-    rows = slot_x.shape[0]
+    rows = slots[0].shape[0]
     step = owners // CHUNKS
     ff = owners * width
+    total = rows * len(slots) // 2
     return pl.pallas_call(
         middle_kernel,
         grid=(CHUNKS,),
-        in_specs=[
-            pl.BlockSpec((step, 2, width, feature), lambda i: (i, 0, 0, 0)),
-            pl.BlockSpec((rows, feature), lambda i: (0, 0)),
-            pl.BlockSpec((rows, feature), lambda i: (0, 0)),
-        ],
+        in_specs=[pl.BlockSpec((step, 2, width, feature), lambda i: (i, 0, 0, 0))]
+        + [pl.BlockSpec((rows, feature), lambda i: (0, 0))] * len(slots),
         out_specs=[
             pl.BlockSpec((step, 2 * width, feature), lambda i: (i, 0, 0)),
-            pl.BlockSpec((step * width, rows), lambda i: (i, 0)),
-            pl.BlockSpec((step * width, rows), lambda i: (i, 0)),
+            pl.BlockSpec((step * width, total), lambda i: (i, 0)),
+            pl.BlockSpec((step * width, total), lambda i: (i, 0)),
         ],
         out_shape=[
-            jax.ShapeDtypeStruct((owners, 2 * width, feature), jnp.bfloat16),
-            jax.ShapeDtypeStruct((ff, rows), jnp.bfloat16),
-            jax.ShapeDtypeStruct((ff, rows), jnp.bfloat16),
-        ],
-        compiler_params=pltpu.CompilerParams(vmem_limit_bytes=VMEM_LIMIT),
-        cost_estimate=pl.CostEstimate(
-            flops=8 * rows * ff * feature,
-            bytes_accessed=8 * ff * feature + 4 * ff * rows,
-            transcendentals=ff * rows,
+            pltpu.HBM((owners, 2 * width, feature), jnp.bfloat16),
+            pltpu.HBM((ff, total), jnp.bfloat16),
+            pltpu.HBM((ff, total), jnp.bfloat16),
+        ],
+        compiler_params=pltpu.CompilerParams(vmem_limit_bytes=VMEM_LIMIT),
+        cost_estimate=pl.CostEstimate(
+            flops=8 * total * ff * feature,
+            bytes_accessed=8 * ff * feature + 4 * ff * total,
+            transcendentals=ff * total,
         ),
         name="middle",
-    )(weights, slot_x, slot_g)
-
-
-def back_kernel(w_ref, hid_ref, pg_ref, out_ref, in_ref, out_acc, in_acc):
+    )(weights, *slots)
+
+
+def back_kernel(w_ref, hid_ref, pg_ref, kept_ref, given_ref, out_acc, in_acc):
     shards, _, width, feature = w_ref.shape
     up = w_ref[:, 0].reshape(shards * width, feature)
     down = w_ref[:, 1].reshape(shards * width, feature)
@@ -98,8 +135,11 @@
 
     @pl.when(pl.program_id(0) == pl.num_programs(0) - 1)
     def _():
-        out_ref[...] = out_acc[...].astype(jnp.bfloat16)
-        in_ref[...] = in_acc[...].astype(jnp.bfloat16)
+        own = out_acc.shape[0] // 2
+        kept_ref[:own] = out_acc[:own]
+        kept_ref[own:] = in_acc[:own]
+        given_ref[:own] = out_acc[own:].astype(jnp.bfloat16)
+        given_ref[own:] = in_acc[own:].astype(jnp.bfloat16)
 
 
 def back(weights, hidden, pre_grad):
@@ -119,7 +159,10 @@
             pl.BlockSpec((rows, feature), lambda i: (0, 0)),
             pl.BlockSpec((rows, feature), lambda i: (0, 0)),
         ],
-        out_shape=[jax.ShapeDtypeStruct((rows, feature), jnp.bfloat16)] * 2,
+        out_shape=[
+            jax.ShapeDtypeStruct((rows, feature), jnp.float32),
+            jax.ShapeDtypeStruct((rows, feature), jnp.bfloat16),
+        ],
         scratch_shapes=[pltpu.VMEM((rows, feature), jnp.float32)] * 2,
         compiler_params=pltpu.CompilerParams(vmem_limit_bytes=VMEM_LIMIT),
         cost_estimate=pl.CostEstimate(
@@ -129,6 +172,36 @@
         ),
         name="back",
     )(weights, hidden, pre_grad)
+
+
+def assemble_kernel(capacity, kept_ref, got_ref, both_ref):
+    f32, bf16 = jnp.float32, jnp.bfloat16
+    total = (kept_ref[...] + got_ref[...].astype(f32)).astype(bf16)
+    rows = total.shape[0]
+    own = rows // 2
+    column = lax.broadcasted_iota(jnp.int32, (rows, own), 1)
+    expert = ((column.astype(f32) + 0.5) * (1.0 / capacity)).astype(jnp.int32)
+    place = lax.broadcasted_iota(jnp.int32, (rows, own), 0) - (column + capacity * expert)
+    both = jnp.dot((place == 0).astype(f32).astype(bf16), total[:own], preferred_element_type=f32)
+    both = both + jnp.dot(
+        (place == capacity).astype(f32).astype(bf16), total[own:], preferred_element_type=f32
+    )
+    both_ref[...] = both.astype(bf16)
+
+
+def assemble(kept, got, capacity):
+    vmem = pl.BlockSpec(memory_space=pltpu.VMEM)
+    return pl.pallas_call(
+        functools.partial(assemble_kernel, capacity),
+        in_specs=[vmem] * 2,
+        out_specs=vmem,
+        out_shape=jax.ShapeDtypeStruct(got.shape, jnp.bfloat16),
+        compiler_params=pltpu.CompilerParams(vmem_limit_bytes=VMEM_LIMIT),
+        cost_estimate=pl.CostEstimate(
+            flops=800_000_000, bytes_accessed=3_000_000, transcendentals=0
+        ),
+        name="assemble",
+    )(kept, got)
 
 
 def window_rows(side, margin, tile):
@@ -306,14 +379,25 @@
     return forward, [(target, source) for source, target in forward]
 
 
+def sharing(axis):
+    count = lax.axis_size(axis)
+    groups = [list(range(parity, count, 2)) for parity in range(2)]
+    return groups, [(i, i ^ 1) for i in range(count)]
+
+
 def per_device(tokens, gate, route, cotangent, w_qkv, w_proj, w_up, w_down):
     tile_rows, tile_cols, feature = tokens.shape
     tok_count = tile_rows * tile_cols
     margin = margin_cells
     experts = lax.axis_size("exp")
     capacity = max(2, 3 * tok_count // (2 * experts))
+    groups, swap = sharing("rep")
     weights = lax.all_gather(
-        jnp.concatenate([w_up, w_down], axis=0), "rep", axis=0, tiled=False
+        jnp.concatenate([w_up, w_down], axis=0),
+        "rep",
+        axis=0,
+        tiled=False,
+        axis_index_groups=groups,
     )
     forward, backward = shifts("rep")
     low = lax.ppermute(tokens[tile_rows - margin :], "rep", forward)
@@ -353,19 +437,18 @@
     sent = lax.all_to_all(
         slots.reshape(experts, 2 * capacity, feature), "exp", 0, 0, tiled=True
     )
-    slot_rows = sent[:, :capacity].reshape(-1, feature)
-    slot_grads = sent[:, capacity:].reshape(-1, feature)
-    grads, hidden, pre_grad = middle(weights, slot_rows, slot_grads)
-    summed = lax.psum_scatter(grads, "rep", scatter_dimension=0, tiled=True)[0]
-    expert_out, input_slots = back(weights, hidden, pre_grad)
-    both = jnp.concatenate(
-        [
-            expert_out.reshape(experts, capacity, feature),
-            input_slots.reshape(experts, capacity, feature),
-        ],
-        axis=1,
-    )
-    returned = lax.all_to_all(both, "exp", 0, 0, tiled=True).reshape(-1, feature)
+    sent = sent.reshape(-1, feature)
+    other = lax.ppermute(sent, "rep", swap)
+    slot_parts = [*unpack(sent, capacity), *unpack(other, capacity)]
+    grads, hidden, pre_grad = middle(weights, slot_parts)
+    summed = lax.psum_scatter(
+        grads, "rep", scatter_dimension=0, tiled=True, axis_index_groups=groups
+    )[0]
+    kept, given = back(weights, hidden, pre_grad)
+    both = assemble(kept, lax.ppermute(given, "rep", swap), capacity)
+    returned = lax.all_to_all(
+        both.reshape(experts, 2 * capacity, feature), "exp", 0, 0, tiled=True
+    ).reshape(-1, feature)
     layer_out, input_grad = combine(returned, target, mixed, gate_rows, capacity)
     average_factor = 1.0 / lax.axis_size("rep")
     width = w_up.shape[1]

time: 191 us -> 193 us (1.010)
  the two profiles are of different devices: /device:TPU:6 before, /device:TPU:65 now
where the time goes in v3:
time: 193 us; the launch traced here: 192 us
  waiting for transfers between devices  73.9 us (38%)
  blocking collectives  50.4 us (26%)
  starting transfers between devices  19.9 us (10%)
  Pallas kernels  18.1 us (9%)
  between operations  14.3 us (7%)
  local copies, waits for them, and re-layouts  12.6 us (7%)
  other arithmetic  3.07 us (2%)
    ppermute x1, waiting for transfers between devices, per_device(): both = assemble(kept, lax.ppermute(given, 'rep', swap), capacity)  42.9 us
    ppermute x1, waiting for transfers between devices, per_device(): other = lax.ppermute(sent, 'rep', swap)  28.8 us
    all_to_all x1, blocking collectives, per_device(): lax.all_to_all(both.reshape(experts, 2 * capacity, feature), 'exp', 0, 0,...  27.6 us
    all_to_all x1, blocking collectives, per_device(): lax.all_to_all(slots.reshape(experts, 2 * capacity, feature), 'exp', 0, 0...  22.8 us
    unnamed x22, local copies, waits for them, and re-layouts  9.02 us
    pallas_call x1, Pallas kernels, middle(): pl.pallas_call(middle_kernel, grid=(CHUNKS,), in_specs=[pl.BlockSpec((ste...  6.43 us
    pallas_call x1, Pallas kernels, front(): pl.pallas_call(functools.partial(front_kernel, experts, capacity), in_spe...  4.77 us
    ppermute x1, starting transfers between devices, per_device(): lax.ppermute(strip(slice(tile_cols - margin, tile_cols)), 'exp', forward)  4.5 us
  transfers between devices with their start and end apart: 8, of which 3 were waited for; matrix products, arithmetic and copies ran while one was open for 2% of the time, Pallas kernels for 6%

profile of v3, /device:TPU:65, one launch (start us, length us, event | category | flops | bytes accessed | tf_op | source)
XLA Modules:
  0.0 192.2 jit_solution(7298045114949134839)
XLA Ops:
  7.2 0.0 copy-start
  7.2 0.0 copy-start.4
  7.2 0.0 copy-start.3
  7.2 0.0 copy-start.6
  7.2 0.0 all-gather.3.cloned.1.call-start
  7.3 1.8 pad_maximum_fusion
  9.1 0.0 all-gather.3.cloned.1.call-update
  9.1 0.0 reduce-scatter.2.cloned.1.call-start
  9.2 0.9 fusion.2
  10.1 1.9 collective-permute-start.1
  12.0 3.5 %collective-permute-start = (bf16[4,16,512]{2,1,0:T(8,128)(2,1)S(1)}, bf16[4,16,512]{2,1,0:T(8,128)(2,1)S(1)}, u32[]{:S(2)}, u32[]{:S(2)}) collective-permute-start(bf16[4,16,512]{2,1,0:T(8,128)(2,1)S(1)} %get-tuple-element.37), channel_id=1, source_target_pairs={{0,32},{32,64},{64,96},{96,128},{128,160},{160,192},{192,224},{224... | collective-permute-start | bytes 196616 | tf_op jit(solution)/shard_map/ppermute | solution.py:403
  15.5 1.0 fusion.1
  16.6 0.8 reshape.72.gate_ref
  17.4 0.0 collective-permute-done.1
  17.4 0.0 collective-permute-done
  17.4 0.1 pad_maximum_fusion.2
  17.6 0.1 pad_maximum_fusion.1
  17.7 4.5 %collective-permute-start.2 = (bf16[96,512]{1,0:T(8,128)(2,1)S(1)}, bf16[96,512]{1,0:T(8,128)(2,1)S(1)}, u32[]{:S(2)}, u32[]{:S(2)}) collective-permute-start(bf16[96,512]{1,0:T(8,128)(2,1)S(1)} %reshape.60), channel_id=1, source_target_pairs={{0,1},{1,2},{2,3},{3,4},{4,5},{5,6},{6,7},{7,8},{8,9},{9,10},{10,1... | collective-permute-start | bytes 294920 | tf_op jit(solution)/shard_map/ppermute | solution.py:411
  22.2 3.7 %collective-permute-start.3 = (bf16[96,512]{1,0:T(8,128)(2,1)S(1)}, bf16[96,512]{1,0:T(8,128)(2,1)S(1)}, u32[]{:S(2)}, u32[]{:S(2)}) collective-permute-start(bf16[96,512]{1,0:T(8,128)(2,1)S(1)} %reshape.61), channel_id=1, source_target_pairs={{1,0},{2,1},{3,2},{4,3},{5,4},{6,5},{7,6},{8,7},{9,8},{10,9},{11,1... | collective-permute-start | bytes 294920 | tf_op jit(solution)/shard_map/ppermute | solution.py:412
  25.9 0.1 pad_add_fusion.at_ref
  25.9 0.0 collective-permute-done.2.left_ref
  25.9 2.2 %collective-permute-done.3.right_ref = bf16[96,512]{1,0:T(8,128)(2,1)S(1)} collective-permute-done((bf16[96,512]{1,0:T(8,128)(2,1)S(1)}, bf16[96,512]{1,0:T(8,128)(2,1)S(1)}, u32[]{:S(2)}, u32[]{:S(2)}) %collective-permute-start.3) | collective-permute-done | bytes 98336 | tf_op jit(solution)/shard_map/ppermute | solution.py:412
  28.1 0.0 copy-done
  28.1 0.0 copy-done.4
  28.1 0.0 copy-done.3
  28.1 0.0 copy-done.6
  28.1 0.0 copy-start.5
  28.1 0.9 copy-done.5
  29.1 0.0 copy-start.7
  29.1 1.1 copy-done.7
  30.2 0.0 copy-start.8
  30.2 1.0 copy-done.8
  31.2 4.8 %front.1 = (bf16[256,512]{1,0:T(8,128)(2,1)S(1)}, bf16[768,512]{1,0:T(8,128)(2,1)S(1)}, s32[1,256]{1,0:T(1,128)S(1)}) custom-call(s32[4]{0:T(128)S(1)} %pad_add_fusion.at_ref, bf16[256,512]{1,0:T(8,128)(2,1)S(1)} %bitcast.19, bf16[64,512]{1,0:T(8,128)(2,1)S(1)} %bitcast.21, bf16[64,512]{1,0:T(8,128)(2,1)S(1)} %bitcast.20, ...), custom_call_target="tpu_custom_call" | custom-call | flops 5000000000 | bytes 8000000 | tf_op jit(solution)/shard_map/front/pallas_call | solution.py:328
  36.0 22.8 %all_to_all.10 = bf16[32,24,512]{2,1,0:T(8,128)(2,1)S(1)} all-to-all(bf16[32,24,512]{2,1,0:T(8,128)(2,1)S(1)} %bitcast.15), channel_id=1, replica_groups=mesh['rep'=16,'exp'=32] {'exp'}, dimensions={0} | all-to-all | bytes 1572864 | tf_op jit(solution)/shard_map/all_to_all | solution.py:437
  58.7 4.3 %collective-permute-start.4 = (bf16[768,512]{1,0:T(8,128)(2,1)S(1)}, bf16[768,512]{1,0:T(8,128)(2,1)S(1)}, u32[]{:S(2)}, u32[]{:S(2)}) collective-permute-start(bf16[768,512]{1,0:T(8,128)(2,1)S(1)} %bitcast.16), channel_id=1, source_target_pairs={{0,32},{32,0},{64,96},{96,64},{128,160},{160,128},{192,224},{224,1... | collective-permute-start | bytes 2359304 | tf_op jit(solution)/shard_map/ppermute | solution.py:441
  63.0 0.8 unpack.2
  63.8 28.8 %collective-permute-done.4.sent_ref = bf16[768,512]{1,0:T(8,128)(2,1)S(1)} collective-permute-done((bf16[768,512]{1,0:T(8,128)(2,1)S(1)}, bf16[768,512]{1,0:T(8,128)(2,1)S(1)}, u32[]{:S(2)}, u32[]{:S(2)}) %collective-permute-start.4) | collective-permute-done | bytes 786464 | tf_op jit(solution)/shard_map/ppermute | solution.py:441
  92.6 0.8 unpack.3
  93.4 0.0 all-gather.3.cloned.1.call-done
  93.4 0.0 copy-start.1
  93.4 1.6 copy-done.1
  95.0 6.4 %middle.1 = (bf16[8,256,512]{2,1,0:T(8,128)(2,1)}, bf16[1024,768]{1,0:T(8,128)(2,1)}, bf16[1024,768]{1,0:T(8,128)(2,1)}) custom-call(bf16[8,2,128,512]{3,2,1,0:T(8,128)(2,1)S(1)} %bitcast.22, bf16[384,512]{1,0:T(8,128)(2,1)S(1)} %get-tuple-element.19.refs_0_, bf16[384,512]{1,0:T(8,128)(2,1)S(1)} %get-tuple-element.20.refs_1_, ...), custom_call_target="tpu_custom_call" | custom-call | flops 3221225472 | bytes 7340032 | tf_op jit(solution)/shard_map/middle/pallas_call | solution.py:98
  101.4 0.0 copy-start.2
  101.5 0.0 reduce-scatter.2.cloned.1.call-update
  101.5 1.6 copy-done.2
  103.0 0.0 copy-start.9
  103.0 1.4 copy-done.9
  104.4 0.0 copy-start.10
  104.5 1.4 copy-done.10
  105.9 2.9 %back.1 = (f32[768,512]{1,0:T(8,128)S(1)}, bf16[768,512]{1,0:T(8,128)(2,1)S(1)}) custom-call(bf16[8,2,128,512]{3,2,1,0:T(8,128)(2,1)S(1)} %bitcast.23, bf16[1024,768]{1,0:T(8,128)(2,1)S(1)} %copy-done.9, bf16[1024,768]{1,0:T(8,128)(2,1)S(1)} %copy-done.10), custom_call_target="tpu_custom_call" | custom-call | flops 1610612736 | bytes 5242880 | tf_op jit(solution)/shard_map/back/pallas_call | solution.py:150
  108.8 1.9 collective-permute-start.5
  110.7 42.9 %collective-permute-done.5.got_ref = bf16[768,512]{1,0:T(8,128)(2,1)S(1)} collective-permute-done((bf16[768,512]{1,0:T(8,128)(2,1)S(1)}, bf16[768,512]{1,0:T(8,128)(2,1)S(1)}, u32[]{:S(2)}, u32[]{:S(2)}) %collective-permute-start.5) | collective-permute-done | bytes 786464 | tf_op jit(solution)/shard_map/ppermute | solution.py:448
  153.6 1.0 assemble.1
  154.7 27.6 %all_to_all.11 = bf16[32,24,512]{2,1,0:T(8,128)(2,1)S(1)} all-to-all(bf16[32,24,512]{2,1,0:T(8,128)(2,1)S(1)} %bitcast.14), channel_id=1, replica_groups=mesh['rep'=16,'exp'=32] {'exp'}, dimensions={0} | all-to-all | bytes 1572864 | tf_op jit(solution)/shard_map/all_to_all | solution.py:449
  182.2 1.3 combine.1
  183.6 0.0 reduce-scatter.2.cloned.1.call-done
  183.6 1.0 convert_multiply_fusion
  184.6 0.8 fusion
  (4 shorter events, 0.1 us)
Async XLA Ops:
  7.2 21.0 %copy-start = (bf16[16,16,512]{2,1,0:T(8,128)(2,1)S(1)}, bf16[16,16,512]{2,1,0:T(8,128)(2,1)}, u32[]{:S(2)}) copy-start(bf16[16,16,512]{2,1,0:T(8,128)(2,1)} %param.10) | copy-start | bytes 786436
  7.2 20.9 %copy-start.4 = (bf16[512,512]{1,0:T(8,128)(2,1)S(1)}, bf16[512,512]{1,0:T(8,128)(2,1)}, u32[]{:S(2)}) copy-start(bf16[512,512]{1,0:T(8,128)(2,1)} %wproj_ref.1) | copy-start | bytes 1572868
  7.2 20.9 %copy-start.3 = (bf16[512,1536]{1,0:T(8,128)(2,1)S(1)}, bf16[512,1536]{1,0:T(8,128)(2,1)}, u32[]{:S(2)}) copy-start(bf16[512,1536]{1,0:T(8,128)(2,1)} %wqkv_ref.1) | copy-start | bytes 4718596
  7.2 20.9 %copy-start.6 = (s32[1,1,256,1]{2,3,1,0:T(1,128)S(1)}, s32[1,1,256,1]{2,3,1,0:T(1,128)}, u32[]{:S(2)}) copy-start(s32[1,1,256,1]{2,3,1,0:T(1,128)} %param.12) | copy-start | bytes 3076
  7.2 86.2 %all-gather.3.cloned.1.call-start = ((), (), s32[]{:S(2)}) async-start(), calls=%async_computation.4 | async-start | bytes 2359296 | tf_op jit(solution)/shard_map/all_gather | solution.py:395
  9.1 174.4 %reduce-scatter.2.cloned.1.call-start = ((), (), s32[]{:S(2)}) async-start(), calls=%async_computation.3 | async-start | bytes 2359296 | tf_op jit(solution)/shard_map/reduce_scatter | solution.py:444
  10.1 7.3 %collective-permute-start.1 = (bf16[4,16,512]{2,1,0:T(8,128)(2,1)S(1)}, bf16[4,16,512]{2,1,0:T(8,128)(2,1)S(1)}, u32[]{:S(2)}, u32[]{:S(2)}) collective-permute-start(bf16[4,16,512]{2,1,0:T(8,128)(2,1)S(1)} %get-tuple-element.36), channel_id=1, source_target_pairs={{32,0},{64,32},{96,64},{128,96},{160,128},{192,160},{224,192},{256... | collective-permute-start | bytes 196616 | tf_op jit(solution)/shard_map/ppermute | solution.py:404
  12.0 5.4 %collective-permute-start = (bf16[4,16,512]{2,1,0:T(8,128)(2,1)S(1)}, bf16[4,16,512]{2,1,0:T(8,128)(2,1)S(1)}, u32[]{:S(2)}, u32[]{:S(2)}) collective-permute-start(bf16[4,16,512]{2,1,0:T(8,128)(2,1)S(1)} %get-tuple-element.37), channel_id=1, source_target_pairs={{0,32},{32,64},{64,96},{96,128},{128,160},{160,192},{192,224},{224... | collective-permute-start | bytes 196616 | tf_op jit(solution)/shard_map/ppermute | solution.py:403
  17.7 8.3 %collective-permute-start.2 = (bf16[96,512]{1,0:T(8,128)(2,1)S(1)}, bf16[96,512]{1,0:T(8,128)(2,1)S(1)}, u32[]{:S(2)}, u32[]{:S(2)}) collective-permute-start(bf16[96,512]{1,0:T(8,128)(2,1)S(1)} %reshape.60), channel_id=1, source_target_pairs={{0,1},{1,2},{2,3},{3,4},{4,5},{5,6},{6,7},{7,8},{8,9},{9,10},{10,1... | collective-permute-start | bytes 294920 | tf_op jit(solution)/shard_map/ppermute | solution.py:411
  22.2 5.9 %collective-permute-start.3 = (bf16[96,512]{1,0:T(8,128)(2,1)S(1)}, bf16[96,512]{1,0:T(8,128)(2,1)S(1)}, u32[]{:S(2)}, u32[]{:S(2)}) collective-permute-start(bf16[96,512]{1,0:T(8,128)(2,1)S(1)} %reshape.61), channel_id=1, source_target_pairs={{1,0},{2,1},{3,2},{4,3},{5,4},{6,5},{7,6},{8,7},{9,8},{10,9},{11,1... | collective-permute-start | bytes 294920 | tf_op jit(solution)/shard_map/ppermute | solution.py:412
  28.1 1.0 copy-start.5
  29.1 1.1 copy-start.7
  30.2 1.0 copy-start.8
  58.7 33.9 %collective-permute-start.4 = (bf16[768,512]{1,0:T(8,128)(2,1)S(1)}, bf16[768,512]{1,0:T(8,128)(2,1)S(1)}, u32[]{:S(2)}, u32[]{:S(2)}) collective-permute-start(bf16[768,512]{1,0:T(8,128)(2,1)S(1)} %bitcast.16), channel_id=1, source_target_pairs={{0,32},{32,0},{64,96},{96,64},{128,160},{160,128},{192,224},{224,1... | collective-permute-start | bytes 2359304 | tf_op jit(solution)/shard_map/ppermute | solution.py:441
  93.4 1.6 copy-start.1
  101.4 1.6 copy-start.2
  103.0 1.4 copy-start.9
  104.4 1.4 copy-start.10
  108.8 44.8 %collective-permute-start.5 = (bf16[768,512]{1,0:T(8,128)(2,1)S(1)}, bf16[768,512]{1,0:T(8,128)(2,1)S(1)}, u32[]{:S(2)}, u32[]{:S(2)}) collective-permute-start(bf16[768,512]{1,0:T(8,128)(2,1)S(1)} %get-tuple-element.26), channel_id=1, source_target_pairs={{0,32},{32,0},{64,96},{96,64},{128,160},{160,128},{192,224},{224,1... | collective-permute-start | bytes 2359304 | tf_op jit(solution)/shard_map/ppermute | solution.py:448
Sparse Core Ops, SparseCore 0:
  10.7 70.8 all-gather.2
  101.6 69.5 reduce-scatter.1

commit v4 on v2

v4 whole, which is shorter than its diff:
```python
import functools
import math

import jax
import jax.numpy as jnp
from jax import lax
from jax.experimental import pallas as pl
from jax.experimental.pallas import tpu as pltpu
from jax.sharding import PartitionSpec as P

HEADS = 16


GELU_C = math.sqrt(2.0 / math.pi)
window_side = 8
margin_cells = 4
CHUNKS = 4
EXTRA = 16

VMEM_LIMIT = 24 * 1024 * 1024
MIDDLE_LIMIT = 58 * 1024 * 1024


def nt(a, b):
    return lax.dot_general(a, b, (((1,), (1,)), ((), ())), preferred_element_type=jnp.float32)


def tn(a, b):
    return lax.dot_general(a, b, (((0,), (0,)), ((), ())), preferred_element_type=jnp.float32)


def nn(a, b):
    return jnp.dot(a, b, preferred_element_type=jnp.float32)


def one_hot(mask):
    return mask.astype(jnp.float32).astype(jnp.bfloat16)


def vmem_call(kernel, out, name, flops, in_specs=None, count=0, **more):
    vmem = pl.BlockSpec(memory_space=pltpu.VMEM)
    return pl.pallas_call(
        kernel,
        in_specs=in_specs or [vmem] * count,
        out_specs=[vmem] * len(out),
        out_shape=[jax.ShapeDtypeStruct(shape, dtype) for shape, dtype in out],
        compiler_params=pltpu.CompilerParams(vmem_limit_bytes=VMEM_LIMIT),
        cost_estimate=pl.CostEstimate(flops=flops, bytes_accessed=3_000_000, transcendentals=0),
        name=name,
        **more,
    )


def upstream_kernel(route_ref, gate_ref, cot_ref, give_ref):
    f32, bf16 = jnp.float32, jnp.bfloat16
    count, feature = cot_ref.shape
    give_ref[:count] = (gate_ref[...] * cot_ref[...].astype(f32)).astype(bf16)
    route = route_ref[...].astype(f32)
    row = jnp.concatenate([route, jnp.zeros((1, feature - count), f32)], axis=1)
    extra = give_ref.shape[0] - count
    give_ref[count:] = jnp.broadcast_to(row, (extra, feature)).astype(bf16)


def slot_numbers(route, experts):
    count = route.shape[1]
    matches = lax.broadcasted_iota(jnp.int32, (experts, count), 0) == route
    earlier = lax.broadcasted_iota(jnp.int32, (count, count), 0) < lax.broadcasted_iota(
        jnp.int32, (count, count), 1
    )
    before = nn(one_hot(matches), one_hot(earlier))
    return jnp.sum(jnp.where(matches, before, 0.0), axis=0, keepdims=True).astype(jnp.int32)


def placer(target, rows):
    return one_hot(lax.broadcasted_iota(jnp.int32, (rows, target.shape[1]), 0) == target)


def grad_slots_kernel(experts, capacity, give_ref, got_ref, slots_ref, target_ref):
    feature = give_ref.shape[1]
    count = give_ref.shape[0] - EXTRA
    total = None
    for n, ref in enumerate((give_ref, got_ref)):
        route = ref[count:, :count].astype(jnp.float32)[:1].astype(jnp.int32)
        target = route * (2 * capacity) + n * capacity + slot_numbers(route, experts)
        target_ref[n : n + 1] = target
        placed = nn(placer(target, 2 * experts * capacity), ref[:count])
        total = placed if total is None else total + placed
    slots_ref[...] = total.astype(jnp.bfloat16)


def token_slots_kernel(target_ref, mixed_ref, got_ref, slots_ref):
    rows = slots_ref.shape[0]
    total = nn(placer(target_ref[0:1], rows), mixed_ref[...])
    total = total + nn(placer(target_ref[1:2], rows), got_ref[...])
    slots_ref[...] = total.astype(jnp.bfloat16)


def back_rows_kernel(target_ref, back_ref, give_ref):
    give_ref[...] = tn(placer(target_ref[1:2], back_ref.shape[0]), back_ref[...]).astype(
        jnp.bfloat16
    )


def combine_kernel(
    target_ref, out_ref, got_out_ref, in_ref, got_in_ref, mixed_ref, gate_ref, layer_ref, grad_ref
):
    f32, bf16 = jnp.float32, jnp.bfloat16
    mine = placer(target_ref[0:1], out_ref.shape[0])
    token_out = tn(mine, out_ref[...]) + got_out_ref[...].astype(f32)
    layer_ref[...] = (mixed_ref[...].astype(f32) + gate_ref[...] * token_out).astype(bf16)
    grad_ref[...] = (tn(mine, in_ref[...]) + got_in_ref[...].astype(f32)).astype(bf16)


def gradients_kernel(scale, sum_ref, up_ref, down_ref):
    width = up_ref.shape[1]
    up_ref[0] = sum_ref[0, :width].astype(jnp.float32) * scale
    down_ref[0] = sum_ref[0, width:].astype(jnp.float32) * scale


def middle_kernel(w_hbm, x_ref, g_ref, grads_ref, hid_ref, pg_ref, w_ref, sems):
    step = pl.program_id(0)
    shards = w_ref.shape[1]
    copies = [
        pltpu.make_async_copy(w_hbm.at[pl.ds(n * shards, shards)], w_ref.at[n], sems.at[n])
        for n in range(CHUNKS)
    ]

    @pl.when(step == 0)
    def _():
        for copy in copies:
            copy.start()

    for n in range(CHUNKS):

        @pl.when(step == n)
        def _():
            copies[n].wait()

    held = w_ref[step]
    _, _, width, feature = held.shape
    up = held[:, 0].reshape(shards * width, feature)
    down = held[:, 1].reshape(shards * width, feature)
    halves = 2
    rows = x_ref.shape[0] // halves
    parts = [slice(n * rows, (n + 1) * rows) for n in range(halves)]
    pres = [nt(up, x_ref[part]) for part in parts]
    backs = [nt(down, g_ref[part]) for part in parts]
    grad_up = grad_down = None
    for n, part in enumerate(parts):
        pre = pres[n]
        square = pre * pre
        inner = jnp.tanh(pre * (GELU_C + (GELU_C * 0.044715) * square))
        half = 0.5 + 0.5 * inner
        hidden = (pre * half).astype(jnp.bfloat16)
        slope = half + (0.5 * pre) * (1.0 - inner * inner) * (
            GELU_C + (3.0 * 0.044715 * GELU_C) * square
        )
        pre_grad = (backs[n] * slope).astype(jnp.bfloat16)
        hid_ref[:, part] = hidden
        pg_ref[:, part] = pre_grad
        by_up = nn(pre_grad, x_ref[part])
        by_down = nn(hidden, g_ref[part])
        grad_up = by_up if grad_up is None else grad_up + by_up
        grad_down = by_down if grad_down is None else grad_down + by_down
    grads_ref[:, :width] = grad_up.astype(jnp.bfloat16).reshape(shards, width, feature)
    grads_ref[:, width:] = grad_down.astype(jnp.bfloat16).reshape(shards, width, feature)


def middle(weights, slot_x, slot_g):
    owners, _, width, feature = weights.shape
    rows = slot_x.shape[0]
    step = owners // CHUNKS
    ff = owners * width
    return pl.pallas_call(
        middle_kernel,
        grid=(CHUNKS,),
        in_specs=[
            pl.BlockSpec(memory_space=pltpu.HBM),
            pl.BlockSpec((rows, feature), lambda i: (0, 0)),
            pl.BlockSpec((rows, feature), lambda i: (0, 0)),
        ],
        out_specs=[
            pl.BlockSpec((step, 2 * width, feature), lambda i: (i, 0, 0)),
            pl.BlockSpec((step * width, rows), lambda i: (i, 0)),
            pl.BlockSpec((step * width, rows), lambda i: (i, 0)),
        ],
        out_shape=[
            pltpu.HBM((owners, 2 * width, feature), jnp.bfloat16),
            pltpu.HBM((ff, rows), jnp.bfloat16),
            pltpu.HBM((ff, rows), jnp.bfloat16),
        ],
        scratch_shapes=[
            pltpu.VMEM((CHUNKS, step, 2, width, feature), jnp.bfloat16),
            pltpu.SemaphoreType.DMA((CHUNKS,)),
        ],
        compiler_params=pltpu.CompilerParams(vmem_limit_bytes=MIDDLE_LIMIT),
        cost_estimate=pl.CostEstimate(
            flops=8 * rows * ff * feature,
            bytes_accessed=8 * ff * feature + 4 * ff * rows,
            transcendentals=ff * rows,
        ),
        name="middle",
    )(weights, slot_x, slot_g)


def back_kernel(side, w_ref, act_ref, out_ref, acc):
    shards, _, width, feature = w_ref.shape
    matrix = w_ref[:, 0].reshape(shards * width, feature)

    @pl.when(pl.program_id(0) == 0)
    def _():
        acc[...] = jnp.zeros_like(acc)

    acc[...] += tn(act_ref[...], matrix)

    @pl.when(pl.program_id(0) == pl.num_programs(0) - 1)
    def _():
        out_ref[...] = acc[...].astype(jnp.bfloat16)


def back(weights, activity, side):
    owners, _, width, feature = weights.shape
    ff, rows = activity.shape
    steps = 2
    step = owners // steps
    return pl.pallas_call(
        functools.partial(back_kernel, side),
        grid=(steps,),
        in_specs=[
            pl.BlockSpec((step, 1, width, feature), lambda i: (i, side, 0, 0)),
            pl.BlockSpec((step * width, rows), lambda i: (i, 0)),
        ],
        out_specs=pl.BlockSpec((rows, feature), lambda i: (0, 0)),
        out_shape=jax.ShapeDtypeStruct((rows, feature), jnp.bfloat16),
        scratch_shapes=[pltpu.VMEM((rows, feature), jnp.float32)],
        compiler_params=pltpu.CompilerParams(vmem_limit_bytes=VMEM_LIMIT),
        cost_estimate=pl.CostEstimate(
            flops=2 * rows * ff * feature,
            bytes_accessed=2 * ff * feature + 2 * ff * rows,
            transcendentals=0,
        ),
        name="back",
    )(weights, activity)


def window_index(row, col, tile):
    wins = (tile + 2 * margin_cells) // window_side
    window = (row // window_side) * wins + col // window_side
    return (window * window_side + row % window_side) * window_side + col % window_side


def into_windows(tile):
    ext = tile + 2 * margin_cells
    edge, strip = margin_cells * tile, margin_cells * ext
    piece = lax.broadcasted_iota(jnp.int32, (1, ext * ext), 1)
    base = tile * tile
    row, col = margin_cells + piece // tile, margin_cells + piece % tile
    low = piece - base
    row = jnp.where(piece >= base, low // tile, row)
    high = piece - (base + edge)
    row = jnp.where(piece >= base + edge, tile + margin_cells + high // tile, row)
    left = piece - (base + 2 * edge)
    side = piece >= base + 2 * edge
    row = jnp.where(side, left // margin_cells, row)
    col = jnp.where(side, left % margin_cells, col)
    right = left - strip
    side = piece >= base + 2 * edge + strip
    row = jnp.where(side, right // margin_cells, row)
    col = jnp.where(side, tile + margin_cells + right % margin_cells, col)
    place = window_index(row, col, tile)
    return one_hot(lax.broadcasted_iota(jnp.int32, (ext * ext, ext * ext), 0) == place)


def out_of_windows(tile):
    ext = tile + 2 * margin_cells
    token = lax.broadcasted_iota(jnp.int32, (tile * tile, 1), 0)
    place = window_index(token // tile + margin_cells, token % tile + margin_cells, tile)
    return one_hot(lax.broadcasted_iota(jnp.int32, (tile * tile, ext * ext), 1) == place)


def front_kernel(
    at_ref, tok_ref, low_ref, high_ref, left_ref, right_ref, wqkv_ref, wproj_ref, mixed_ref, qkv_ref, ctx_ref
):
    bf16, f32 = jnp.bfloat16, jnp.float32
    tokens = tok_ref[...]
    count, feature = tokens.shape
    cells = window_side * window_side
    head = feature // HEADS
    group = 128 // head
    pieces = jnp.concatenate(
        [tokens, low_ref[...], high_ref[...], left_ref[...], right_ref[...]], axis=0
    )
    placed = nn(into_windows(math.isqrt(count)), pieces).astype(bf16)
    qkv_ref[...] = jnp.dot(placed, wqkv_ref[...], preferred_element_type=f32).astype(bf16)
    first_row, last_row = at_ref[0] == 0, at_ref[0] == at_ref[1] - 1
    first_col, last_col = at_ref[2] == 0, at_ref[2] == at_ref[3] - 1
    lane = lax.broadcasted_iota(jnp.int32, (1, 128), 1)
    own = [
        ((lane >= h * head) & (lane < (h + 1) * head)).astype(f32) for h in range(group)
    ]
    own16 = [o.astype(bf16) for o in own]
    key = lax.broadcasted_iota(jnp.int32, (cells, 128), 0)
    key_row, key_col = key // window_side, key % window_side
    half = window_side // 2
    low_bias = jnp.float32(-1e30)
    edge_bias = {
        (0, 0): jnp.where(key_row < half, jnp.where(first_row, low_bias, 0.0), 0.0),
        (0, 2): jnp.where(key_row >= half, jnp.where(last_row, low_bias, 0.0), 0.0),
        (1, 0): jnp.where(key_col < half, jnp.where(first_col, low_bias, 0.0), 0.0),
        (1, 2): jnp.where(key_col >= half, jnp.where(last_col, low_bias, 0.0), 0.0),
    }
    scale = 1.0 / math.sqrt(head)
    for window in range(9):
        wi, wj = window // 3, window % 3
        bias = None
        if wi != 1:
            bias = edge_bias[0, wi]
        if wj != 1:
            bias = edge_bias[1, wj] if bias is None else bias + edge_bias[1, wj]
        if bias is not None:
            bias = jnp.concatenate([bias] * (group * cells // 128), axis=1)
        rows = slice(window * cells, (window + 1) * cells)
        for g in range(feature // 128):
            q = qkv_ref[rows, g * 128 : (g + 1) * 128]
            k = qkv_ref[rows, feature + g * 128 : feature + (g + 1) * 128]
            v = qkv_ref[rows, 2 * feature + g * 128 : 2 * feature + (g + 1) * 128]
            spread = jnp.concatenate([q * o for o in own16], axis=0)
            scores = nt(k, spread)
            if bias is not None:
                scores = scores + bias
            peak = jnp.max(scores, axis=0, keepdims=True)
            weights = jnp.exp((scores - peak) * scale)
            probs = (weights * (1.0 / jnp.sum(weights, axis=0, keepdims=True))).astype(bf16)
            wide = tn(probs, v)
            mine = wide[:cells] * own[0]
            for h in range(1, group):
                mine = mine + wide[h * cells : (h + 1) * cells] * own[h]
            ctx_ref[rows, g * 128 : (g + 1) * 128] = mine.astype(bf16)
    context = nn(out_of_windows(math.isqrt(count)), ctx_ref[...]).astype(bf16)
    attended = jnp.dot(context, wproj_ref[...], preferred_element_type=f32)
    centred = attended - jnp.mean(attended, axis=-1, keepdims=True)
    spread_of = jnp.mean(centred * centred, axis=-1, keepdims=True)
    mixed = (tokens.astype(f32) + centred * lax.rsqrt(spread_of + 1e-05)).astype(bf16)
    mixed_ref[...] = mixed


def front(at, tokens, low, high, left, right, w_qkv, w_proj):
    count, feature = tokens.shape
    ext = (math.isqrt(count) + 2 * margin_cells) ** 2
    smem = pl.BlockSpec(memory_space=pltpu.SMEM)
    vmem = pl.BlockSpec(memory_space=pltpu.VMEM)
    return vmem_call(
        front_kernel,
        [((count, feature), jnp.bfloat16)],
        "front",
        4_000_000_000,
        in_specs=[smem] + [vmem] * 7,
        scratch_shapes=[
            pltpu.VMEM((ext, 3 * feature), jnp.bfloat16),
            pltpu.VMEM((ext, feature), jnp.bfloat16),
        ],
    )(at, tokens, low, high, left, right, w_qkv, w_proj)[0]


def shifts(axis):
    count = lax.axis_size(axis)
    forward = [(i, i + 1) for i in range(count - 1)]
    return forward, [(target, source) for source, target in forward]


def sharing(axis):
    count = lax.axis_size(axis)
    groups = [list(range(parity, count, 2)) for parity in range(2)]
    return groups, [(i, i ^ 1) for i in range(count)]


def per_device(tokens, gate, route, cotangent, w_qkv, w_proj, w_up, w_down):
    tile_rows, tile_cols, feature = tokens.shape
    tok_count = tile_rows * tile_cols
    margin = margin_cells
    experts = lax.axis_size("exp")
    capacity = max(2, 3 * tok_count // (2 * experts))
    slot_count = 2 * experts * capacity
    bf16, f32 = jnp.bfloat16, jnp.float32
    rows_of = ((slot_count, feature), bf16)
    groups, swap = sharing("rep")

    def dispatch(rows):
        blocks = rows.reshape(experts, -1, feature)
        return lax.all_to_all(blocks, "exp", 0, 0, tiled=True).reshape(-1, feature)

    weights = lax.all_gather(
        jnp.concatenate([w_up, w_down], axis=0),
        "rep",
        axis=0,
        tiled=False,
        axis_index_groups=groups,
    )
    forward, backward = shifts("rep")
    low = lax.ppermute(tokens[tile_rows - margin :], "rep", forward)
    high = lax.ppermute(tokens[:margin], "rep", backward)
    gate_rows = gate.reshape(tok_count, 1)
    [give] = vmem_call(
        upstream_kernel, [((tok_count + EXTRA, feature), bf16)], "upstream", 1_000_000, count=3
    )(route.reshape(1, tok_count), gate_rows, cotangent.reshape(tok_count, feature))
    got = lax.ppermute(give, "rep", swap)
    forward, backward = shifts("exp")

    def strip(cols):
        parts = [low[:, cols], tokens[:, cols], high[:, cols]]
        return jnp.concatenate(parts, axis=0).reshape(-1, feature)

    left = lax.ppermute(strip(slice(tile_cols - margin, tile_cols)), "exp", forward)
    right = lax.ppermute(strip(slice(0, margin)), "exp", backward)
    at = jnp.stack(
        [
            lax.axis_index("rep"),
            jnp.int32(lax.axis_size("rep")),
            lax.axis_index("exp"),
            jnp.int32(experts),
        ]
    ).astype(jnp.int32)
    mixed = front(
        at,
        tokens.reshape(tok_count, feature),
        low.reshape(-1, feature),
        high.reshape(-1, feature),
        left,
        right,
        w_qkv,
        w_proj,
    )
    got_mixed = lax.ppermute(mixed, "rep", swap)
    slots_g, target = vmem_call(
        functools.partial(grad_slots_kernel, experts, capacity),
        [rows_of, ((2, tok_count), jnp.int32)],
        "grad_slots",
        500_000_000,
        count=2,
    )(give, got)
    slot_g = dispatch(slots_g)
    [slots_x] = vmem_call(token_slots_kernel, [rows_of], "token_slots", 400_000_000, count=3)(
        target, mixed, got_mixed
    )
    slot_x = dispatch(slots_x)
    grads, hidden, pre_grad = middle(weights, slot_x, slot_g)
    summed = lax.psum_scatter(
        grads, "rep", scatter_dimension=0, tiled=True, axis_index_groups=groups
    )

    def returned(activity, side):
        rows = dispatch(back(weights, activity, side))
        [theirs] = vmem_call(
            back_rows_kernel, [((tok_count, feature), bf16)], "back_rows", 200_000_000, count=2
        )(target, rows)
        return rows, lax.ppermute(theirs, "rep", swap)

    layer_out, input_grad = vmem_call(
        combine_kernel, [((tok_count, feature), bf16)] * 2, "combine", 400_000_000, count=7
    )(target, *returned(hidden, 1), *returned(pre_grad, 0), mixed, gate_rows)
    grad_up, grad_down = vmem_call(
        functools.partial(gradients_kernel, 1.0 / lax.axis_size("rep")),
        [(w_up.shape, f32)] * 2,
        "gradients",
        1_000_000,
        count=1,
    )(summed)
    return (
        layer_out.reshape(tile_rows, tile_cols, feature),
        input_grad.reshape(tile_rows, tile_cols, feature),
        grad_up,
        grad_down,
    )


def solution(mesh):
    placed = (
        P("rep", "exp", None),
        P("rep", "exp"),
        P("rep", "exp", None, None),
        P("rep", "exp", None),
        P(),
        P(),
        P("exp", "rep", None),
        P("exp", "rep", None),
    )
    return jax.shard_map(
        per_device,
        mesh=mesh,
        in_specs=placed,
        out_specs=(
            P("rep", "exp", None),
            P("rep", "exp", None),
            P("exp", "rep", None),
            P("exp", "rep", None),
        ),
        check_vma=False,
    )
```

time: 191 us -> 184 us (0.963)
  starting transfers between devices: 11.5 us -> 45.7 us
  waiting for transfers between devices: 88.2 us -> 65.7 us
  blocking collectives: 41.4 us -> 19.4 us
  local copies, waits for them, and re-layouts: 10.8 us -> 12.9 us
    reduce_scatter x1, waiting for transfers between devices: 49.3 us -> 0.01 us  [per_device(): lax.psum_scatter(grads, 'rep', scatter_dimension=0, tiled=True, axis_inde...]
    ppermute x0 -> x4, waiting for transfers between devices: none -> 45.8 us  [the longest x2 26.6 us: returned(): return (rows, lax.ppermute(theirs, 'rep', swap))]
    all_gather x1, waiting for transfers between devices: 36.8 us -> 0.01 us  [per_device(): lax.all_gather(jnp.concatenate([w_up, w_down], axis=0), 'rep', axis=0, ti...]
    all_to_all x2 -> x1, blocking collectives: 41.4 us -> 19.4 us  [dispatch(): return lax.all_to_all(blocks, 'exp', 0, 0, tiled=True).reshape(-1, feature)]
    all_to_all x0 -> x3, starting transfers between devices: none -> 20.8 us  [dispatch(): return lax.all_to_all(blocks, 'exp', 0, 0, tiled=True).reshape(-1, feature)]
    all_to_all x0 -> x3, waiting for transfers between devices: none -> 19.8 us  [dispatch(): return lax.all_to_all(blocks, 'exp', 0, 0, tiled=True).reshape(-1, feature)]
    ppermute x0 -> x4, starting transfers between devices: none -> 13.3 us  [the longest x2 6.65 us: returned(): return (rows, lax.ppermute(theirs, 'rep', swap))]
    unnamed x26, local copies, waits for them, and re-layouts: 4.82 us -> 10.4 us
  transfers between devices with their start and end apart: 6 -> 13, of which waited for: 4 -> 5; matrix products, arithmetic and copies ran while one was open for 3% -> 1% of each run, Pallas kernels for 6% -> 7%
where the time goes in v4:
time: 184 us; the launch traced here: 182 us
  waiting for transfers between devices  65.7 us (36%)
  starting transfers between devices  45.7 us (25%)
  Pallas kernels  21.6 us (12%)
  blocking collectives  19.4 us (11%)
  between operations  14.4 us (8%)
  local copies, waits for them, and re-layouts  12.9 us (7%)
  other arithmetic  1.96 us (1%)
    ppermute x2, waiting for transfers between devices, returned(): return (rows, lax.ppermute(theirs, 'rep', swap))  26.6 us
    all_to_all x3, starting transfers between devices, dispatch(): return lax.all_to_all(blocks, 'exp', 0, 0, tiled=True).reshape(-1, feature)  20.8 us
    all_to_all x3, waiting for transfers between devices, dispatch(): return lax.all_to_all(blocks, 'exp', 0, 0, tiled=True).reshape(-1, feature)  19.8 us
    all_to_all x1, blocking collectives, dispatch(): return lax.all_to_all(blocks, 'exp', 0, 0, tiled=True).reshape(-1, feature)  19.4 us
    ppermute x1, waiting for transfers between devices, per_device(): got_mixed = lax.ppermute(mixed, 'rep', swap)  19.2 us
    unnamed x26, local copies, waits for them, and re-layouts  10.4 us
    pallas_call x1, Pallas kernels, middle(): pl.pallas_call(middle_kernel, grid=(CHUNKS,), in_specs=[pl.BlockSpec(memo...  8.92 us
    ppermute x2, starting transfers between devices, returned(): return (rows, lax.ppermute(theirs, 'rep', swap))  6.65 us
  transfers between devices with their start and end apart: 13, of which 5 were waited for; matrix products, arithmetic and copies ran while one was open for 1% of the time, Pallas kernels for 7%

profile of v4, /device:TPU:6, one launch (start us, length us, event | category | flops | bytes accessed | tf_op | source)
XLA Modules:
  0.0 181.6 jit_solution(5099448061676426482)
XLA Ops:
  7.2 0.0 copy-start.6
  7.2 0.0 all-gather.3.cloned.1.call-start
  7.2 1.7 pad_maximum_fusion
  9.0 0.0 all-gather.3.cloned.1.call-update
  9.0 0.9 fusion.1
  9.9 1.3 collective-permute-start.2
  11.2 4.5 %collective-permute-start.1 = (bf16[4,16,512]{2,1,0:T(8,128)(2,1)S(1)}, bf16[4,16,512]{2,1,0:T(8,128)(2,1)S(1)}, u32[]{:S(2)}, u32[]{:S(2)}) collective-permute-start(bf16[4,16,512]{2,1,0:T(8,128)(2,1)S(1)} %get-tuple-element.25), channel_id=1, source_target_pairs={{0,32},{32,64},{64,96},{96,128},{128,160},{160,192},{192,224},{224... | collective-permute-start | bytes 196616 | tf_op jit(solution)/shard_map/ppermute | solution.py:400
  15.7 0.8 reshape.81.gate_ref
  16.5 0.0 copy-start.5
  16.5 0.9 copy-done.5
  17.5 0.7 copy-done.8
  18.2 0.1 upstream.1.give_ref
  18.3 3.8 %collective-permute-start = (bf16[272,512]{1,0:T(8,128)(2,1)S(1)}, bf16[272,512]{1,0:T(8,128)(2,1)S(1)}, u32[]{:S(2)}, u32[]{:S(2)}) collective-permute-start(bf16[272,512]{1,0:T(8,128)(2,1)S(1)} %upstream.1.give_ref), channel_id=1, source_target_pairs={{0,32},{32,0},{64,96},{96,64},{128,160},{160,128},{192,224},{224,1... | collective-permute-start | bytes 835592 | tf_op jit(solution)/shard_map/ppermute | solution.py:406
  22.1 0.0 copy-done.6
  22.1 0.1 fusion
  22.2 0.0 collective-permute-done.2
  22.2 0.0 collective-permute-done.1
  22.3 0.1 pad_maximum_fusion.2
  22.4 0.1 pad_maximum_fusion.1
  22.5 0.7 reshape.68
  23.1 2.0 %collective-permute-start.3 = (bf16[96,512]{1,0:T(8,128)(2,1)}, bf16[96,512]{1,0:T(8,128)(2,1)S(1)}, u32[]{:S(2)}, u32[]{:S(2)}) collective-permute-start(bf16[96,512]{1,0:T(8,128)(2,1)} %reshape.68), channel_id=1, source_target_pairs={{0,1},{1,2},{2,3},{3,4},{4,5},{5,6},{6,7},{7,8},{8,9},{9,10},{10,1... | collective-permute-start | bytes 294920 | tf_op jit(solution)/shard_map/ppermute | solution.py:413
  25.2 3.6 %collective-permute-start.4 = (bf16[96,512]{1,0:T(8,128)(2,1)S(1)}, bf16[96,512]{1,0:T(8,128)(2,1)S(1)}, u32[]{:S(2)}, u32[]{:S(2)}) collective-permute-start(bf16[96,512]{1,0:T(8,128)(2,1)S(1)} %reshape.69), channel_id=1, source_target_pairs={{1,0},{2,1},{3,2},{4,3},{5,4},{6,5},{7,6},{8,7},{9,8},{10,9},{11,1... | collective-permute-start | bytes 294920 | tf_op jit(solution)/shard_map/ppermute | solution.py:414
  28.8 0.0 collective-permute-done.got_ref
  28.8 0.0 copy-start.11
  28.8 0.7 copy-done.11
  29.5 1.0 copy-done.12
  30.5 1.6 grad_slots.1
  32.1 8.0 %all-to-all-start.1 = ((bf16[32,24,512]{2,1,0:T(8,128)(2,1)}), bf16[32,24,512]{2,1,0:T(8,128)(2,1)}, u32[]{:S(2)}, u32[]{:S(2)}) async-start(bf16[32,24,512]{2,1,0:T(8,128)(2,1)} %bitcast.10), calls=%async_computation.1 | async-start | bytes 1572864 | tf_op jit(solution)/shard_map/all_to_all | solution.py:390
  40.1 0.0 reduce-scatter.2.cloned.1.call-start
  40.1 0.1 pad_add_fusion.at_ref
  40.2 0.0 collective-permute-done.3.left_ref
  40.2 0.0 collective-permute-done.4.right_ref
  40.2 0.0 copy-done.9
  40.2 0.0 copy-done.10
  40.3 4.4 %front.1.mixed_ref = bf16[256,512]{1,0:T(8,128)(2,1)S(1)} custom-call(s32[4]{0:T(128)S(1)} %pad_add_fusion.at_ref, bf16[256,512]{1,0:T(8,128)(2,1)S(1)} %bitcast.29, bf16[64,512]{1,0:T(8,128)(2,1)S(1)} %bitcast.31, bf16[64,512]{1,0:T(8,128)(2,1)S(1)} %bitcast.30, bf16[96,512]{1,0:T(8,128)(2,1)S(1)} %collective-permute-done.3.left_ref, ...), custom_call_target="tpu_custom_call" | custom-call | flops 4000000000 | bytes 3000000 | tf_op jit(solution)/shard_map/front/pallas_call | solution.py:352
  44.7 2.8 %collective-permute-start.5 = (bf16[256,512]{1,0:T(8,128)(2,1)S(1)}, bf16[256,512]{1,0:T(8,128)(2,1)S(1)}, u32[]{:S(2)}, u32[]{:S(2)}) collective-permute-start(bf16[256,512]{1,0:T(8,128)(2,1)S(1)} %front.1.mixed_ref), channel_id=1, source_target_pairs={{0,32},{32,0},{64,96},{96,64},{128,160},{160,128},{192,224},{224,1... | collective-permute-start | bytes 786440 | tf_op jit(solution)/shard_map/ppermute | solution.py:433
  47.5 19.2 %collective-permute-done.5.got_ref = bf16[256,512]{1,0:T(8,128)(2,1)S(1)} collective-permute-done((bf16[256,512]{1,0:T(8,128)(2,1)S(1)}, bf16[256,512]{1,0:T(8,128)(2,1)S(1)}, u32[]{:S(2)}, u32[]{:S(2)}) %collective-permute-start.5) | collective-permute-done | bytes 262176 | tf_op jit(solution)/shard_map/ppermute | solution.py:433
  66.7 0.6 token_slots.1
  67.2 0.0 all-to-all-done.1
  67.3 19.4 %all_to_all.20 = bf16[32,24,512]{2,1,0:T(8,128)(2,1)} all-to-all(bf16[32,24,512]{2,1,0:T(8,128)(2,1)S(1)} %bitcast.27), channel_id=1, replica_groups=mesh['rep'=16,'exp'=32] {'exp'}, dimensions={0} | all-to-all | bytes 1572864 | tf_op jit(solution)/shard_map/all_to_all | solution.py:390
  86.6 8.9 %middle.1 = (bf16[8,256,512]{2,1,0:T(8,128)(2,1)}, bf16[1024,768]{1,0:T(8,128)(2,1)}, bf16[1024,768]{1,0:T(8,128)(2,1)}) custom-call(bf16[8,2,128,512]{3,2,1,0:T(8,128)(2,1)} %bitcast.18, bf16[768,512]{1,0:T(8,128)(2,1)} %bitcast.33, bf16[768,512]{1,0:T(8,128)(2,1)} %bitcast.11.g_ref), custom_call_target="tpu_custom_call" | custom-call | flops 3221225472 | bytes 7340032 | tf_op jit(solution)/shard_map/middle/pallas_call | solution.py:174
  95.6 0.0 copy-start
  95.6 0.0 reduce-scatter.2.cloned.1.call-update
  95.6 1.6 copy-done
  97.2 1.4 copy-done.4
  98.6 1.5 back.3
  100.1 0.9 copy-done.2
  101.0 6.4 %all-to-all-start.3 = ((bf16[32,24,512]{2,1,0:T(8,128)(2,1)}), bf16[32,24,512]{2,1,0:T(8,128)(2,1)S(1)}, u32[]{:S(2)}, u32[]{:S(2)}) async-start(bf16[32,24,512]{2,1,0:T(8,128)(2,1)} %bitcast.26), calls=%async_computation.3 | async-start | bytes 1572864 | tf_op jit(solution)/shard_map/all_to_all | solution.py:390
  107.5 1.4 copy-done.3
  108.9 1.5 back.2
  110.4 0.0 copy-start.1
  110.4 0.9 copy-done.1
  111.3 8.2 %all-to-all-done.3 = bf16[32,24,512]{2,1,0:T(8,128)(2,1)S(1)} async-done(((bf16[32,24,512]{2,1,0:T(8,128)(2,1)}), bf16[32,24,512]{2,1,0:T(8,128)(2,1)S(1)}, u32[]{:S(2)}, u32[]{:S(2)}) %all-to-all-start.3) | async-done | bytes 786464 | tf_op jit(solution)/shard_map/all_to_all | solution.py:390
  119.5 6.4 %all-to-all-start.2 = ((bf16[32,24,512]{2,1,0:T(8,128)(2,1)}), bf16[32,24,512]{2,1,0:T(8,128)(2,1)S(1)}, u32[]{:S(2)}, u32[]{:S(2)}) async-start(bf16[32,24,512]{2,1,0:T(8,128)(2,1)} %bitcast.25), calls=%async_computation.2 | async-start | bytes 1572864 | tf_op jit(solution)/shard_map/all_to_all | solution.py:390
  125.9 0.4 back_rows.3
  126.3 11.7 %all-to-all-done.2 = bf16[32,24,512]{2,1,0:T(8,128)(2,1)S(1)} async-done(((bf16[32,24,512]{2,1,0:T(8,128)(2,1)}), bf16[32,24,512]{2,1,0:T(8,128)(2,1)S(1)}, u32[]{:S(2)}, u32[]{:S(2)}) %all-to-all-start.2) | async-done | bytes 786464 | tf_op jit(solution)/shard_map/all_to_all | solution.py:390
  138.0 0.4 back_rows.2
  138.4 4.7 %collective-permute-start.6 = (bf16[256,512]{1,0:T(8,128)(2,1)S(1)}, bf16[256,512]{1,0:T(8,128)(2,1)S(1)}, u32[]{:S(2)}, u32[]{:S(2)}) collective-permute-start(bf16[256,512]{1,0:T(8,128)(2,1)S(1)} %back_rows.2), channel_id=1, source_target_pairs={{0,32},{32,0},{64,96},{96,64},{128,160},{160,128},{192,224},{224,1... | collective-permute-start | bytes 786440 | tf_op jit(solution)/shard_map/ppermute | solution.py:456
  143.1 1.9 %collective-permute-start.7 = (bf16[256,512]{1,0:T(8,128)(2,1)S(1)}, bf16[256,512]{1,0:T(8,128)(2,1)S(1)}, u32[]{:S(2)}, u32[]{:S(2)}) collective-permute-start(bf16[256,512]{1,0:T(8,128)(2,1)S(1)} %back_rows.3), channel_id=1, source_target_pairs={{0,32},{32,0},{64,96},{96,64},{128,160},{160,128},{192,224},{224,1... | collective-permute-start | bytes 786440 | tf_op jit(solution)/shard_map/ppermute | solution.py:456
  145.0 16.7 %collective-permute-done.6.got_out_ref = bf16[256,512]{1,0:T(8,128)(2,1)S(1)} collective-permute-done((bf16[256,512]{1,0:T(8,128)(2,1)S(1)}, bf16[256,512]{1,0:T(8,128)(2,1)S(1)}, u32[]{:S(2)}, u32[]{:S(2)}) %collective-permute-start.6) | collective-permute-done | bytes 262176 | tf_op jit(solution)/shard_map/ppermute | solution.py:456
  161.7 9.9 %collective-permute-done.7.got_in_ref = bf16[256,512]{1,0:T(8,128)(2,1)S(1)} collective-permute-done((bf16[256,512]{1,0:T(8,128)(2,1)S(1)}, bf16[256,512]{1,0:T(8,128)(2,1)S(1)}, u32[]{:S(2)}, u32[]{:S(2)}) %collective-permute-start.7) | collective-permute-done | bytes 262176 | tf_op jit(solution)/shard_map/ppermute | solution.py:456
  171.6 1.3 combine.1
  173.0 0.9 copy-done.7
  173.9 0.8 gradients.1
  (13 shorter events, 0.1 us)
Async XLA Ops:
  7.2 14.9 %copy-start.6 = (bf16[16,16,512]{2,1,0:T(8,128)(2,1)S(1)}, bf16[16,16,512]{2,1,0:T(8,128)(2,1)}, u32[]{:S(2)}) copy-start(bf16[16,16,512]{2,1,0:T(8,128)(2,1)} %param.8) | copy-start | bytes 786436
  7.2 79.5 %all-gather.3.cloned.1.call-start = ((), (), s32[]{:S(2)}) async-start(), calls=%async_computation.6 | async-start | bytes 2359296 | tf_op jit(solution)/shard_map/all_gather | solution.py:392
  9.9 12.3 %collective-permute-start.2 = (bf16[4,16,512]{2,1,0:T(8,128)(2,1)S(1)}, bf16[4,16,512]{2,1,0:T(8,128)(2,1)S(1)}, u32[]{:S(2)}, u32[]{:S(2)}) collective-permute-start(bf16[4,16,512]{2,1,0:T(8,128)(2,1)S(1)} %get-tuple-element.24), channel_id=1, source_target_pairs={{32,0},{64,32},{96,64},{128,96},{160,128},{192,160},{224,192},{256... | collective-permute-start | bytes 196616 | tf_op jit(solution)/shard_map/ppermute | solution.py:401
  11.2 11.1 %collective-permute-start.1 = (bf16[4,16,512]{2,1,0:T(8,128)(2,1)S(1)}, bf16[4,16,512]{2,1,0:T(8,128)(2,1)S(1)}, u32[]{:S(2)}, u32[]{:S(2)}) collective-permute-start(bf16[4,16,512]{2,1,0:T(8,128)(2,1)S(1)} %get-tuple-element.25), channel_id=1, source_target_pairs={{0,32},{32,64},{64,96},{96,128},{128,160},{160,192},{192,224},{224... | collective-permute-start | bytes 196616 | tf_op jit(solution)/shard_map/ppermute | solution.py:400
  16.5 1.0 copy-start.5
  17.5 0.7 copy-start.8
  18.3 10.6 %collective-permute-start = (bf16[272,512]{1,0:T(8,128)(2,1)S(1)}, bf16[272,512]{1,0:T(8,128)(2,1)S(1)}, u32[]{:S(2)}, u32[]{:S(2)}) collective-permute-start(bf16[272,512]{1,0:T(8,128)(2,1)S(1)} %upstream.1.give_ref), channel_id=1, source_target_pairs={{0,32},{32,0},{64,96},{96,64},{128,160},{160,128},{192,224},{224,1... | collective-permute-start | bytes 835592 | tf_op jit(solution)/shard_map/ppermute | solution.py:406
  23.1 17.1 %copy-start.9 = (bf16[512,1536]{1,0:T(8,128)(2,1)S(1)}, bf16[512,1536]{1,0:T(8,128)(2,1)}, u32[]{:S(2)}) copy-start(bf16[512,1536]{1,0:T(8,128)(2,1)} %wqkv_ref.1) | copy-start | bytes 4718596
  23.1 17.1 %copy-start.10 = (bf16[512,512]{1,0:T(8,128)(2,1)S(1)}, bf16[512,512]{1,0:T(8,128)(2,1)}, u32[]{:S(2)}) copy-start(bf16[512,512]{1,0:T(8,128)(2,1)} %wproj_ref.1) | copy-start | bytes 1572868
  23.1 17.1 %collective-permute-start.3 = (bf16[96,512]{1,0:T(8,128)(2,1)}, bf16[96,512]{1,0:T(8,128)(2,1)S(1)}, u32[]{:S(2)}, u32[]{:S(2)}) collective-permute-start(bf16[96,512]{1,0:T(8,128)(2,1)} %reshape.68), channel_id=1, source_target_pairs={{0,1},{1,2},{2,3},{3,4},{4,5},{5,6},{6,7},{7,8},{8,9},{9,10},{10,1... | collective-permute-start | bytes 294920 | tf_op jit(solution)/shard_map/ppermute | solution.py:413
  25.2 15.1 %collective-permute-start.4 = (bf16[96,512]{1,0:T(8,128)(2,1)S(1)}, bf16[96,512]{1,0:T(8,128)(2,1)S(1)}, u32[]{:S(2)}, u32[]{:S(2)}) collective-permute-start(bf16[96,512]{1,0:T(8,128)(2,1)S(1)} %reshape.69), channel_id=1, source_target_pairs={{1,0},{2,1},{3,2},{4,3},{5,4},{6,5},{7,6},{8,7},{9,8},{10,9},{11,1... | collective-permute-start | bytes 294920 | tf_op jit(solution)/shard_map/ppermute | solution.py:414
  28.8 0.7 copy-start.11
  29.5 1.0 copy-start.12
  32.1 35.1 %all-to-all-start.1 = ((bf16[32,24,512]{2,1,0:T(8,128)(2,1)}), bf16[32,24,512]{2,1,0:T(8,128)(2,1)}, u32[]{:S(2)}, u32[]{:S(2)}) async-start(bf16[32,24,512]{2,1,0:T(8,128)(2,1)} %bitcast.10), calls=%async_computation.1 | async-start | bytes 1572864 | tf_op jit(solution)/shard_map/all_to_all | solution.py:390
  40.1 132.9 %reduce-scatter.2.cloned.1.call-start = ((), (), s32[]{:S(2)}) async-start(), calls=%async_computation.5 | async-start | bytes 2359296 | tf_op jit(solution)/shard_map/reduce_scatter | solution.py:447
  44.7 22.0 %collective-permute-start.5 = (bf16[256,512]{1,0:T(8,128)(2,1)S(1)}, bf16[256,512]{1,0:T(8,128)(2,1)S(1)}, u32[]{:S(2)}, u32[]{:S(2)}) collective-permute-start(bf16[256,512]{1,0:T(8,128)(2,1)S(1)} %front.1.mixed_ref), channel_id=1, source_target_pairs={{0,32},{32,0},{64,96},{96,64},{128,160},{160,128},{192,224},{224,1... | collective-permute-start | bytes 786440 | tf_op jit(solution)/shard_map/ppermute | solution.py:433
  95.6 1.6 copy-start
  97.2 1.4 copy-start.4
  100.1 0.9 copy-start.2
  101.0 18.5 %all-to-all-start.3 = ((bf16[32,24,512]{2,1,0:T(8,128)(2,1)}), bf16[32,24,512]{2,1,0:T(8,128)(2,1)S(1)}, u32[]{:S(2)}, u32[]{:S(2)}) async-start(bf16[32,24,512]{2,1,0:T(8,128)(2,1)} %bitcast.26), calls=%async_computation.3 | async-start | bytes 1572864 | tf_op jit(solution)/shard_map/all_to_all | solution.py:390
  107.4 1.4 copy-start.3
  110.4 0.9 copy-start.1
  119.5 18.5 %all-to-all-start.2 = ((bf16[32,24,512]{2,1,0:T(8,128)(2,1)}), bf16[32,24,512]{2,1,0:T(8,128)(2,1)S(1)}, u32[]{:S(2)}, u32[]{:S(2)}) async-start(bf16[32,24,512]{2,1,0:T(8,128)(2,1)} %bitcast.25), calls=%async_computation.2 | async-start | bytes 1572864 | tf_op jit(solution)/shard_map/all_to_all | solution.py:390
  138.4 23.4 %collective-permute-start.6 = (bf16[256,512]{1,0:T(8,128)(2,1)S(1)}, bf16[256,512]{1,0:T(8,128)(2,1)S(1)}, u32[]{:S(2)}, u32[]{:S(2)}) collective-permute-start(bf16[256,512]{1,0:T(8,128)(2,1)S(1)} %back_rows.2), channel_id=1, source_target_pairs={{0,32},{32,0},{64,96},{96,64},{128,160},{160,128},{192,224},{224,1... | collective-permute-start | bytes 786440 | tf_op jit(solution)/shard_map/ppermute | solution.py:456
  143.1 28.5 %collective-permute-start.7 = (bf16[256,512]{1,0:T(8,128)(2,1)S(1)}, bf16[256,512]{1,0:T(8,128)(2,1)S(1)}, u32[]{:S(2)}, u32[]{:S(2)}) collective-permute-start(bf16[256,512]{1,0:T(8,128)(2,1)S(1)} %back_rows.3), channel_id=1, source_target_pairs={{0,32},{32,0},{64,96},{96,64},{128,160},{160,128},{192,224},{224,1... | collective-permute-start | bytes 786440 | tf_op jit(solution)/shard_map/ppermute | solution.py:456
  173.0 1.0 copy-start.7
Sparse Core Ops, SparseCore 0:
  10.7 74.8 all-gather.2
  95.7 73.1 reduce-scatter.1

commit v5 on v4

--- a/solution.py
+++ b/solution.py
@@ -88,13 +88,6 @@
     slots_ref[...] = total.astype(jnp.bfloat16)
 
 
-def token_slots_kernel(target_ref, mixed_ref, got_ref, slots_ref):
-    rows = slots_ref.shape[0]
-    total = nn(placer(target_ref[0:1], rows), mixed_ref[...])
-    total = total + nn(placer(target_ref[1:2], rows), got_ref[...])
-    slots_ref[...] = total.astype(jnp.bfloat16)
-
-
 def back_rows_kernel(target_ref, back_ref, give_ref):
     give_ref[...] = tn(placer(target_ref[1:2], back_ref.shape[0]), back_ref[...]).astype(
         jnp.bfloat16
@@ -117,29 +110,10 @@
     down_ref[0] = sum_ref[0, width:].astype(jnp.float32) * scale
 
 
-def middle_kernel(w_hbm, x_ref, g_ref, grads_ref, hid_ref, pg_ref, w_ref, sems):
-    step = pl.program_id(0)
-    shards = w_ref.shape[1]
-    copies = [
-        pltpu.make_async_copy(w_hbm.at[pl.ds(n * shards, shards)], w_ref.at[n], sems.at[n])
-        for n in range(CHUNKS)
-    ]
-
-    @pl.when(step == 0)
-    def _():
-        for copy in copies:
-            copy.start()
-
-    for n in range(CHUNKS):
-
-        @pl.when(step == n)
-        def _():
-            copies[n].wait()
-
-    held = w_ref[step]
-    _, _, width, feature = held.shape
-    up = held[:, 0].reshape(shards * width, feature)
-    down = held[:, 1].reshape(shards * width, feature)
+def middle_kernel(w_ref, x_ref, g_ref, grads_ref, hid_ref, pg_ref):
+    shards, _, width, feature = w_ref.shape
+    up = w_ref[:, 0].reshape(shards * width, feature)
+    down = w_ref[:, 1].reshape(shards * width, feature)
     halves = 2
     rows = x_ref.shape[0] // halves
     parts = [slice(n * rows, (n + 1) * rows) for n in range(halves)]
@@ -175,7 +149,7 @@
         middle_kernel,
         grid=(CHUNKS,),
         in_specs=[
-            pl.BlockSpec(memory_space=pltpu.HBM),
+            pl.BlockSpec((step, 2, width, feature), lambda i: (i, 0, 0, 0)),
             pl.BlockSpec((rows, feature), lambda i: (0, 0)),
             pl.BlockSpec((rows, feature), lambda i: (0, 0)),
         ],
@@ -188,10 +162,6 @@
             pltpu.HBM((owners, 2 * width, feature), jnp.bfloat16),
             pltpu.HBM((ff, rows), jnp.bfloat16),
             pltpu.HBM((ff, rows), jnp.bfloat16),
-        ],
-        scratch_shapes=[
-            pltpu.VMEM((CHUNKS, step, 2, width, feature), jnp.bfloat16),
-            pltpu.SemaphoreType.DMA((CHUNKS,)),
         ],
         compiler_params=pltpu.CompilerParams(vmem_limit_bytes=MIDDLE_LIMIT),
         cost_estimate=pl.CostEstimate(
@@ -249,50 +219,76 @@
     return (window * window_side + row % window_side) * window_side + col % window_side
 
 
-def into_windows(tile):
-    ext = tile + 2 * margin_cells
-    edge, strip = margin_cells * tile, margin_cells * ext
-    piece = lax.broadcasted_iota(jnp.int32, (1, ext * ext), 1)
+def tile_top(tile, odd, other):
+    return margin_cells + tile * ((1 - odd) if other else odd)
+
+
+def edge_top(tile, odd, far):
+    high = (1 - odd) if far else odd
+    return (2 * tile + margin_cells) * high
+
+
+def into_windows(tile, odd):
+    margin, base = margin_cells, tile * tile
+    tall = 2 * tile + 2 * margin
+    edge, strip = margin * tile, margin * tall
+    cells = tall * (tile + 2 * margin)
+    piece = lax.broadcasted_iota(jnp.int32, (1, cells), 1)
+    in_tile = piece % base
+    row = tile_top(tile, odd, False) + in_tile // tile
+    row = jnp.where(piece >= base, tile_top(tile, odd, True) + in_tile // tile, row)
+    col = margin + in_tile % tile
+    start = 2 * base
+    for far in (False, True):
+        row = jnp.where(piece >= start, edge_top(tile, odd, far) + (piece - start) // tile, row)
+        start += edge
+    for side in (0, margin + tile):
+        at = (piece - start) // margin
+        side_row = edge_top(tile, odd, False) + at
+        side_row = jnp.where(at >= margin, tile_top(tile, odd, False) + at - margin, side_row)
+        side_row = jnp.where(
+            at >= margin + tile, tile_top(tile, odd, True) + at - margin - tile, side_row
+        )
+        side_row = jnp.where(
+            at >= margin + 2 * tile, edge_top(tile, odd, True) + at - margin - 2 * tile, side_row
+        )
+        row = jnp.where(piece >= start, side_row, row)
+        col = jnp.where(piece >= start, side + (piece - start) % margin, col)
+        start += strip
+    place = window_index(row, col, tile)
+    return one_hot(lax.broadcasted_iota(jnp.int32, (cells, cells), 0) == place)
+
+
+def out_of_windows(tile, odd):
     base = tile * tile
-    row, col = margin_cells + piece // tile, margin_cells + piece % tile
-    low = piece - base
-    row = jnp.where(piece >= base, low // tile, row)
-    high = piece - (base + edge)
-    row = jnp.where(piece >= base + edge, tile + margin_cells + high // tile, row)
-    left = piece - (base + 2 * edge)
-    side = piece >= base + 2 * edge
-    row = jnp.where(side, left // margin_cells, row)
-    col = jnp.where(side, left % margin_cells, col)
-    right = left - strip
-    side = piece >= base + 2 * edge + strip
-    row = jnp.where(side, right // margin_cells, row)
-    col = jnp.where(side, tile + margin_cells + right % margin_cells, col)
-    place = window_index(row, col, tile)
-    return one_hot(lax.broadcasted_iota(jnp.int32, (ext * ext, ext * ext), 0) == place)
-
-
-def out_of_windows(tile):
-    ext = tile + 2 * margin_cells
-    token = lax.broadcasted_iota(jnp.int32, (tile * tile, 1), 0)
-    place = window_index(token // tile + margin_cells, token % tile + margin_cells, tile)
-    return one_hot(lax.broadcasted_iota(jnp.int32, (tile * tile, ext * ext), 1) == place)
+    cells = (2 * tile + 2 * margin_cells) * (tile + 2 * margin_cells)
+    token = lax.broadcasted_iota(jnp.int32, (2 * base, 1), 0)
+    in_tile = token % base
+    top = jnp.where(token >= base, tile_top(tile, odd, True), tile_top(tile, odd, False))
+    place = window_index(top + in_tile // tile, margin_cells + in_tile % tile, tile)
+    return one_hot(lax.broadcasted_iota(jnp.int32, (2 * base, cells), 1) == place)
 
 
 def front_kernel(
-    at_ref, tok_ref, low_ref, high_ref, left_ref, right_ref, wqkv_ref, wproj_ref, mixed_ref, qkv_ref, ctx_ref
+    at_ref, target_ref, own_ref, other_ref, near_ref, far_ref, left_ref, right_ref, wqkv_ref, wproj_ref,
+    mixed_ref, slots_ref, qkv_ref, ctx_ref,
 ):
     bf16, f32 = jnp.bfloat16, jnp.float32
-    tokens = tok_ref[...]
-    count, feature = tokens.shape
+    count, feature = own_ref.shape
+    tile = math.isqrt(count)
     cells = window_side * window_side
     head = feature // HEADS
     group = 128 // head
+    odd = at_ref[0] % 2
+    tokens = jnp.concatenate([own_ref[...], other_ref[...]], axis=0)
     pieces = jnp.concatenate(
-        [tokens, low_ref[...], high_ref[...], left_ref[...], right_ref[...]], axis=0
-    )
-    placed = nn(into_windows(math.isqrt(count)), pieces).astype(bf16)
-    qkv_ref[...] = jnp.dot(placed, wqkv_ref[...], preferred_element_type=f32).astype(bf16)
-    first_row, last_row = at_ref[0] == 0, at_ref[0] == at_ref[1] - 1
+        [tokens, near_ref[...], far_ref[...], left_ref[...], right_ref[...]], axis=0
+    )
+    placed = nn(into_windows(tile, odd), pieces).astype(bf16)
+    for part in range(3):
+        columns = slice(part * feature, (part + 1) * feature)
+        qkv_ref[:, columns] = nn(placed, wqkv_ref[:, columns]).astype(bf16)
+    first_row, last_row = at_ref[0] < 2, at_ref[0] >= at_ref[1] - 2
     first_col, last_col = at_ref[2] == 0, at_ref[2] == at_ref[3] - 1
     lane = lax.broadcasted_iota(jnp.int32, (1, 128), 1)
     own = [
@@ -305,15 +301,15 @@
     low_bias = jnp.float32(-1e30)
     edge_bias = {
         (0, 0): jnp.where(key_row < half, jnp.where(first_row, low_bias, 0.0), 0.0),
-        (0, 2): jnp.where(key_row >= half, jnp.where(last_row, low_bias, 0.0), 0.0),
+        (0, 4): jnp.where(key_row >= half, jnp.where(last_row, low_bias, 0.0), 0.0),
         (1, 0): jnp.where(key_col < half, jnp.where(first_col, low_bias, 0.0), 0.0),
         (1, 2): jnp.where(key_col >= half, jnp.where(last_col, low_bias, 0.0), 0.0),
     }
     scale = 1.0 / math.sqrt(head)
-    for window in range(9):
+    for window in range(15):
         wi, wj = window // 3, window % 3
         bias = None
-        if wi != 1:
+        if wi in (0, 4):
             bias = edge_bias[0, wi]
         if wj != 1:
             bias = edge_bias[1, wj] if bias is None else bias + edge_bias[1, wj]
@@ -336,30 +332,35 @@
             for h in range(1, group):
                 mine = mine + wide[h * cells : (h + 1) * cells] * own[h]
             ctx_ref[rows, g * 128 : (g + 1) * 128] = mine.astype(bf16)
-    context = nn(out_of_windows(math.isqrt(count)), ctx_ref[...]).astype(bf16)
-    attended = jnp.dot(context, wproj_ref[...], preferred_element_type=f32)
+    context = nn(out_of_windows(tile, odd), ctx_ref[...]).astype(bf16)
+    attended = nn(context, wproj_ref[...])
     centred = attended - jnp.mean(attended, axis=-1, keepdims=True)
     spread_of = jnp.mean(centred * centred, axis=-1, keepdims=True)
     mixed = (tokens.astype(f32) + centred * lax.rsqrt(spread_of + 1e-05)).astype(bf16)
-    mixed_ref[...] = mixed
-
-
-def front(at, tokens, low, high, left, right, w_qkv, w_proj):
-    count, feature = tokens.shape
-    ext = (math.isqrt(count) + 2 * margin_cells) ** 2
+    mixed_ref[...] = mixed[:count]
+    rows = slots_ref.shape[0]
+    slots = nn(placer(target_ref[0:1], rows), mixed[:count])
+    slots = slots + nn(placer(target_ref[1:2], rows), mixed[count:])
+    slots_ref[...] = slots.astype(bf16)
+
+
+def front(at, target, own, other, near, far, left, right, w_qkv, w_proj, slot_count):
+    count, feature = own.shape
+    tile = math.isqrt(count)
+    cells = (2 * tile + 2 * margin_cells) * (tile + 2 * margin_cells)
     smem = pl.BlockSpec(memory_space=pltpu.SMEM)
     vmem = pl.BlockSpec(memory_space=pltpu.VMEM)
     return vmem_call(
         front_kernel,
-        [((count, feature), jnp.bfloat16)],
+        [((count, feature), jnp.bfloat16), ((slot_count, feature), jnp.bfloat16)],
         "front",
-        4_000_000_000,
-        in_specs=[smem] + [vmem] * 7,
+        7_000_000_000,
+        in_specs=[smem] + [vmem] * 9,
         scratch_shapes=[
-            pltpu.VMEM((ext, 3 * feature), jnp.bfloat16),
-            pltpu.VMEM((ext, feature), jnp.bfloat16),
+            pltpu.VMEM((cells, 3 * feature), jnp.bfloat16),
+            pltpu.VMEM((cells, feature), jnp.bfloat16),
         ],
-    )(at, tokens, low, high, left, right, w_qkv, w_proj)[0]
+    )(at, target, own, other, near, far, left, right, w_qkv, w_proj)
 
 
 def shifts(axis):
@@ -372,6 +373,15 @@
     count = lax.axis_size(axis)
     groups = [list(range(parity, count, 2)) for parity in range(2)]
     return groups, [(i, i ^ 1) for i in range(count)]
+
+
+def pair_edges(axis):
+    count = lax.axis_size(axis)
+    near = [(z, z + 1) for z in range(1, count - 1, 2)]
+    near += [(z, z - 1) for z in range(2, count, 2)]
+    far = [(z, z + 2) for z in range(1, count - 2, 2)]
+    far += [(z, z - 2) for z in range(2, count, 2)]
+    return near, far
 
 
 def per_device(tokens, gate, route, cotangent, w_qkv, w_proj, w_up, w_down):
@@ -396,9 +406,12 @@
         tiled=False,
         axis_index_groups=groups,
     )
-    forward, backward = shifts("rep")
-    low = lax.ppermute(tokens[tile_rows - margin :], "rep", forward)
-    high = lax.ppermute(tokens[:margin], "rep", backward)
+    near_swap, far_swap = pair_edges("rep")
+    odd = lax.axis_index("rep") % 2
+    edge = jnp.where(odd == 0, tokens[:margin], tokens[tile_rows - margin :])
+    other = lax.ppermute(tokens, "rep", swap)
+    near = lax.ppermute(edge, "rep", near_swap)
+    far = lax.ppermute(edge, "rep", far_swap)
     gate_rows = gate.reshape(tok_count, 1)
     [give] = vmem_call(
         upstream_kernel, [((tok_count + EXTRA, feature), bf16)], "upstream", 1_000_000, count=3
@@ -407,7 +420,7 @@
     forward, backward = shifts("exp")
 
     def strip(cols):
-        parts = [low[:, cols], tokens[:, cols], high[:, cols]]
+        parts = [near[:, cols], tokens[:, cols], other[:, cols], far[:, cols]]
         return jnp.concatenate(parts, axis=0).reshape(-1, feature)
 
     left = lax.ppermute(strip(slice(tile_cols - margin, tile_cols)), "exp", forward)
@@ -420,17 +433,6 @@
             jnp.int32(experts),
         ]
     ).astype(jnp.int32)
-    mixed = front(
-        at,
-        tokens.reshape(tok_count, feature),
-        low.reshape(-1, feature),
-        high.reshape(-1, feature),
-        left,
-        right,
-        w_qkv,
-        w_proj,
-    )
-    got_mixed = lax.ppermute(mixed, "rep", swap)
     slots_g, target = vmem_call(
         functools.partial(grad_slots_kernel, experts, capacity),
         [rows_of, ((2, tok_count), jnp.int32)],
@@ -439,8 +441,18 @@
         count=2,
     )(give, got)
     slot_g = dispatch(slots_g)
-    [slots_x] = vmem_call(token_slots_kernel, [rows_of], "token_slots", 400_000_000, count=3)(
-        target, mixed, got_mixed
+    mixed, slots_x = front(
+        at,
+        target,
+        tokens.reshape(tok_count, feature),
+        other.reshape(tok_count, feature),
+        near.reshape(-1, feature),
+        far.reshape(-1, feature),
+        left,
+        right,
+        w_qkv,
+        w_proj,
+        slot_count,
     )
     slot_x = dispatch(slots_x)
     grads, hidden, pre_grad = middle(weights, slot_x, slot_g)
@@ -448,16 +460,19 @@
         grads, "rep", scatter_dimension=0, tiled=True, axis_index_groups=groups
     )
 
-    def returned(activity, side):
-        rows = dispatch(back(weights, activity, side))
+    def exchanged(rows):
         [theirs] = vmem_call(
             back_rows_kernel, [((tok_count, feature), bf16)], "back_rows", 200_000_000, count=2
         )(target, rows)
-        return rows, lax.ppermute(theirs, "rep", swap)
-
+        return lax.ppermute(theirs, "rep", swap)
+
+    back_out = dispatch(back(weights, hidden, 1))
+    back_in = dispatch(back(weights, pre_grad, 0))
+    got_out = exchanged(back_out)
+    back_in, got_out = lax.optimization_barrier((back_in, got_out))
     layer_out, input_grad = vmem_call(
         combine_kernel, [((tok_count, feature), bf16)] * 2, "combine", 400_000_000, count=7
-    )(target, *returned(hidden, 1), *returned(pre_grad, 0), mixed, gate_rows)
+    )(target, back_out, got_out, back_in, exchanged(back_in), mixed, gate_rows)
     grad_up, grad_down = vmem_call(
         functools.partial(gradients_kernel, 1.0 / lax.axis_size("rep")),
         [(w_up.shape, f32)] * 2,

time: 184 us -> 179 us (0.973)
  waiting for transfers between devices: 65.7 us -> 51.2 us
  starting transfers between devices: 45.7 us -> 53.7 us
  Pallas kernels: 21.6 us -> 23.8 us
    ppermute x5, waiting for transfers between devices: 45.8 us -> 28.7 us  [the longest x2 26.4 us: exchanged(): return lax.ppermute(theirs, 'rep', swap)]
    all_to_all x3, starting transfers between devices: 20.8 us -> 30 us  [dispatch(): return lax.all_to_all(blocks, 'exp', 0, 0, tiled=True).reshape(-1, feature)]
    pallas_call x5 -> x4, Pallas kernels: 14.7 us -> 16.9 us  [the longest x1 8.19 us: front(): vmem_call(front_kernel, [((count, feature), jnp.bfloat16), ((slot_count,...]
    ppermute x1, starting transfers between devices: 3.83 us -> 1.92 us  [per_device(): got = lax.ppermute(give, 'rep', swap)]
    all_gather x1, waiting for transfers between devices: 0.01 us -> 1.88 us  [per_device(): lax.all_gather(jnp.concatenate([w_up, w_down], axis=0), 'rep', axis=0, ti...]
    unnamed x26 -> x22, local copies, waits for them, and re-layouts: 10.4 us -> 10.1 us
  transfers between devices with their start and end apart: 13 -> 13, of which waited for: 5 -> 8; matrix products, arithmetic and copies ran while one was open for 1% -> 1% of each run, Pallas kernels for 7% -> 9%
where the time goes in v5:
time: 179 us; the launch traced here: 175 us
  starting transfers between devices  53.7 us (30%)
  waiting for transfers between devices  51.2 us (29%)
  Pallas kernels  23.8 us (13%)
  blocking collectives  18.2 us (10%)
  between operations  14.3 us (8%)
  local copies, waits for them, and re-layouts  11.2 us (6%)
  other arithmetic  2.95 us (2%)
    all_to_all x3, starting transfers between devices, dispatch(): return lax.all_to_all(blocks, 'exp', 0, 0, tiled=True).reshape(-1, feature)  30 us
    ppermute x2, waiting for transfers between devices, exchanged(): return lax.ppermute(theirs, 'rep', swap)  26.4 us
    all_to_all x3, waiting for transfers between devices, dispatch(): return lax.all_to_all(blocks, 'exp', 0, 0, tiled=True).reshape(-1, feature)  20.2 us
    all_to_all x1, blocking collectives, dispatch(): return lax.all_to_all(blocks, 'exp', 0, 0, tiled=True).reshape(-1, feature)  18.2 us
    unnamed x22, local copies, waits for them, and re-layouts  10.1 us
    ppermute x1, starting transfers between devices, per_device(): other = lax.ppermute(tokens, 'rep', swap)  8.97 us
    pallas_call x1, Pallas kernels, front(): vmem_call(front_kernel, [((count, feature), jnp.bfloat16), ((slot_count,...  8.19 us
    pallas_call x1, Pallas kernels, middle(): pl.pallas_call(middle_kernel, grid=(CHUNKS,), in_specs=[pl.BlockSpec((ste...  7.89 us
  transfers between devices with their start and end apart: 13, of which 8 were waited for; matrix products, arithmetic and copies ran while one was open for 1% of the time, Pallas kernels for 9%

profile of v5, /device:TPU:6, one launch (start us, length us, event | category | flops | bytes accessed | tf_op | source)
XLA Modules:
  0.0 175.3 jit_solution(6404470818501597297)
XLA Ops:
  7.2 0.0 copy-start.6
  7.2 0.0 all-gather.3.cloned.1.call-start
  7.2 1.7 pad_maximum_fusion
  9.0 0.0 all-gather.3.cloned.1.call-update
  9.0 0.9 slice_select_fusion
  9.9 1.3 collective-permute-start.3
  11.2 0.7 collective-permute-start.2
  11.8 9.0 %collective-permute-start.1 = (bf16[16,16,512]{2,1,0:T(8,128)(2,1)}, bf16[16,16,512]{2,1,0:T(8,128)(2,1)S(1)}, u32[]{:S(2)}, u32[]{:S(2)}) collective-permute-start(bf16[16,16,512]{2,1,0:T(8,128)(2,1)} %param.8), channel_id=1, source_target_pairs={{0,32},{32,0},{64,96},{96,64},{128,160},{160,128},{192,224},{224,1... | collective-permute-start | bytes 786440 | tf_op jit(solution)/shard_map/ppermute | solution.py:412
  20.8 0.8 reshape.85.gate_ref
  21.6 0.0 copy-start.5
  21.6 0.9 copy-done.5
  22.6 0.7 copy-done.8
  23.3 0.1 upstream.1.give_ref
  23.4 1.9 %collective-permute-start = (bf16[272,512]{1,0:T(8,128)(2,1)S(1)}, bf16[272,512]{1,0:T(8,128)(2,1)S(1)}, u32[]{:S(2)}, u32[]{:S(2)}) collective-permute-start(bf16[272,512]{1,0:T(8,128)(2,1)S(1)} %upstream.1.give_ref), channel_id=1, source_target_pairs={{0,32},{32,0},{64,96},{96,64},{128,160},{160,128},{192,224},{224,1... | collective-permute-start | bytes 835592 | tf_op jit(solution)/shard_map/ppermute | solution.py:419
  25.3 0.0 copy-done.6
  25.3 0.1 fusion
  25.4 0.0 collective-permute-done.3
  25.4 0.0 collective-permute-done.2
  25.4 2.2 %collective-permute-done.1 = bf16[16,16,512]{2,1,0:T(8,128)(2,1)S(1)} collective-permute-done((bf16[16,16,512]{2,1,0:T(8,128)(2,1)}, bf16[16,16,512]{2,1,0:T(8,128)(2,1)S(1)}, u32[]{:S(2)}, u32[]{:S(2)}) %collective-permute-start.1) | collective-permute-done | bytes 262176 | tf_op jit(solution)/shard_map/ppermute | solution.py:412
  27.7 0.1 fusion.1
  27.7 0.1 pad_maximum_fusion.2
  27.9 0.1 pad_maximum_fusion.1
  28.1 1.9 %collective-permute-start.4 = (bf16[160,512]{1,0:T(8,128)(2,1)S(1)}, bf16[160,512]{1,0:T(8,128)(2,1)S(1)}, u32[]{:S(2)}, u32[]{:S(2)}) collective-permute-start(bf16[160,512]{1,0:T(8,128)(2,1)S(1)} %reshape.72), channel_id=1, source_target_pairs={{0,1},{1,2},{2,3},{3,4},{4,5},{5,6},{6,7},{7,8},{8,9},{9,10},{10,1... | collective-permute-start | bytes 491528 | tf_op jit(solution)/shard_map/ppermute | solution.py:426
  30.0 3.6 %collective-permute-start.5 = (bf16[160,512]{1,0:T(8,128)(2,1)S(1)}, bf16[160,512]{1,0:T(8,128)(2,1)S(1)}, u32[]{:S(2)}, u32[]{:S(2)}) collective-permute-start(bf16[160,512]{1,0:T(8,128)(2,1)S(1)} %reshape.73), channel_id=1, source_target_pairs={{1,0},{2,1},{3,2},{4,3},{5,4},{6,5},{7,6},{8,7},{9,8},{10,9},{11,1... | collective-permute-start | bytes 491528 | tf_op jit(solution)/shard_map/ppermute | solution.py:427
  33.7 0.0 copy-start.10
  33.7 0.3 collective-permute-done.got_ref
  34.0 1.6 grad_slots.1
  35.6 16.0 %all-to-all-start.1 = ((bf16[32,24,512]{2,1,0:T(8,128)(2,1)}), bf16[32,24,512]{2,1,0:T(8,128)(2,1)}, u32[]{:S(2)}, u32[]{:S(2)}) async-start(bf16[32,24,512]{2,1,0:T(8,128)(2,1)} %bitcast.11), calls=%async_computation.1 | async-start | bytes 1572864 | tf_op jit(solution)/shard_map/all_to_all | solution.py:400
  51.6 0.0 reduce-scatter.2.cloned.1.call-start
  51.7 0.1 pad_add_fusion.at_ref
  51.8 0.0 collective-permute-done.4.left_ref
  51.8 0.0 collective-permute-done.5.right_ref
  51.8 0.0 copy-done.10
  51.8 0.0 copy-start.9
  51.8 1.4 copy-done.9
  53.2 8.2 %front.1 = (bf16[256,512]{1,0:T(8,128)(2,1)S(1)}, bf16[768,512]{1,0:T(8,128)(2,1)S(1)}) custom-call(s32[4]{0:T(128)S(1)} %pad_add_fusion.at_ref, s32[2,256]{1,0:T(2,128)S(1)} %get-tuple-element.17.target_ref, bf16[256,512]{1,0:T(8,128)(2,1)S(1)} %bitcast.30, bf16[256,512]{1,0:T(8,128)(2,1)S(1)} %bitcast.31, bf16[64,512]{1,0:T(8,128)(2,1)S(1)} %bitcast.33, ...), custom_call_target="tpu_custom_call" | custom-call | flops 7000000000 | bytes 3000000 | tf_op jit(solution)/shard_map/front/pallas_call | solution.py:353
  61.4 2.4 %all-to-all-done.1 = bf16[32,24,512]{2,1,0:T(8,128)(2,1)} async-done(((bf16[32,24,512]{2,1,0:T(8,128)(2,1)}), bf16[32,24,512]{2,1,0:T(8,128)(2,1)}, u32[]{:S(2)}, u32[]{:S(2)}) %all-to-all-start.1) | async-done | bytes 786464 | tf_op jit(solution)/shard_map/all_to_all | solution.py:400
  63.8 18.2 %all_to_all.20 = bf16[32,24,512]{2,1,0:T(8,128)(2,1)} all-to-all(bf16[32,24,512]{2,1,0:T(8,128)(2,1)S(1)} %bitcast.28), channel_id=1, replica_groups=mesh['rep'=16,'exp'=32] {'exp'}, dimensions={0} | all-to-all | bytes 1572864 | tf_op jit(solution)/shard_map/all_to_all | solution.py:400
  82.0 1.9 %all-gather.3.cloned.1.call-done = bf16[16,128,512]{2,1,0:T(8,128)(2,1)} async-done(((bf16[2,128,512]{2,1,0:T(8,128)(2,1)}), bf16[16,128,512]{2,1,0:T(8,128)(2,1)}) %all-gather.3.cloned.1.call-update) | async-done | bytes 2097168 | tf_op jit(solution)/shard_map/all_gather | solution.py:402
  83.8 7.9 %middle.1 = (bf16[8,256,512]{2,1,0:T(8,128)(2,1)}, bf16[1024,768]{1,0:T(8,128)(2,1)}, bf16[1024,768]{1,0:T(8,128)(2,1)}) custom-call(bf16[8,2,128,512]{3,2,1,0:T(8,128)(2,1)} %bitcast.19, bf16[768,512]{1,0:T(8,128)(2,1)} %bitcast.35, bf16[768,512]{1,0:T(8,128)(2,1)} %bitcast.12.g_ref), custom_call_target="tpu_custom_call" | custom-call | flops 3221225472 | bytes 7340032 | tf_op jit(solution)/shard_map/middle/pallas_call | solution.py:148
  91.7 0.0 reduce-scatter.2.cloned.1.call-update
  91.8 1.6 copy-done
  93.3 1.4 copy-done.4
  94.7 1.5 back.2
  96.3 0.0 copy-start.2
  96.3 0.9 copy-done.2
  97.2 7.6 %all-to-all-start.2 = ((bf16[32,24,512]{2,1,0:T(8,128)(2,1)}), bf16[32,24,512]{2,1,0:T(8,128)(2,1)S(1)}, u32[]{:S(2)}, u32[]{:S(2)}) async-start(bf16[32,24,512]{2,1,0:T(8,128)(2,1)} %bitcast.27), calls=%async_computation.2 | async-start | bytes 1572864 | tf_op jit(solution)/shard_map/all_to_all | solution.py:400
  104.8 0.0 copy-start.3
  104.8 1.4 copy-done.3
  106.2 1.5 back.3
  107.8 0.0 copy-start.1
  107.8 0.9 copy-done.1
  108.7 8.1 %all-to-all-done.2 = bf16[32,24,512]{2,1,0:T(8,128)(2,1)S(1)} async-done(((bf16[32,24,512]{2,1,0:T(8,128)(2,1)}), bf16[32,24,512]{2,1,0:T(8,128)(2,1)S(1)}, u32[]{:S(2)}, u32[]{:S(2)}) %all-to-all-start.2) | async-done | bytes 786464 | tf_op jit(solution)/shard_map/all_to_all | solution.py:400
  116.8 6.4 %all-to-all-start.3 = ((bf16[32,24,512]{2,1,0:T(8,128)(2,1)}), bf16[32,24,512]{2,1,0:T(8,128)(2,1)S(1)}, u32[]{:S(2)}, u32[]{:S(2)}) async-start(bf16[32,24,512]{2,1,0:T(8,128)(2,1)} %bitcast.26), calls=%async_computation.3 | async-start | bytes 1572864 | tf_op jit(solution)/shard_map/all_to_all | solution.py:400
  123.2 0.4 back_rows.2
  123.6 1.9 %collective-permute-start.6 = (bf16[256,512]{1,0:T(8,128)(2,1)S(1)}, bf16[256,512]{1,0:T(8,128)(2,1)S(1)}, u32[]{:S(2)}, u32[]{:S(2)}) collective-permute-start(bf16[256,512]{1,0:T(8,128)(2,1)S(1)} %back_rows.2), channel_id=1, source_target_pairs={{0,32},{32,0},{64,96},{96,64},{128,160},{160,128},{192,224},{224,1... | collective-permute-start | bytes 786440 | tf_op jit(solution)/shard_map/ppermute | solution.py:467
  125.6 9.7 %all-to-all-done.3 = bf16[32,24,512]{2,1,0:T(8,128)(2,1)S(1)} async-done(((bf16[32,24,512]{2,1,0:T(8,128)(2,1)}), bf16[32,24,512]{2,1,0:T(8,128)(2,1)S(1)}, u32[]{:S(2)}, u32[]{:S(2)}) %all-to-all-start.3) | async-done | bytes 786464 | tf_op jit(solution)/shard_map/all_to_all | solution.py:400
  135.3 11.6 %collective-permute-done.6.got_out_ref = bf16[256,512]{1,0:T(8,128)(2,1)S(1)} collective-permute-done((bf16[256,512]{1,0:T(8,128)(2,1)S(1)}, bf16[256,512]{1,0:T(8,128)(2,1)S(1)}, u32[]{:S(2)}, u32[]{:S(2)}) %collective-permute-start.6) | collective-permute-done | bytes 262176 | tf_op jit(solution)/shard_map/ppermute | solution.py:467
  146.9 0.4 back_rows.3
  147.3 3.2 %collective-permute-start.7 = (bf16[256,512]{1,0:T(8,128)(2,1)S(1)}, bf16[256,512]{1,0:T(8,128)(2,1)S(1)}, u32[]{:S(2)}, u32[]{:S(2)}) collective-permute-start(bf16[256,512]{1,0:T(8,128)(2,1)S(1)} %back_rows.3), channel_id=1, source_target_pairs={{0,32},{32,0},{64,96},{96,64},{128,160},{160,128},{192,224},{224,1... | collective-permute-start | bytes 786440 | tf_op jit(solution)/shard_map/ppermute | solution.py:467
  150.6 14.8 %collective-permute-done.7.got_in_ref = bf16[256,512]{1,0:T(8,128)(2,1)S(1)} collective-permute-done((bf16[256,512]{1,0:T(8,128)(2,1)S(1)}, bf16[256,512]{1,0:T(8,128)(2,1)S(1)}, u32[]{:S(2)}, u32[]{:S(2)}) %collective-permute-start.7) | collective-permute-done | bytes 262176 | tf_op jit(solution)/shard_map/ppermute | solution.py:467
  165.4 1.3 combine.1
  166.7 0.9 copy-done.7
  167.7 0.8 gradients.1
  (9 shorter events, 0.1 us)
Async XLA Ops:
  7.2 18.1 %copy-start.6 = (bf16[16,16,512]{2,1,0:T(8,128)(2,1)S(1)}, bf16[16,16,512]{2,1,0:T(8,128)(2,1)}, u32[]{:S(2)}) copy-start(bf16[16,16,512]{2,1,0:T(8,128)(2,1)} %param.8) | copy-start | bytes 786436
  7.2 76.7 %all-gather.3.cloned.1.call-start = ((), (), s32[]{:S(2)}) async-start(), calls=%async_computation.6 | async-start | bytes 2359296 | tf_op jit(solution)/shard_map/all_gather | solution.py:402
  9.9 15.5 %collective-permute-start.3 = (bf16[4,16,512]{2,1,0:T(8,128)(2,1)S(1)}, bf16[4,16,512]{2,1,0:T(8,128)(2,1)S(1)}, u32[]{:S(2)}, u32[]{:S(2)}) collective-permute-start(bf16[4,16,512]{2,1,0:T(8,128)(2,1)S(1)} %slice_select_fusion), channel_id=1, source_target_pairs={{32,96},{96,160},{160,224},{224,288},{288,352},{352,416},{416,480}... | collective-permute-start | bytes 196616 | tf_op jit(solution)/shard_map/ppermute | solution.py:414
  11.2 14.2 %collective-permute-start.2 = (bf16[4,16,512]{2,1,0:T(8,128)(2,1)S(1)}, bf16[4,16,512]{2,1,0:T(8,128)(2,1)S(1)}, u32[]{:S(2)}, u32[]{:S(2)}) collective-permute-start(bf16[4,16,512]{2,1,0:T(8,128)(2,1)S(1)} %slice_select_fusion), channel_id=1, source_target_pairs={{32,64},{96,128},{160,192},{224,256},{288,320},{352,384},{416,448}... | collective-permute-start | bytes 196616 | tf_op jit(solution)/shard_map/ppermute | solution.py:413
  11.8 15.8 %collective-permute-start.1 = (bf16[16,16,512]{2,1,0:T(8,128)(2,1)}, bf16[16,16,512]{2,1,0:T(8,128)(2,1)S(1)}, u32[]{:S(2)}, u32[]{:S(2)}) collective-permute-start(bf16[16,16,512]{2,1,0:T(8,128)(2,1)} %param.8), channel_id=1, source_target_pairs={{0,32},{32,0},{64,96},{96,64},{128,160},{160,128},{192,224},{224,1... | collective-permute-start | bytes 786440 | tf_op jit(solution)/shard_map/ppermute | solution.py:412
  21.6 1.0 copy-start.5
  22.6 0.7 copy-start.8
  23.4 10.6 %collective-permute-start = (bf16[272,512]{1,0:T(8,128)(2,1)S(1)}, bf16[272,512]{1,0:T(8,128)(2,1)S(1)}, u32[]{:S(2)}, u32[]{:S(2)}) collective-permute-start(bf16[272,512]{1,0:T(8,128)(2,1)S(1)} %upstream.1.give_ref), channel_id=1, source_target_pairs={{0,32},{32,0},{64,96},{96,64},{128,160},{160,128},{192,224},{224,1... | collective-permute-start | bytes 835592 | tf_op jit(solution)/shard_map/ppermute | solution.py:419
  28.1 23.6 %collective-permute-start.4 = (bf16[160,512]{1,0:T(8,128)(2,1)S(1)}, bf16[160,512]{1,0:T(8,128)(2,1)S(1)}, u32[]{:S(2)}, u32[]{:S(2)}) collective-permute-start(bf16[160,512]{1,0:T(8,128)(2,1)S(1)} %reshape.72), channel_id=1, source_target_pairs={{0,1},{1,2},{2,3},{3,4},{4,5},{5,6},{6,7},{7,8},{8,9},{9,10},{10,1... | collective-permute-start | bytes 491528 | tf_op jit(solution)/shard_map/ppermute | solution.py:426
  30.0 21.7 %collective-permute-start.5 = (bf16[160,512]{1,0:T(8,128)(2,1)S(1)}, bf16[160,512]{1,0:T(8,128)(2,1)S(1)}, u32[]{:S(2)}, u32[]{:S(2)}) collective-permute-start(bf16[160,512]{1,0:T(8,128)(2,1)S(1)} %reshape.73), channel_id=1, source_target_pairs={{1,0},{2,1},{3,2},{4,3},{5,4},{6,5},{7,6},{8,7},{9,8},{10,9},{11,1... | collective-permute-start | bytes 491528 | tf_op jit(solution)/shard_map/ppermute | solution.py:427
  33.7 18.1 %copy-start.10 = (bf16[512,512]{1,0:T(8,128)(2,1)S(1)}, bf16[512,512]{1,0:T(8,128)(2,1)}, u32[]{:S(2)}) copy-start(bf16[512,512]{1,0:T(8,128)(2,1)} %wproj_ref.1) | copy-start | bytes 1572868
  35.6 28.1 %all-to-all-start.1 = ((bf16[32,24,512]{2,1,0:T(8,128)(2,1)}), bf16[32,24,512]{2,1,0:T(8,128)(2,1)}, u32[]{:S(2)}, u32[]{:S(2)}) async-start(bf16[32,24,512]{2,1,0:T(8,128)(2,1)} %bitcast.11), calls=%async_computation.1 | async-start | bytes 1572864 | tf_op jit(solution)/shard_map/all_to_all | solution.py:400
  51.6 115.1 %reduce-scatter.2.cloned.1.call-start = ((), (), s32[]{:S(2)}) async-start(), calls=%async_computation.5 | async-start | bytes 2359296 | tf_op jit(solution)/shard_map/reduce_scatter | solution.py:459
  51.8 1.4 copy-start.9
  91.7 1.6 copy-start
  93.3 1.4 copy-start.4
  96.3 0.9 copy-start.2
  97.2 19.6 %all-to-all-start.2 = ((bf16[32,24,512]{2,1,0:T(8,128)(2,1)}), bf16[32,24,512]{2,1,0:T(8,128)(2,1)S(1)}, u32[]{:S(2)}, u32[]{:S(2)}) async-start(bf16[32,24,512]{2,1,0:T(8,128)(2,1)} %bitcast.27), calls=%async_computation.2 | async-start | bytes 1572864 | tf_op jit(solution)/shard_map/all_to_all | solution.py:400
  104.8 1.4 copy-start.3
  107.8 0.9 copy-start.1
  116.8 18.5 %all-to-all-start.3 = ((bf16[32,24,512]{2,1,0:T(8,128)(2,1)}), bf16[32,24,512]{2,1,0:T(8,128)(2,1)S(1)}, u32[]{:S(2)}, u32[]{:S(2)}) async-start(bf16[32,24,512]{2,1,0:T(8,128)(2,1)} %bitcast.26), calls=%async_computation.3 | async-start | bytes 1572864 | tf_op jit(solution)/shard_map/all_to_all | solution.py:400
  123.6 23.3 %collective-permute-start.6 = (bf16[256,512]{1,0:T(8,128)(2,1)S(1)}, bf16[256,512]{1,0:T(8,128)(2,1)S(1)}, u32[]{:S(2)}, u32[]{:S(2)}) collective-permute-start(bf16[256,512]{1,0:T(8,128)(2,1)S(1)} %back_rows.2), channel_id=1, source_target_pairs={{0,32},{32,0},{64,96},{96,64},{128,160},{160,128},{192,224},{224,1... | collective-permute-start | bytes 786440 | tf_op jit(solution)/shard_map/ppermute | solution.py:467
  147.3 18.0 %collective-permute-start.7 = (bf16[256,512]{1,0:T(8,128)(2,1)S(1)}, bf16[256,512]{1,0:T(8,128)(2,1)S(1)}, u32[]{:S(2)}, u32[]{:S(2)}) collective-permute-start(bf16[256,512]{1,0:T(8,128)(2,1)S(1)} %back_rows.3), channel_id=1, source_target_pairs={{0,32},{32,0},{64,96},{96,64},{128,160},{160,128},{192,224},{224,1... | collective-permute-start | bytes 786440 | tf_op jit(solution)/shard_map/ppermute | solution.py:467
  166.7 1.0 copy-start.7
Sparse Core Ops, SparseCore 0:
  10.7 73.1 all-gather.2
  91.9 74.0 reduce-scatter.1

commit v6 on v4

--- a/solution.py
+++ b/solution.py
@@ -117,29 +117,10 @@
     down_ref[0] = sum_ref[0, width:].astype(jnp.float32) * scale
 
 
-def middle_kernel(w_hbm, x_ref, g_ref, grads_ref, hid_ref, pg_ref, w_ref, sems):
-    step = pl.program_id(0)
-    shards = w_ref.shape[1]
-    copies = [
-        pltpu.make_async_copy(w_hbm.at[pl.ds(n * shards, shards)], w_ref.at[n], sems.at[n])
-        for n in range(CHUNKS)
-    ]
-
-    @pl.when(step == 0)
-    def _():
-        for copy in copies:
-            copy.start()
-
-    for n in range(CHUNKS):
-
-        @pl.when(step == n)
-        def _():
-            copies[n].wait()
-
-    held = w_ref[step]
-    _, _, width, feature = held.shape
-    up = held[:, 0].reshape(shards * width, feature)
-    down = held[:, 1].reshape(shards * width, feature)
+def middle_kernel(w_ref, x_ref, g_ref, grads_ref, hid_ref, pg_ref):
+    shards, _, width, feature = w_ref.shape
+    up = w_ref[:, 0].reshape(shards * width, feature)
+    down = w_ref[:, 1].reshape(shards * width, feature)
     halves = 2
     rows = x_ref.shape[0] // halves
     parts = [slice(n * rows, (n + 1) * rows) for n in range(halves)]
@@ -175,7 +156,7 @@
         middle_kernel,
         grid=(CHUNKS,),
         in_specs=[
-            pl.BlockSpec(memory_space=pltpu.HBM),
+            pl.BlockSpec((step, 2, width, feature), lambda i: (i, 0, 0, 0)),
             pl.BlockSpec((rows, feature), lambda i: (0, 0)),
             pl.BlockSpec((rows, feature), lambda i: (0, 0)),
         ],
@@ -188,10 +169,6 @@
             pltpu.HBM((owners, 2 * width, feature), jnp.bfloat16),
             pltpu.HBM((ff, rows), jnp.bfloat16),
             pltpu.HBM((ff, rows), jnp.bfloat16),
-        ],
-        scratch_shapes=[
-            pltpu.VMEM((CHUNKS, step, 2, width, feature), jnp.bfloat16),
-            pltpu.SemaphoreType.DMA((CHUNKS,)),
         ],
         compiler_params=pltpu.CompilerParams(vmem_limit_bytes=MIDDLE_LIMIT),
         cost_estimate=pl.CostEstimate(
@@ -368,10 +345,15 @@
     return forward, [(target, source) for source, target in forward]
 
 
-def sharing(axis):
-    count = lax.axis_size(axis)
+def sharing():
+    count, width = lax.axis_size("rep"), lax.axis_size("exp")
     groups = [list(range(parity, count, 2)) for parity in range(2)]
-    return groups, [(i, i ^ 1) for i in range(count)]
+    swap = []
+    for rep in range(count):
+        for exp in range(width):
+            partner = (rep + 1) % count if (rep + exp) % 2 == 0 else (rep - 1) % count
+            swap.append((rep * width + exp, partner * width + exp))
+    return groups, swap
 
 
 def per_device(tokens, gate, route, cotangent, w_qkv, w_proj, w_up, w_down):
@@ -383,7 +365,10 @@
     slot_count = 2 * experts * capacity
     bf16, f32 = jnp.bfloat16, jnp.float32
     rows_of = ((slot_count, feature), bf16)
-    groups, swap = sharing("rep")
+    groups, swap = sharing()
+
+    def exchange(rows):
+        return lax.ppermute(rows, ("rep", "exp"), swap)
 
     def dispatch(rows):
         blocks = rows.reshape(experts, -1, feature)
@@ -403,7 +388,7 @@
     [give] = vmem_call(
         upstream_kernel, [((tok_count + EXTRA, feature), bf16)], "upstream", 1_000_000, count=3
     )(route.reshape(1, tok_count), gate_rows, cotangent.reshape(tok_count, feature))
-    got = lax.ppermute(give, "rep", swap)
+    got = exchange(give)
     forward, backward = shifts("exp")
 
     def strip(cols):
@@ -430,7 +415,7 @@
         w_qkv,
         w_proj,
     )
-    got_mixed = lax.ppermute(mixed, "rep", swap)
+    got_mixed = exchange(mixed)
     slots_g, target = vmem_call(
         functools.partial(grad_slots_kernel, experts, capacity),
         [rows_of, ((2, tok_count), jnp.int32)],
@@ -448,16 +433,19 @@
         grads, "rep", scatter_dimension=0, tiled=True, axis_index_groups=groups
     )
 
-    def returned(activity, side):
-        rows = dispatch(back(weights, activity, side))
+    def exchanged(rows):
         [theirs] = vmem_call(
             back_rows_kernel, [((tok_count, feature), bf16)], "back_rows", 200_000_000, count=2
         )(target, rows)
-        return rows, lax.ppermute(theirs, "rep", swap)
-
+        return exchange(theirs)
+
+    back_out = dispatch(back(weights, hidden, 1))
+    back_in = dispatch(back(weights, pre_grad, 0))
+    got_out = exchanged(back_out)
+    back_in, got_out = lax.optimization_barrier((back_in, got_out))
     layer_out, input_grad = vmem_call(
         combine_kernel, [((tok_count, feature), bf16)] * 2, "combine", 400_000_000, count=7
-    )(target, *returned(hidden, 1), *returned(pre_grad, 0), mixed, gate_rows)
+    )(target, back_out, got_out, back_in, exchanged(back_in), mixed, gate_rows)
     grad_up, grad_down = vmem_call(
         functools.partial(gradients_kernel, 1.0 / lax.axis_size("rep")),
         [(w_up.shape, f32)] * 2,

time: 184 us -> 174 us (0.946)
  the two profiles are of different devices: /device:TPU:6 before, /device:TPU:1 now
where the time goes in v6:
time: 174 us; the launch traced here: 173 us
  starting transfers between devices  51.1 us (29%)
  waiting for transfers between devices  50.9 us (29%)
  blocking collectives  21.3 us (12%)
  Pallas kernels  20.6 us (12%)
  between operations  14.3 us (8%)
  local copies, waits for them, and re-layouts  12.9 us (7%)
  other arithmetic  1.96 us (1%)
    ppermute x4, waiting for transfers between devices, exchange(): return lax.ppermute(rows, ('rep', 'exp'), swap)  32 us
    ppermute x4, starting transfers between devices, exchange(): return lax.ppermute(rows, ('rep', 'exp'), swap)  24.7 us
    all_to_all x1, blocking collectives, dispatch(): return lax.all_to_all(blocks, 'exp', 0, 0, tiled=True).reshape(-1, feature)  21.3 us
    all_to_all x3, waiting for transfers between devices, dispatch(): return lax.all_to_all(blocks, 'exp', 0, 0, tiled=True).reshape(-1, feature)  18.9 us
    all_to_all x3, starting transfers between devices, dispatch(): return lax.all_to_all(blocks, 'exp', 0, 0, tiled=True).reshape(-1, feature)  15.6 us
    unnamed x26, local copies, waits for them, and re-layouts  10.4 us
    pallas_call x1, Pallas kernels, middle(): pl.pallas_call(middle_kernel, grid=(CHUNKS,), in_specs=[pl.BlockSpec((ste...  7.89 us
    ppermute x1, starting transfers between devices, per_device(): low = lax.ppermute(tokens[tile_rows - margin:], 'rep', forward)  5 us
  transfers between devices with their start and end apart: 13, of which 5 were waited for; matrix products, arithmetic and copies ran while one was open for 2% of the time, Pallas kernels for 7%

profile of v6, /device:TPU:1, one launch (start us, length us, event | category | flops | bytes accessed | tf_op | source)
XLA Modules:
  0.0 173.2 jit_solution(13963522194654651117)
XLA Ops:
  7.2 0.0 copy-start.6
  7.2 0.0 all-gather.3.cloned.1.call-start
  7.2 1.7 pad_maximum_fusion
  9.0 0.0 all-gather.3.cloned.1.call-update
  9.0 0.9 fusion.1
  9.9 1.3 collective-permute-start.2
  11.2 5.0 %collective-permute-start.1 = (bf16[4,16,512]{2,1,0:T(8,128)(2,1)S(1)}, bf16[4,16,512]{2,1,0:T(8,128)(2,1)S(1)}, u32[]{:S(2)}, u32[]{:S(2)}) collective-permute-start(bf16[4,16,512]{2,1,0:T(8,128)(2,1)S(1)} %get-tuple-element.29), channel_id=1, source_target_pairs={{0,32},{32,64},{64,96},{96,128},{128,160},{160,192},{192,224},{224... | collective-permute-start | bytes 196616 | tf_op jit(solution)/shard_map/ppermute | solution.py:385
  16.2 0.8 reshape.81.gate_ref
  17.0 0.0 copy-start.5
  17.0 0.9 copy-done.5
  17.9 0.7 copy-done.8
  18.6 0.1 upstream.1.give_ref
  18.7 9.6 %collective-permute-start = (bf16[272,512]{1,0:T(8,128)(2,1)S(1)}, bf16[272,512]{1,0:T(8,128)(2,1)S(1)}, u32[]{:S(2)}, u32[]{:S(2)}) collective-permute-start(bf16[272,512]{1,0:T(8,128)(2,1)S(1)} %upstream.1.give_ref), channel_id=1, source_target_pairs={{0,32},{1,481},{2,34},{3,483},{4,36},{5,485},{6,38},{7,487},{8,40}... | collective-permute-start | bytes 835592 | tf_op jit(solution)/shard_map/ppermute | solution.py:371
  28.3 0.0 copy-done.6
  28.3 0.1 fusion
  28.4 0.0 collective-permute-done.2
  28.4 0.0 collective-permute-done.1
  28.5 0.1 pad_maximum_fusion.2
  28.6 0.1 pad_maximum_fusion.1
  28.7 0.7 reshape.68
  29.3 2.0 %collective-permute-start.3 = (bf16[96,512]{1,0:T(8,128)(2,1)}, bf16[96,512]{1,0:T(8,128)(2,1)S(1)}, u32[]{:S(2)}, u32[]{:S(2)}) collective-permute-start(bf16[96,512]{1,0:T(8,128)(2,1)} %reshape.68), channel_id=1, source_target_pairs={{0,1},{1,2},{2,3},{3,4},{4,5},{5,6},{6,7},{7,8},{8,9},{9,10},{10,1... | collective-permute-start | bytes 294920 | tf_op jit(solution)/shard_map/ppermute | solution.py:398
  31.4 2.4 %collective-permute-start.4 = (bf16[96,512]{1,0:T(8,128)(2,1)S(1)}, bf16[96,512]{1,0:T(8,128)(2,1)S(1)}, u32[]{:S(2)}, u32[]{:S(2)}) collective-permute-start(bf16[96,512]{1,0:T(8,128)(2,1)S(1)} %reshape.69), channel_id=1, source_target_pairs={{1,0},{2,1},{3,2},{4,3},{5,4},{6,5},{7,6},{8,7},{9,8},{10,9},{11,1... | collective-permute-start | bytes 294920 | tf_op jit(solution)/shard_map/ppermute | solution.py:399
  33.8 0.0 collective-permute-done.got_ref
  33.8 0.0 copy-start.11
  33.8 0.7 copy-done.11
  34.5 1.0 copy-done.12
  35.5 1.6 grad_slots.1
  37.1 7.3 %all-to-all-start.1 = ((bf16[32,24,512]{2,1,0:T(8,128)(2,1)}), bf16[32,24,512]{2,1,0:T(8,128)(2,1)}, u32[]{:S(2)}, u32[]{:S(2)}) async-start(bf16[32,24,512]{2,1,0:T(8,128)(2,1)} %bitcast.10), calls=%async_computation.1 | async-start | bytes 1572864 | tf_op jit(solution)/shard_map/all_to_all | solution.py:375
  44.4 0.0 reduce-scatter.2.cloned.1.call-start
  44.4 0.1 pad_add_fusion.at_ref
  44.5 0.0 collective-permute-done.3.left_ref
  44.5 0.0 collective-permute-done.4.right_ref
  44.5 0.0 copy-done.9
  44.5 0.0 copy-done.10
  44.6 4.4 %front.1.mixed_ref = bf16[256,512]{1,0:T(8,128)(2,1)S(1)} custom-call(s32[4]{0:T(128)S(1)} %pad_add_fusion.at_ref, bf16[256,512]{1,0:T(8,128)(2,1)S(1)} %bitcast.29, bf16[64,512]{1,0:T(8,128)(2,1)S(1)} %bitcast.31, bf16[64,512]{1,0:T(8,128)(2,1)S(1)} %bitcast.30, bf16[96,512]{1,0:T(8,128)(2,1)S(1)} %collective-permute-done.3.left_ref, ...), custom_call_target="tpu_custom_call" | custom-call | flops 4000000000 | bytes 3000000 | tf_op jit(solution)/shard_map/front/pallas_call | solution.py:329
  49.0 7.0 %collective-permute-start.5 = (bf16[256,512]{1,0:T(8,128)(2,1)S(1)}, bf16[256,512]{1,0:T(8,128)(2,1)S(1)}, u32[]{:S(2)}, u32[]{:S(2)}) collective-permute-start(bf16[256,512]{1,0:T(8,128)(2,1)S(1)} %front.1.mixed_ref), channel_id=1, source_target_pairs={{0,32},{1,481},{2,34},{3,483},{4,36},{5,485},{6,38},{7,487},{8,40}... | collective-permute-start | bytes 786440 | tf_op jit(solution)/shard_map/ppermute | solution.py:371
  56.0 15.5 %collective-permute-done.5.got_ref = bf16[256,512]{1,0:T(8,128)(2,1)S(1)} collective-permute-done((bf16[256,512]{1,0:T(8,128)(2,1)S(1)}, bf16[256,512]{1,0:T(8,128)(2,1)S(1)}, u32[]{:S(2)}, u32[]{:S(2)}) %collective-permute-start.5) | collective-permute-done | bytes 262176 | tf_op jit(solution)/shard_map/ppermute | solution.py:371
  71.5 0.6 token_slots.1
  72.1 0.0 all-to-all-done.1
  72.1 21.3 %all_to_all.20 = bf16[32,24,512]{2,1,0:T(8,128)(2,1)} all-to-all(bf16[32,24,512]{2,1,0:T(8,128)(2,1)S(1)} %bitcast.27), channel_id=1, replica_groups=mesh['rep'=16,'exp'=32] {'exp'}, dimensions={0} | all-to-all | bytes 1572864 | tf_op jit(solution)/shard_map/all_to_all | solution.py:375
  93.5 7.9 %middle.1 = (bf16[8,256,512]{2,1,0:T(8,128)(2,1)}, bf16[1024,768]{1,0:T(8,128)(2,1)}, bf16[1024,768]{1,0:T(8,128)(2,1)}) custom-call(bf16[8,2,128,512]{3,2,1,0:T(8,128)(2,1)} %bitcast.18, bf16[768,512]{1,0:T(8,128)(2,1)} %bitcast.33, bf16[768,512]{1,0:T(8,128)(2,1)} %bitcast.11.g_ref), custom_call_target="tpu_custom_call" | custom-call | flops 3221225472 | bytes 7340032 | tf_op jit(solution)/shard_map/middle/pallas_call | solution.py:155
  101.3 0.0 reduce-scatter.2.cloned.1.call-update
  101.4 1.6 copy-done
  102.9 1.4 copy-done.4
  104.3 1.5 back.2
  105.9 0.0 copy-start.2
  105.9 0.9 copy-done.2
  106.8 4.1 %all-to-all-start.2 = ((bf16[32,24,512]{2,1,0:T(8,128)(2,1)}), bf16[32,24,512]{2,1,0:T(8,128)(2,1)S(1)}, u32[]{:S(2)}, u32[]{:S(2)}) async-start(bf16[32,24,512]{2,1,0:T(8,128)(2,1)} %bitcast.26), calls=%async_computation.2 | async-start | bytes 1572864 | tf_op jit(solution)/shard_map/all_to_all | solution.py:375
  110.9 0.0 copy-start.3
  110.9 1.4 copy-done.3
  112.4 1.5 back.3
  113.9 0.9 copy-done.1
  114.8 10.4 %all-to-all-done.2 = bf16[32,24,512]{2,1,0:T(8,128)(2,1)S(1)} async-done(((bf16[32,24,512]{2,1,0:T(8,128)(2,1)}), bf16[32,24,512]{2,1,0:T(8,128)(2,1)S(1)}, u32[]{:S(2)}, u32[]{:S(2)}) %all-to-all-start.2) | async-done | bytes 786464 | tf_op jit(solution)/shard_map/all_to_all | solution.py:375
  125.3 4.1 %all-to-all-start.3 = ((bf16[32,24,512]{2,1,0:T(8,128)(2,1)}), bf16[32,24,512]{2,1,0:T(8,128)(2,1)S(1)}, u32[]{:S(2)}, u32[]{:S(2)}) async-start(bf16[32,24,512]{2,1,0:T(8,128)(2,1)} %bitcast.25), calls=%async_computation.3 | async-start | bytes 1572864 | tf_op jit(solution)/shard_map/all_to_all | solution.py:375
  129.4 0.4 back_rows.2
  129.8 5.5 %collective-permute-start.6 = (bf16[256,512]{1,0:T(8,128)(2,1)S(1)}, bf16[256,512]{1,0:T(8,128)(2,1)S(1)}, u32[]{:S(2)}, u32[]{:S(2)}) collective-permute-start(bf16[256,512]{1,0:T(8,128)(2,1)S(1)} %back_rows.2), channel_id=1, source_target_pairs={{0,32},{1,481},{2,34},{3,483},{4,36},{5,485},{6,38},{7,487},{8,40}... | collective-permute-start | bytes 786440 | tf_op jit(solution)/shard_map/ppermute | solution.py:371
  135.3 8.4 %all-to-all-done.3 = bf16[32,24,512]{2,1,0:T(8,128)(2,1)S(1)} async-done(((bf16[32,24,512]{2,1,0:T(8,128)(2,1)}), bf16[32,24,512]{2,1,0:T(8,128)(2,1)S(1)}, u32[]{:S(2)}, u32[]{:S(2)}) %all-to-all-start.3) | async-done | bytes 786464 | tf_op jit(solution)/shard_map/all_to_all | solution.py:375
  143.7 4.7 %collective-permute-done.6.got_out_ref = bf16[256,512]{1,0:T(8,128)(2,1)S(1)} collective-permute-done((bf16[256,512]{1,0:T(8,128)(2,1)S(1)}, bf16[256,512]{1,0:T(8,128)(2,1)S(1)}, u32[]{:S(2)}, u32[]{:S(2)}) %collective-permute-start.6) | collective-permute-done | bytes 262176 | tf_op jit(solution)/shard_map/ppermute | solution.py:371
  148.5 0.4 back_rows.3
  148.9 2.6 %collective-permute-start.7 = (bf16[256,512]{1,0:T(8,128)(2,1)S(1)}, bf16[256,512]{1,0:T(8,128)(2,1)S(1)}, u32[]{:S(2)}, u32[]{:S(2)}) collective-permute-start(bf16[256,512]{1,0:T(8,128)(2,1)S(1)} %back_rows.3), channel_id=1, source_target_pairs={{0,32},{1,481},{2,34},{3,483},{4,36},{5,485},{6,38},{7,487},{8,40}... | collective-permute-start | bytes 786440 | tf_op jit(solution)/shard_map/ppermute | solution.py:371
  151.5 11.7 %collective-permute-done.7.got_in_ref = bf16[256,512]{1,0:T(8,128)(2,1)S(1)} collective-permute-done((bf16[256,512]{1,0:T(8,128)(2,1)S(1)}, bf16[256,512]{1,0:T(8,128)(2,1)S(1)}, u32[]{:S(2)}, u32[]{:S(2)}) %collective-permute-start.7) | collective-permute-done | bytes 262176 | tf_op jit(solution)/shard_map/ppermute | solution.py:371
  163.2 1.3 combine.1
  164.6 0.9 copy-done.7
  165.5 0.8 gradients.1
  (13 shorter events, 0.1 us)
Async XLA Ops:
  7.2 21.2 %copy-start.6 = (bf16[16,16,512]{2,1,0:T(8,128)(2,1)S(1)}, bf16[16,16,512]{2,1,0:T(8,128)(2,1)}, u32[]{:S(2)}) copy-start(bf16[16,16,512]{2,1,0:T(8,128)(2,1)} %param.8) | copy-start | bytes 786436
  7.2 86.3 %all-gather.3.cloned.1.call-start = ((), (), s32[]{:S(2)}) async-start(), calls=%async_computation.6 | async-start | bytes 2359296 | tf_op jit(solution)/shard_map/all_gather | solution.py:377
  9.9 18.5 %collective-permute-start.2 = (bf16[4,16,512]{2,1,0:T(8,128)(2,1)S(1)}, bf16[4,16,512]{2,1,0:T(8,128)(2,1)S(1)}, u32[]{:S(2)}, u32[]{:S(2)}) collective-permute-start(bf16[4,16,512]{2,1,0:T(8,128)(2,1)S(1)} %get-tuple-element.28), channel_id=1, source_target_pairs={{32,0},{64,32},{96,64},{128,96},{160,128},{192,160},{224,192},{256... | collective-permute-start | bytes 196616 | tf_op jit(solution)/shard_map/ppermute | solution.py:386
  11.2 17.3 %collective-permute-start.1 = (bf16[4,16,512]{2,1,0:T(8,128)(2,1)S(1)}, bf16[4,16,512]{2,1,0:T(8,128)(2,1)S(1)}, u32[]{:S(2)}, u32[]{:S(2)}) collective-permute-start(bf16[4,16,512]{2,1,0:T(8,128)(2,1)S(1)} %get-tuple-element.29), channel_id=1, source_target_pairs={{0,32},{32,64},{64,96},{96,128},{128,160},{160,192},{192,224},{224... | collective-permute-start | bytes 196616 | tf_op jit(solution)/shard_map/ppermute | solution.py:385
  17.0 1.0 copy-start.5
  17.9 0.7 copy-start.8
  18.7 15.1 %collective-permute-start = (bf16[272,512]{1,0:T(8,128)(2,1)S(1)}, bf16[272,512]{1,0:T(8,128)(2,1)S(1)}, u32[]{:S(2)}, u32[]{:S(2)}) collective-permute-start(bf16[272,512]{1,0:T(8,128)(2,1)S(1)} %upstream.1.give_ref), channel_id=1, source_target_pairs={{0,32},{1,481},{2,34},{3,483},{4,36},{5,485},{6,38},{7,487},{8,40}... | collective-permute-start | bytes 835592 | tf_op jit(solution)/shard_map/ppermute | solution.py:371
  29.3 15.2 %copy-start.9 = (bf16[512,1536]{1,0:T(8,128)(2,1)S(1)}, bf16[512,1536]{1,0:T(8,128)(2,1)}, u32[]{:S(2)}) copy-start(bf16[512,1536]{1,0:T(8,128)(2,1)} %wqkv_ref.1) | copy-start | bytes 4718596
  29.3 15.2 %copy-start.10 = (bf16[512,512]{1,0:T(8,128)(2,1)S(1)}, bf16[512,512]{1,0:T(8,128)(2,1)}, u32[]{:S(2)}) copy-start(bf16[512,512]{1,0:T(8,128)(2,1)} %wproj_ref.1) | copy-start | bytes 1572868
  29.3 15.2 %collective-permute-start.3 = (bf16[96,512]{1,0:T(8,128)(2,1)}, bf16[96,512]{1,0:T(8,128)(2,1)S(1)}, u32[]{:S(2)}, u32[]{:S(2)}) collective-permute-start(bf16[96,512]{1,0:T(8,128)(2,1)} %reshape.68), channel_id=1, source_target_pairs={{0,1},{1,2},{2,3},{3,4},{4,5},{5,6},{6,7},{7,8},{8,9},{9,10},{10,1... | collective-permute-start | bytes 294920 | tf_op jit(solution)/shard_map/ppermute | solution.py:398
  31.4 13.2 %collective-permute-start.4 = (bf16[96,512]{1,0:T(8,128)(2,1)S(1)}, bf16[96,512]{1,0:T(8,128)(2,1)S(1)}, u32[]{:S(2)}, u32[]{:S(2)}) collective-permute-start(bf16[96,512]{1,0:T(8,128)(2,1)S(1)} %reshape.69), channel_id=1, source_target_pairs={{1,0},{2,1},{3,2},{4,3},{5,4},{6,5},{7,6},{8,7},{9,8},{10,9},{11,1... | collective-permute-start | bytes 294920 | tf_op jit(solution)/shard_map/ppermute | solution.py:399
  33.8 0.7 copy-start.11
  34.5 1.0 copy-start.12
  37.1 35.0 %all-to-all-start.1 = ((bf16[32,24,512]{2,1,0:T(8,128)(2,1)}), bf16[32,24,512]{2,1,0:T(8,128)(2,1)}, u32[]{:S(2)}, u32[]{:S(2)}) async-start(bf16[32,24,512]{2,1,0:T(8,128)(2,1)} %bitcast.10), calls=%async_computation.1 | async-start | bytes 1572864 | tf_op jit(solution)/shard_map/all_to_all | solution.py:375
  44.4 120.2 %reduce-scatter.2.cloned.1.call-start = ((), (), s32[]{:S(2)}) async-start(), calls=%async_computation.5 | async-start | bytes 2359296 | tf_op jit(solution)/shard_map/reduce_scatter | solution.py:432
  49.0 22.6 %collective-permute-start.5 = (bf16[256,512]{1,0:T(8,128)(2,1)S(1)}, bf16[256,512]{1,0:T(8,128)(2,1)S(1)}, u32[]{:S(2)}, u32[]{:S(2)}) collective-permute-start(bf16[256,512]{1,0:T(8,128)(2,1)S(1)} %front.1.mixed_ref), channel_id=1, source_target_pairs={{0,32},{1,481},{2,34},{3,483},{4,36},{5,485},{6,38},{7,487},{8,40}... | collective-permute-start | bytes 786440 | tf_op jit(solution)/shard_map/ppermute | solution.py:371
  101.3 1.6 copy-start
  102.9 1.4 copy-start.4
  105.9 0.9 copy-start.2
  106.8 18.5 %all-to-all-start.2 = ((bf16[32,24,512]{2,1,0:T(8,128)(2,1)}), bf16[32,24,512]{2,1,0:T(8,128)(2,1)S(1)}, u32[]{:S(2)}, u32[]{:S(2)}) async-start(bf16[32,24,512]{2,1,0:T(8,128)(2,1)} %bitcast.26), calls=%async_computation.2 | async-start | bytes 1572864 | tf_op jit(solution)/shard_map/all_to_all | solution.py:375
  110.9 1.4 copy-start.3
  113.9 0.9 copy-start.1
  125.3 18.5 %all-to-all-start.3 = ((bf16[32,24,512]{2,1,0:T(8,128)(2,1)}), bf16[32,24,512]{2,1,0:T(8,128)(2,1)S(1)}, u32[]{:S(2)}, u32[]{:S(2)}) async-start(bf16[32,24,512]{2,1,0:T(8,128)(2,1)} %bitcast.25), calls=%async_computation.3 | async-start | bytes 1572864 | tf_op jit(solution)/shard_map/all_to_all | solution.py:375
  129.8 18.7 %collective-permute-start.6 = (bf16[256,512]{1,0:T(8,128)(2,1)S(1)}, bf16[256,512]{1,0:T(8,128)(2,1)S(1)}, u32[]{:S(2)}, u32[]{:S(2)}) collective-permute-start(bf16[256,512]{1,0:T(8,128)(2,1)S(1)} %back_rows.2), channel_id=1, source_target_pairs={{0,32},{1,481},{2,34},{3,483},{4,36},{5,485},{6,38},{7,487},{8,40}... | collective-permute-start | bytes 786440 | tf_op jit(solution)/shard_map/ppermute | solution.py:371
  148.9 14.3 %collective-permute-start.7 = (bf16[256,512]{1,0:T(8,128)(2,1)S(1)}, bf16[256,512]{1,0:T(8,128)(2,1)S(1)}, u32[]{:S(2)}, u32[]{:S(2)}) collective-permute-start(bf16[256,512]{1,0:T(8,128)(2,1)S(1)} %back_rows.3), channel_id=1, source_target_pairs={{0,32},{1,481},{2,34},{3,483},{4,36},{5,485},{6,38},{7,487},{8,40}... | collective-permute-start | bytes 786440 | tf_op jit(solution)/shard_map/ppermute | solution.py:371
  164.6 1.0 copy-start.7
Sparse Core Ops, SparseCore 0:
  10.7 70.6 all-gather.2
  101.5 60.2 reduce-scatter.1

commit v7 on v6

--- a/solution.py
+++ b/solution.py
@@ -75,40 +75,86 @@
     return one_hot(lax.broadcasted_iota(jnp.int32, (rows, target.shape[1]), 0) == target)
 
 
-def grad_slots_kernel(experts, capacity, give_ref, got_ref, slots_ref, target_ref):
-    feature = give_ref.shape[1]
-    count = give_ref.shape[0] - EXTRA
-    total = None
-    for n, ref in enumerate((give_ref, got_ref)):
-        route = ref[count:, :count].astype(jnp.float32)[:1].astype(jnp.int32)
-        target = route * (2 * capacity) + n * capacity + slot_numbers(route, experts)
-        target_ref[n : n + 1] = target
-        placed = nn(placer(target, 2 * experts * capacity), ref[:count])
-        total = placed if total is None else total + placed
-    slots_ref[...] = total.astype(jnp.bfloat16)
-
-
-def token_slots_kernel(target_ref, mixed_ref, got_ref, slots_ref):
+def slots_kernel(experts, capacity, give_ref, mixed_ref, slots_ref, target_ref):
+    count = mixed_ref.shape[0]
+    route = give_ref[count:, :count].astype(jnp.float32)[:1].astype(jnp.int32)
+    target = route * (2 * capacity) + slot_numbers(route, experts)
+    target_ref[...] = target
     rows = slots_ref.shape[0]
-    total = nn(placer(target_ref[0:1], rows), mixed_ref[...])
-    total = total + nn(placer(target_ref[1:2], rows), got_ref[...])
-    slots_ref[...] = total.astype(jnp.bfloat16)
-
-
-def back_rows_kernel(target_ref, back_ref, give_ref):
-    give_ref[...] = tn(placer(target_ref[1:2], back_ref.shape[0]), back_ref[...]).astype(
-        jnp.bfloat16
-    )
-
-
-def combine_kernel(
-    target_ref, out_ref, got_out_ref, in_ref, got_in_ref, mixed_ref, gate_ref, layer_ref, grad_ref
-):
+    slots = nn(placer(target, rows), mixed_ref[...])
+    slots = slots + nn(placer(target + capacity, rows), give_ref[:count])
+    slots_ref[...] = slots.astype(jnp.bfloat16)
+
+
+def first_rows(slots, capacity):
+    column = lax.broadcasted_iota(jnp.int32, (1, slots), 1)
+    expert = ((column.astype(jnp.float32) + 0.5) * (1.0 / capacity)).astype(jnp.int32)
+    return column + capacity * expert
+
+
+def unpack_kernel(capacity, sent_ref, x_ref, g_ref):
+    sent = sent_ref[...]
+    first = first_rows(x_ref.shape[0], capacity)
+    x_ref[...] = tn(placer(first, sent.shape[0]), sent).astype(jnp.bfloat16)
+    g_ref[...] = tn(placer(first + capacity, sent.shape[0]), sent).astype(jnp.bfloat16)
+
+
+def unpack(sent, capacity):
+    rows, feature = sent.shape
+    half = pl.BlockSpec((rows // 2, feature), lambda i: (0, 0))
+    return pl.pallas_call(
+        functools.partial(unpack_kernel, capacity),
+        grid=(1,),
+        in_specs=[pl.BlockSpec((rows, feature), lambda i: (0, 0))],
+        out_specs=[half] * 2,
+        out_shape=[pltpu.HBM((rows // 2, feature), jnp.bfloat16)] * 2,
+        compiler_params=pltpu.CompilerParams(vmem_limit_bytes=VMEM_LIMIT),
+        cost_estimate=pl.CostEstimate(
+            flops=600_000_000, bytes_accessed=1_600_000, transcendentals=0
+        ),
+        name="unpack",
+    )(sent)
+
+
+def interleave_kernel(capacity, out_ref, in_ref, both_ref):
+    rows = both_ref.shape[0]
+    first = first_rows(out_ref.shape[0], capacity)
+    both = nn(placer(first, rows), out_ref[...]) + nn(placer(first + capacity, rows), in_ref[...])
+    both_ref[...] = both.astype(jnp.bfloat16)
+
+
+def interleave(outs, ins, half, capacity):
+    rows, feature = outs.shape
+    block = pl.BlockSpec((rows // 2, feature), lambda i: (half, 0))
+    return pl.pallas_call(
+        functools.partial(interleave_kernel, capacity),
+        grid=(1,),
+        in_specs=[block] * 2,
+        out_specs=pl.BlockSpec((rows, feature), lambda i: (0, 0)),
+        out_shape=jax.ShapeDtypeStruct((rows, feature), jnp.bfloat16),
+        compiler_params=pltpu.CompilerParams(vmem_limit_bytes=MIDDLE_LIMIT),
+        cost_estimate=pl.CostEstimate(
+            flops=600_000_000, bytes_accessed=1_600_000, transcendentals=0
+        ),
+        name="interleave",
+    )(outs, ins)
+
+
+def back_rows_kernel(capacity, target_ref, back_ref, give_ref):
+    count, rows = target_ref.shape[1], back_ref.shape[0]
+    target = target_ref[...]
+    give_ref[:count] = tn(placer(target, rows), back_ref[...]).astype(jnp.bfloat16)
+    give_ref[count:] = tn(placer(target + capacity, rows), back_ref[...]).astype(jnp.bfloat16)
+
+
+def combine_kernel(capacity, target_ref, back_ref, got_ref, mixed_ref, gate_ref, layer_ref, grad_ref):
     f32, bf16 = jnp.float32, jnp.bfloat16
-    mine = placer(target_ref[0:1], out_ref.shape[0])
-    token_out = tn(mine, out_ref[...]) + got_out_ref[...].astype(f32)
+    count, rows = target_ref.shape[1], back_ref.shape[0]
+    target = target_ref[...]
+    token_out = tn(placer(target, rows), back_ref[...]) + got_ref[:count].astype(f32)
     layer_ref[...] = (mixed_ref[...].astype(f32) + gate_ref[...] * token_out).astype(bf16)
-    grad_ref[...] = (tn(mine, in_ref[...]) + got_in_ref[...].astype(f32)).astype(bf16)
+    token_grad = tn(placer(target + capacity, rows), back_ref[...]) + got_ref[count:].astype(f32)
+    grad_ref[...] = token_grad.astype(bf16)
 
 
 def gradients_kernel(scale, sum_ref, up_ref, down_ref):
@@ -117,17 +163,33 @@
     down_ref[0] = sum_ref[0, width:].astype(jnp.float32) * scale
 
 
-def middle_kernel(w_ref, x_ref, g_ref, grads_ref, hid_ref, pg_ref):
+def gradients(summed, scale):
+    _, rows, feature = summed.shape
+    width = rows // 2
+    block = pl.BlockSpec((1, width, feature), lambda i: (0, 0, 0))
+    return pl.pallas_call(
+        functools.partial(gradients_kernel, scale),
+        grid=(1,),
+        in_specs=[pl.BlockSpec((1, rows, feature), lambda i: (0, 0, 0))],
+        out_specs=[block] * 2,
+        out_shape=[jax.ShapeDtypeStruct((1, width, feature), jnp.float32)] * 2,
+        compiler_params=pltpu.CompilerParams(vmem_limit_bytes=MIDDLE_LIMIT),
+        cost_estimate=pl.CostEstimate(flops=1_000_000, bytes_accessed=800_000, transcendentals=0),
+        name="gradients",
+    )(summed)
+
+
+def middle_kernel(w_ref, *refs):
+    slots, (grads_ref, hid_ref, pg_ref) = refs[:-3], refs[-3:]
     shards, _, width, feature = w_ref.shape
     up = w_ref[:, 0].reshape(shards * width, feature)
     down = w_ref[:, 1].reshape(shards * width, feature)
-    halves = 2
-    rows = x_ref.shape[0] // halves
-    parts = [slice(n * rows, (n + 1) * rows) for n in range(halves)]
-    pres = [nt(up, x_ref[part]) for part in parts]
-    backs = [nt(down, g_ref[part]) for part in parts]
+    rows = slots[0].shape[0]
+    halves = len(slots) // 2
+    pres = [nt(up, slots[2 * n][...]) for n in range(halves)]
+    backs = [nt(down, slots[2 * n + 1][...]) for n in range(halves)]
     grad_up = grad_down = None
-    for n, part in enumerate(parts):
+    for n in range(halves):
         pre = pres[n]
         square = pre * pre
         inner = jnp.tanh(pre * (GELU_C + (GELU_C * 0.044715) * square))
@@ -137,47 +199,45 @@
             GELU_C + (3.0 * 0.044715 * GELU_C) * square
         )
         pre_grad = (backs[n] * slope).astype(jnp.bfloat16)
-        hid_ref[:, part] = hidden
-        pg_ref[:, part] = pre_grad
-        by_up = nn(pre_grad, x_ref[part])
-        by_down = nn(hidden, g_ref[part])
+        hid_ref[:, n * rows : (n + 1) * rows] = hidden
+        pg_ref[:, n * rows : (n + 1) * rows] = pre_grad
+        by_up = nn(pre_grad, slots[2 * n][...])
+        by_down = nn(hidden, slots[2 * n + 1][...])
         grad_up = by_up if grad_up is None else grad_up + by_up
         grad_down = by_down if grad_down is None else grad_down + by_down
     grads_ref[:, :width] = grad_up.astype(jnp.bfloat16).reshape(shards, width, feature)
     grads_ref[:, width:] = grad_down.astype(jnp.bfloat16).reshape(shards, width, feature)
 
 
-def middle(weights, slot_x, slot_g):
+def middle(weights, slots):
     owners, _, width, feature = weights.shape
-    rows = slot_x.shape[0]
+    rows = slots[0].shape[0]
     step = owners // CHUNKS
     ff = owners * width
+    total = rows * len(slots) // 2
     return pl.pallas_call(
         middle_kernel,
         grid=(CHUNKS,),
-        in_specs=[
-            pl.BlockSpec((step, 2, width, feature), lambda i: (i, 0, 0, 0)),
-            pl.BlockSpec((rows, feature), lambda i: (0, 0)),
-            pl.BlockSpec((rows, feature), lambda i: (0, 0)),
-        ],
+        in_specs=[pl.BlockSpec((step, 2, width, feature), lambda i: (i, 0, 0, 0))]
+        + [pl.BlockSpec((rows, feature), lambda i: (0, 0))] * len(slots),
         out_specs=[
             pl.BlockSpec((step, 2 * width, feature), lambda i: (i, 0, 0)),
-            pl.BlockSpec((step * width, rows), lambda i: (i, 0)),
-            pl.BlockSpec((step * width, rows), lambda i: (i, 0)),
+            pl.BlockSpec((step * width, total), lambda i: (i, 0)),
+            pl.BlockSpec((step * width, total), lambda i: (i, 0)),
         ],
         out_shape=[
             pltpu.HBM((owners, 2 * width, feature), jnp.bfloat16),
-            pltpu.HBM((ff, rows), jnp.bfloat16),
-            pltpu.HBM((ff, rows), jnp.bfloat16),
+            pltpu.HBM((ff, total), jnp.bfloat16),
+            pltpu.HBM((ff, total), jnp.bfloat16),
         ],
         compiler_params=pltpu.CompilerParams(vmem_limit_bytes=MIDDLE_LIMIT),
         cost_estimate=pl.CostEstimate(
-            flops=8 * rows * ff * feature,
-            bytes_accessed=8 * ff * feature + 4 * ff * rows,
-            transcendentals=ff * rows,
+            flops=8 * total * ff * feature,
+            bytes_accessed=8 * ff * feature + 4 * ff * total,
+            transcendentals=ff * total,
         ),
         name="middle",
-    )(weights, slot_x, slot_g)
+    )(weights, *slots)
 
 
 def back_kernel(side, w_ref, act_ref, out_ref, acc):
@@ -210,7 +270,7 @@
         out_specs=pl.BlockSpec((rows, feature), lambda i: (0, 0)),
         out_shape=jax.ShapeDtypeStruct((rows, feature), jnp.bfloat16),
         scratch_shapes=[pltpu.VMEM((rows, feature), jnp.float32)],
-        compiler_params=pltpu.CompilerParams(vmem_limit_bytes=VMEM_LIMIT),
+        compiler_params=pltpu.CompilerParams(vmem_limit_bytes=MIDDLE_LIMIT),
         cost_estimate=pl.CostEstimate(
             flops=2 * rows * ff * feature,
             bytes_accessed=2 * ff * feature + 2 * ff * rows,
@@ -397,6 +457,7 @@
 
     left = lax.ppermute(strip(slice(tile_cols - margin, tile_cols)), "exp", forward)
     right = lax.ppermute(strip(slice(0, margin)), "exp", backward)
+    left, got = lax.optimization_barrier((left, got))
     at = jnp.stack(
         [
             lax.axis_index("rep"),
@@ -416,43 +477,43 @@
         w_proj,
     )
     got_mixed = exchange(mixed)
-    slots_g, target = vmem_call(
-        functools.partial(grad_slots_kernel, experts, capacity),
-        [rows_of, ((2, tok_count), jnp.int32)],
-        "grad_slots",
-        500_000_000,
-        count=2,
-    )(give, got)
-    slot_g = dispatch(slots_g)
-    [slots_x] = vmem_call(token_slots_kernel, [rows_of], "token_slots", 400_000_000, count=3)(
-        target, mixed, got_mixed
-    )
-    slot_x = dispatch(slots_x)
-    grads, hidden, pre_grad = middle(weights, slot_x, slot_g)
+
+    def dispatched(side, features):
+        slots, target = vmem_call(
+            functools.partial(slots_kernel, experts, capacity),
+            [rows_of, ((1, tok_count), jnp.int32)],
+            "slots",
+            500_000_000,
+            count=2,
+        )(side, features)
+        return unpack(dispatch(slots), capacity), target
+
+    own_parts, target = dispatched(give, mixed)
+    other_parts, other_target = dispatched(got, got_mixed)
+    grads, hidden, pre_grad = middle(weights, [*own_parts, *other_parts])
     summed = lax.psum_scatter(
         grads, "rep", scatter_dimension=0, tiled=True, axis_index_groups=groups
     )
 
-    def exchanged(rows):
-        [theirs] = vmem_call(
-            back_rows_kernel, [((tok_count, feature), bf16)], "back_rows", 200_000_000, count=2
-        )(target, rows)
-        return exchange(theirs)
-
-    back_out = dispatch(back(weights, hidden, 1))
-    back_in = dispatch(back(weights, pre_grad, 0))
-    got_out = exchanged(back_out)
-    back_in, got_out = lax.optimization_barrier((back_in, got_out))
+    outs, ins = back(weights, hidden, 1), back(weights, pre_grad, 0)
+    back_other = dispatch(interleave(outs, ins, 1, capacity))
+    [theirs] = vmem_call(
+        functools.partial(back_rows_kernel, capacity),
+        [((2 * tok_count, feature), bf16)],
+        "back_rows",
+        400_000_000,
+        count=2,
+    )(other_target, back_other)
+    outs, back_other = lax.optimization_barrier((outs, back_other))
+    back_own = dispatch(interleave(outs, ins, 0, capacity))
     layer_out, input_grad = vmem_call(
-        combine_kernel, [((tok_count, feature), bf16)] * 2, "combine", 400_000_000, count=7
-    )(target, back_out, got_out, back_in, exchanged(back_in), mixed, gate_rows)
-    grad_up, grad_down = vmem_call(
-        functools.partial(gradients_kernel, 1.0 / lax.axis_size("rep")),
-        [(w_up.shape, f32)] * 2,
-        "gradients",
-        1_000_000,
-        count=1,
-    )(summed)
+        functools.partial(combine_kernel, capacity),
+        [((tok_count, feature), bf16)] * 2,
+        "combine",
+        400_000_000,
+        count=5,
+    )(target, back_own, exchange(theirs), mixed, gate_rows)
+    grad_up, grad_down = gradients(summed, 1.0 / lax.axis_size("rep"))
     return (
         layer_out.reshape(tile_rows, tile_cols, feature),
         input_grad.reshape(tile_rows, tile_cols, feature),

time: 174 us -> 180 us (1.034)
  the two profiles are of different devices: /device:TPU:1 before, /device:TPU:6 now
where the time goes in v7:
time: 180 us; the launch traced here: 177 us
  starting transfers between devices  51.9 us (29%)
  waiting for transfers between devices  50.3 us (28%)
  Pallas kernels  36.9 us (20%)
  blocking collectives  18.5 us (10%)
  between operations  14.3 us (8%)
  local copies, waits for them, and re-layouts  3.47 us (2%)
  other arithmetic  1.99 us (1%)
    ppermute x3, waiting for transfers between devices, exchange(): return lax.ppermute(rows, ('rep', 'exp'), swap)  37.8 us
    all_to_all x3, starting transfers between devices, dispatch(): return lax.all_to_all(blocks, 'exp', 0, 0, tiled=True).reshape(-1, feature)  28.7 us
    all_to_all x1, blocking collectives, dispatch(): return lax.all_to_all(blocks, 'exp', 0, 0, tiled=True).reshape(-1, feature)  18.5 us
    all_to_all x3, waiting for transfers between devices, dispatch(): return lax.all_to_all(blocks, 'exp', 0, 0, tiled=True).reshape(-1, feature)  10.3 us
    pallas_call x1, Pallas kernels, middle(): pl.pallas_call(middle_kernel, grid=(CHUNKS,), in_specs=[pl.BlockSpec((ste...  7.87 us
    ppermute x3, starting transfers between devices, exchange(): return lax.ppermute(rows, ('rep', 'exp'), swap)  7.8 us
    pallas_call x2, Pallas kernels, back(): pl.pallas_call(functools.partial(back_kernel, side), grid=(steps,), in_sp...  7.36 us
    ppermute x1, starting transfers between devices, per_device(): lax.ppermute(strip(slice(tile_cols - margin, tile_cols)), 'exp', forward)  7.12 us
  transfers between devices with their start and end apart: 12, of which 5 were waited for; matrix products, arithmetic and copies ran while one was open for 1% of the time, Pallas kernels for 15%

profile of v7, /device:TPU:6, one launch (start us, length us, event | category | flops | bytes accessed | tf_op | source)
XLA Modules:
  0.0 177.3 jit_solution(9214179743039822636)
XLA Ops:
  7.2 0.0 copy-start.1
  7.2 0.0 copy-start.4
  7.2 0.0 all-gather.3.cloned.1.call-start
  7.2 1.8 pad_maximum_fusion
  9.0 0.0 all-gather.3.cloned.1.call-update
  9.0 0.9 fusion.1
  9.9 1.3 collective-permute-start.1
  11.2 4.5 %collective-permute-start = (bf16[4,16,512]{2,1,0:T(8,128)(2,1)S(1)}, bf16[4,16,512]{2,1,0:T(8,128)(2,1)S(1)}, u32[]{:S(2)}, u32[]{:S(2)}) collective-permute-start(bf16[4,16,512]{2,1,0:T(8,128)(2,1)S(1)} %get-tuple-element.43), channel_id=1, source_target_pairs={{0,32},{32,64},{64,96},{96,128},{128,160},{160,192},{192,224},{224... | collective-permute-start | bytes 196616 | tf_op jit(solution)/shard_map/ppermute | solution.py:445
  15.8 0.8 reshape.81.gate_ref
  16.6 0.0 copy-start
  16.6 0.9 copy-done
  17.5 0.0 copy-start.2
  17.5 0.7 copy-done.2
  18.2 0.0 copy-start.3
  18.2 0.1 upstream.1.give_ref
  18.3 4.0 %collective-permute-start.3 = (bf16[272,512]{1,0:T(8,128)(2,1)S(1)}, bf16[272,512]{1,0:T(8,128)(2,1)}, u32[]{:S(2)}, u32[]{:S(2)}) collective-permute-start(bf16[272,512]{1,0:T(8,128)(2,1)S(1)} %upstream.1.give_ref), channel_id=1, source_target_pairs={{0,32},{1,481},{2,34},{3,483},{4,36},{5,485},{6,38},{7,487},{8,40}... | collective-permute-start | bytes 835592 | tf_op jit(solution)/shard_map/ppermute | solution.py:431
  22.3 0.0 copy-done.1
  22.3 0.1 fusion
  22.4 0.0 collective-permute-done.1
  22.4 0.0 collective-permute-done
  22.4 0.1 pad_maximum_fusion.2
  22.5 0.1 pad_maximum_fusion.1
  22.7 7.1 %collective-permute-start.2 = (bf16[96,512]{1,0:T(8,128)(2,1)S(1)}, bf16[96,512]{1,0:T(8,128)(2,1)S(1)}, u32[]{:S(2)}, u32[]{:S(2)}) collective-permute-start(bf16[96,512]{1,0:T(8,128)(2,1)S(1)} %reshape.68), channel_id=1, source_target_pairs={{0,1},{1,2},{2,3},{3,4},{4,5},{5,6},{6,7},{7,8},{8,9},{9,10},{10,1... | collective-permute-start | bytes 294920 | tf_op jit(solution)/shard_map/ppermute | solution.py:458
  29.8 2.4 %collective-permute-start.4 = (bf16[96,512]{1,0:T(8,128)(2,1)S(1)}, bf16[96,512]{1,0:T(8,128)(2,1)S(1)}, u32[]{:S(2)}, u32[]{:S(2)}) collective-permute-start(bf16[96,512]{1,0:T(8,128)(2,1)S(1)} %reshape.69), channel_id=1, source_target_pairs={{1,0},{2,1},{3,2},{4,3},{5,4},{6,5},{7,6},{8,7},{9,8},{10,9},{11,1... | collective-permute-start | bytes 294920 | tf_op jit(solution)/shard_map/ppermute | solution.py:459
  32.1 0.1 pad_add_fusion.at_ref
  32.2 0.3 collective-permute-done.2.left_ref
  32.5 0.0 collective-permute-done.3.give_ref
  32.5 1.8 %collective-permute-done.4.right_ref = bf16[96,512]{1,0:T(8,128)(2,1)S(1)} collective-permute-done((bf16[96,512]{1,0:T(8,128)(2,1)S(1)}, bf16[96,512]{1,0:T(8,128)(2,1)S(1)}, u32[]{:S(2)}, u32[]{:S(2)}) %collective-permute-start.4) | collective-permute-done | bytes 98336 | tf_op jit(solution)/shard_map/ppermute | solution.py:459
  34.3 0.0 copy-done.4
  34.3 0.0 copy-done.3
  34.3 4.4 %front.1.mixed_ref = bf16[256,512]{1,0:T(8,128)(2,1)S(1)} custom-call(s32[4]{0:T(128)S(1)} %pad_add_fusion.at_ref, bf16[256,512]{1,0:T(8,128)(2,1)S(1)} %bitcast.23, bf16[64,512]{1,0:T(8,128)(2,1)S(1)} %bitcast.25, bf16[64,512]{1,0:T(8,128)(2,1)S(1)} %bitcast.24, bf16[96,512]{1,0:T(8,128)(2,1)S(1)} %collective-permute-done.2.left_ref, ...), custom_call_target="tpu_custom_call" | custom-call | flops 4000000000 | bytes 3000000 | tf_op jit(solution)/shard_map/front/pallas_call | solution.py:389
  38.7 1.7 slots.2
  40.4 10.8 %all-to-all-start = ((bf16[32,24,512]{2,1,0:T(8,128)(2,1)}), bf16[32,24,512]{2,1,0:T(8,128)(2,1)S(1)}, u32[]{:S(2)}, u32[]{:S(2)}) async-start(bf16[32,24,512]{2,1,0:T(8,128)(2,1)} %bitcast.8), calls=%async_computation | async-start | bytes 1572864 | tf_op jit(solution)/shard_map/all_to_all | solution.py:435
  51.2 1.9 %collective-permute-start.5 = (bf16[256,512]{1,0:T(8,128)(2,1)S(1)}, bf16[256,512]{1,0:T(8,128)(2,1)S(1)}, u32[]{:S(2)}, u32[]{:S(2)}) collective-permute-start(bf16[256,512]{1,0:T(8,128)(2,1)S(1)} %front.1.mixed_ref), channel_id=1, source_target_pairs={{0,32},{1,481},{2,34},{3,483},{4,36},{5,485},{6,38},{7,487},{8,40}... | collective-permute-start | bytes 786440 | tf_op jit(solution)/shard_map/ppermute | solution.py:431
  53.2 15.3 %collective-permute-done.5.mixed_ref = bf16[256,512]{1,0:T(8,128)(2,1)S(1)} collective-permute-done((bf16[256,512]{1,0:T(8,128)(2,1)S(1)}, bf16[256,512]{1,0:T(8,128)(2,1)S(1)}, u32[]{:S(2)}, u32[]{:S(2)}) %collective-permute-start.5) | collective-permute-done | bytes 262176 | tf_op jit(solution)/shard_map/ppermute | solution.py:431
  68.4 2.6 %slots.3 = (bf16[768,512]{1,0:T(8,128)(2,1)}, s32[1,256]{1,0:T(1,128)S(1)}) custom-call(bf16[272,512]{1,0:T(8,128)(2,1)} %collective-permute-done.3.give_ref, bf16[256,512]{1,0:T(8,128)(2,1)S(1)} %collective-permute-done.5.mixed_ref), custom_call_target="tpu_custom_call" | custom-call | flops 500000000 | bytes 3000000 | tf_op jit(solution)/shard_map/slots/pallas_call | solution.py:482
  71.0 0.0 all-to-all-done
  71.0 11.5 %all-to-all-start.1 = ((bf16[32,24,512]{2,1,0:T(8,128)(2,1)}), bf16[32,24,512]{2,1,0:T(8,128)(2,1)S(1)}, u32[]{:S(2)}, u32[]{:S(2)}) async-start(bf16[32,24,512]{2,1,0:T(8,128)(2,1)} %bitcast.10), calls=%async_computation.1 | async-start | bytes 1572864 | tf_op jit(solution)/shard_map/all_to_all | solution.py:435
  82.5 0.0 reduce-scatter.2.cloned.1.call-start
  82.6 1.6 unpack.2
  84.2 10.3 %all-to-all-done.1 = bf16[32,24,512]{2,1,0:T(8,128)(2,1)S(1)} async-done(((bf16[32,24,512]{2,1,0:T(8,128)(2,1)}), bf16[32,24,512]{2,1,0:T(8,128)(2,1)S(1)}, u32[]{:S(2)}, u32[]{:S(2)}) %all-to-all-start.1) | async-done | bytes 786464 | tf_op jit(solution)/shard_map/all_to_all | solution.py:435
  94.5 1.6 unpack.3
  96.1 0.0 all-gather.3.cloned.1.call-done
  96.1 7.9 %middle.1 = (bf16[8,256,512]{2,1,0:T(8,128)(2,1)}, bf16[1024,768]{1,0:T(8,128)(2,1)}, bf16[1024,768]{1,0:T(8,128)(2,1)}) custom-call(bf16[8,2,128,512]{3,2,1,0:T(8,128)(2,1)} %bitcast.27, bf16[384,512]{1,0:T(8,128)(2,1)} %get-tuple-element.25.refs_0_, bf16[384,512]{1,0:T(8,128)(2,1)} %get-tuple-element.26.refs_1_, ...), custom_call_target="tpu_custom_call" | custom-call | flops 3221225472 | bytes 7340032 | tf_op jit(solution)/shard_map/middle/pallas_call | solution.py:218
  104.0 0.0 reduce-scatter.2.cloned.1.call-update
  104.0 3.7 %back.2.out_ref = bf16[768,512]{1,0:T(8,128)(2,1)} custom-call(bf16[8,2,128,512]{3,2,1,0:T(8,128)(2,1)} %bitcast.28, bf16[1024,768]{1,0:T(8,128)(2,1)} %get-tuple-element.31.act_ref), custom_call_target="tpu_custom_call" | custom-call | flops 805306368 | bytes 2621440 | tf_op jit(solution)/shard_map/back/pallas_call | solution.py:263
  107.8 3.6 %back.3.in_ref = bf16[768,512]{1,0:T(8,128)(2,1)} custom-call(bf16[8,2,128,512]{3,2,1,0:T(8,128)(2,1)} %bitcast.29, bf16[1024,768]{1,0:T(8,128)(2,1)} %get-tuple-element.32.act_ref), custom_call_target="tpu_custom_call" | custom-call | flops 805306368 | bytes 2621440 | tf_op jit(solution)/shard_map/back/pallas_call | solution.py:263
  111.4 3.0 %interleave.2 = bf16[768,512]{1,0:T(8,128)(2,1)} custom-call(bf16[768,512]{1,0:T(8,128)(2,1)} %back.2.out_ref, bf16[768,512]{1,0:T(8,128)(2,1)} %back.3.in_ref), custom_call_target="tpu_custom_call" | custom-call | flops 600000000 | bytes 1600000 | tf_op jit(solution)/shard_map/interleave/pallas_call | solution.py:129
  114.4 18.5 %all_to_all.20 = bf16[32,24,512]{2,1,0:T(8,128)(2,1)S(1)} all-to-all(bf16[32,24,512]{2,1,0:T(8,128)(2,1)} %bitcast.31), channel_id=1, replica_groups=mesh['rep'=16,'exp'=32] {'exp'}, dimensions={0} | all-to-all | bytes 1572864 | tf_op jit(solution)/shard_map/all_to_all | solution.py:435
  132.8 3.0 %interleave.3 = bf16[768,512]{1,0:T(8,128)(2,1)} custom-call(bf16[768,512]{1,0:T(8,128)(2,1)} %back.2.out_ref, bf16[768,512]{1,0:T(8,128)(2,1)} %back.3.in_ref), custom_call_target="tpu_custom_call" | custom-call | flops 600000000 | bytes 1600000 | tf_op jit(solution)/shard_map/interleave/pallas_call | solution.py:129
  135.8 6.4 %all-to-all-start.3 = ((bf16[32,24,512]{2,1,0:T(8,128)(2,1)}), bf16[32,24,512]{2,1,0:T(8,128)(2,1)S(1)}, u32[]{:S(2)}, u32[]{:S(2)}) async-start(bf16[32,24,512]{2,1,0:T(8,128)(2,1)} %bitcast.30), calls=%async_computation.3 | async-start | bytes 1572864 | tf_op jit(solution)/shard_map/all_to_all | solution.py:435
  142.2 0.6 back_rows.1
  142.8 1.9 %collective-permute-start.6 = (bf16[512,512]{1,0:T(8,128)(2,1)S(1)}, bf16[512,512]{1,0:T(8,128)(2,1)S(1)}, u32[]{:S(2)}, u32[]{:S(2)}) collective-permute-start(bf16[512,512]{1,0:T(8,128)(2,1)S(1)} %back_rows.1), channel_id=1, source_target_pairs={{0,32},{1,481},{2,34},{3,483},{4,36},{5,485},{6,38},{7,487},{8,40}... | collective-permute-start | bytes 1572872 | tf_op jit(solution)/shard_map/ppermute | solution.py:431
  144.7 22.6 %collective-permute-done.6.got_ref = bf16[512,512]{1,0:T(8,128)(2,1)S(1)} collective-permute-done((bf16[512,512]{1,0:T(8,128)(2,1)S(1)}, bf16[512,512]{1,0:T(8,128)(2,1)S(1)}, u32[]{:S(2)}, u32[]{:S(2)}) %collective-permute-start.6) | collective-permute-done | bytes 524320 | tf_op jit(solution)/shard_map/ppermute | solution.py:431
  167.3 0.0 all-to-all-done.3
  167.3 1.4 combine.1
  168.7 0.0 reduce-scatter.2.cloned.1.call-done.sum_ref
  168.7 1.8 gradients.1
  (4 shorter events, 0.1 us)
Async XLA Ops:
  7.2 15.1 %copy-start.1 = (bf16[16,16,512]{2,1,0:T(8,128)(2,1)S(1)}, bf16[16,16,512]{2,1,0:T(8,128)(2,1)}, u32[]{:S(2)}) copy-start(bf16[16,16,512]{2,1,0:T(8,128)(2,1)} %param.8) | copy-start | bytes 786436
  7.2 27.2 %copy-start.4 = (bf16[512,512]{1,0:T(8,128)(2,1)S(1)}, bf16[512,512]{1,0:T(8,128)(2,1)}, u32[]{:S(2)}) copy-start(bf16[512,512]{1,0:T(8,128)(2,1)} %wproj_ref.1) | copy-start | bytes 1572868
  7.2 89.0 %all-gather.3.cloned.1.call-start = ((), (), s32[]{:S(2)}) async-start(), calls=%async_computation.6 | async-start | bytes 2359296 | tf_op jit(solution)/shard_map/all_gather | solution.py:437
  9.9 12.5 %collective-permute-start.1 = (bf16[4,16,512]{2,1,0:T(8,128)(2,1)S(1)}, bf16[4,16,512]{2,1,0:T(8,128)(2,1)S(1)}, u32[]{:S(2)}, u32[]{:S(2)}) collective-permute-start(bf16[4,16,512]{2,1,0:T(8,128)(2,1)S(1)} %get-tuple-element.42), channel_id=1, source_target_pairs={{32,0},{64,32},{96,64},{128,96},{160,128},{192,160},{224,192},{256... | collective-permute-start | bytes 196616 | tf_op jit(solution)/shard_map/ppermute | solution.py:446
  11.2 11.2 %collective-permute-start = (bf16[4,16,512]{2,1,0:T(8,128)(2,1)S(1)}, bf16[4,16,512]{2,1,0:T(8,128)(2,1)S(1)}, u32[]{:S(2)}, u32[]{:S(2)}) collective-permute-start(bf16[4,16,512]{2,1,0:T(8,128)(2,1)S(1)} %get-tuple-element.43), channel_id=1, source_target_pairs={{0,32},{32,64},{64,96},{96,128},{128,160},{160,192},{192,224},{224... | collective-permute-start | bytes 196616 | tf_op jit(solution)/shard_map/ppermute | solution.py:445
  16.6 1.0 copy-start
  17.5 0.7 copy-start.2
  18.2 16.2 %copy-start.3 = (bf16[512,1536]{1,0:T(8,128)(2,1)S(1)}, bf16[512,1536]{1,0:T(8,128)(2,1)}, u32[]{:S(2)}) copy-start(bf16[512,1536]{1,0:T(8,128)(2,1)} %wqkv_ref.1) | copy-start | bytes 4718596
  18.3 14.2 %collective-permute-start.3 = (bf16[272,512]{1,0:T(8,128)(2,1)S(1)}, bf16[272,512]{1,0:T(8,128)(2,1)}, u32[]{:S(2)}, u32[]{:S(2)}) collective-permute-start(bf16[272,512]{1,0:T(8,128)(2,1)S(1)} %upstream.1.give_ref), channel_id=1, source_target_pairs={{0,32},{1,481},{2,34},{3,483},{4,36},{5,485},{6,38},{7,487},{8,40}... | collective-permute-start | bytes 835592 | tf_op jit(solution)/shard_map/ppermute | solution.py:431
  22.7 9.9 %collective-permute-start.2 = (bf16[96,512]{1,0:T(8,128)(2,1)S(1)}, bf16[96,512]{1,0:T(8,128)(2,1)S(1)}, u32[]{:S(2)}, u32[]{:S(2)}) collective-permute-start(bf16[96,512]{1,0:T(8,128)(2,1)S(1)} %reshape.68), channel_id=1, source_target_pairs={{0,1},{1,2},{2,3},{3,4},{4,5},{5,6},{6,7},{7,8},{8,9},{9,10},{10,1... | collective-permute-start | bytes 294920 | tf_op jit(solution)/shard_map/ppermute | solution.py:458
  29.8 4.6 %collective-permute-start.4 = (bf16[96,512]{1,0:T(8,128)(2,1)S(1)}, bf16[96,512]{1,0:T(8,128)(2,1)S(1)}, u32[]{:S(2)}, u32[]{:S(2)}) collective-permute-start(bf16[96,512]{1,0:T(8,128)(2,1)S(1)} %reshape.69), channel_id=1, source_target_pairs={{1,0},{2,1},{3,2},{4,3},{5,4},{6,5},{7,6},{8,7},{9,8},{10,9},{11,1... | collective-permute-start | bytes 294920 | tf_op jit(solution)/shard_map/ppermute | solution.py:459
  40.4 30.6 %all-to-all-start = ((bf16[32,24,512]{2,1,0:T(8,128)(2,1)}), bf16[32,24,512]{2,1,0:T(8,128)(2,1)S(1)}, u32[]{:S(2)}, u32[]{:S(2)}) async-start(bf16[32,24,512]{2,1,0:T(8,128)(2,1)} %bitcast.8), calls=%async_computation | async-start | bytes 1572864 | tf_op jit(solution)/shard_map/all_to_all | solution.py:435
  51.2 17.2 %collective-permute-start.5 = (bf16[256,512]{1,0:T(8,128)(2,1)S(1)}, bf16[256,512]{1,0:T(8,128)(2,1)S(1)}, u32[]{:S(2)}, u32[]{:S(2)}) collective-permute-start(bf16[256,512]{1,0:T(8,128)(2,1)S(1)} %front.1.mixed_ref), channel_id=1, source_target_pairs={{0,32},{1,481},{2,34},{3,483},{4,36},{5,485},{6,38},{7,487},{8,40}... | collective-permute-start | bytes 786440 | tf_op jit(solution)/shard_map/ppermute | solution.py:431
  71.0 23.5 %all-to-all-start.1 = ((bf16[32,24,512]{2,1,0:T(8,128)(2,1)}), bf16[32,24,512]{2,1,0:T(8,128)(2,1)S(1)}, u32[]{:S(2)}, u32[]{:S(2)}) async-start(bf16[32,24,512]{2,1,0:T(8,128)(2,1)} %bitcast.10), calls=%async_computation.1 | async-start | bytes 1572864 | tf_op jit(solution)/shard_map/all_to_all | solution.py:435
  82.5 86.1 %reduce-scatter.2.cloned.1.call-start = ((), (), s32[]{:S(2)}) async-start(), calls=%async_computation.5 | async-start | bytes 2359296 | tf_op jit(solution)/shard_map/reduce_scatter | solution.py:494
  135.8 31.5 %all-to-all-start.3 = ((bf16[32,24,512]{2,1,0:T(8,128)(2,1)}), bf16[32,24,512]{2,1,0:T(8,128)(2,1)S(1)}, u32[]{:S(2)}, u32[]{:S(2)}) async-start(bf16[32,24,512]{2,1,0:T(8,128)(2,1)} %bitcast.30), calls=%async_computation.3 | async-start | bytes 1572864 | tf_op jit(solution)/shard_map/all_to_all | solution.py:435
  142.8 24.5 %collective-permute-start.6 = (bf16[512,512]{1,0:T(8,128)(2,1)S(1)}, bf16[512,512]{1,0:T(8,128)(2,1)S(1)}, u32[]{:S(2)}, u32[]{:S(2)}) collective-permute-start(bf16[512,512]{1,0:T(8,128)(2,1)S(1)} %back_rows.1), channel_id=1, source_target_pairs={{0,32},{1,481},{2,34},{3,483},{4,36},{5,485},{6,38},{7,487},{8,40}... | collective-permute-start | bytes 1572872 | tf_op jit(solution)/shard_map/ppermute | solution.py:431
Sparse Core Ops, SparseCore 0:
  10.7 70.2 all-gather.2
  104.2 63.3 reduce-scatter.1

commit v8 on v6

--- a/solution.py
+++ b/solution.py
@@ -88,10 +88,11 @@
     slots_ref[...] = total.astype(jnp.bfloat16)
 
 
-def token_slots_kernel(target_ref, mixed_ref, got_ref, slots_ref):
+def token_slots_kernel(target_ref, mixed_ref, first_ref, second_ref, slots_ref):
     rows = slots_ref.shape[0]
     total = nn(placer(target_ref[0:1], rows), mixed_ref[...])
-    total = total + nn(placer(target_ref[1:2], rows), got_ref[...])
+    got = jnp.concatenate([first_ref[...], second_ref[...]], axis=0)
+    total = total + nn(placer(target_ref[1:2], rows), got)
     slots_ref[...] = total.astype(jnp.bfloat16)
 
 
@@ -210,7 +211,7 @@
         out_specs=pl.BlockSpec((rows, feature), lambda i: (0, 0)),
         out_shape=jax.ShapeDtypeStruct((rows, feature), jnp.bfloat16),
         scratch_shapes=[pltpu.VMEM((rows, feature), jnp.float32)],
-        compiler_params=pltpu.CompilerParams(vmem_limit_bytes=VMEM_LIMIT),
+        compiler_params=pltpu.CompilerParams(vmem_limit_bytes=MIDDLE_LIMIT),
         cost_estimate=pl.CostEstimate(
             flops=2 * rows * ff * feature,
             bytes_accessed=2 * ff * feature + 2 * ff * rows,
@@ -256,7 +257,8 @@
 
 
 def front_kernel(
-    at_ref, tok_ref, low_ref, high_ref, left_ref, right_ref, wqkv_ref, wproj_ref, mixed_ref, qkv_ref, ctx_ref
+    at_ref, tok_ref, low_ref, high_ref, left_ref, right_ref, wqkv_ref, wproj_ref,
+    mixed_ref, first_ref, second_ref, qkv_ref, ctx_ref,
 ):
     bf16, f32 = jnp.bfloat16, jnp.float32
     tokens = tok_ref[...]
@@ -319,6 +321,8 @@
     spread_of = jnp.mean(centred * centred, axis=-1, keepdims=True)
     mixed = (tokens.astype(f32) + centred * lax.rsqrt(spread_of + 1e-05)).astype(bf16)
     mixed_ref[...] = mixed
+    for n, ref in enumerate((first_ref, second_ref)):
+        ref[...] = mixed[n * count // 2 : (n + 1) * count // 2]
 
 
 def front(at, tokens, low, high, left, right, w_qkv, w_proj):
@@ -328,7 +332,7 @@
     vmem = pl.BlockSpec(memory_space=pltpu.VMEM)
     return vmem_call(
         front_kernel,
-        [((count, feature), jnp.bfloat16)],
+        [((count, feature), jnp.bfloat16)] + [((count // 2, feature), jnp.bfloat16)] * 2,
         "front",
         4_000_000_000,
         in_specs=[smem] + [vmem] * 7,
@@ -336,7 +340,7 @@
             pltpu.VMEM((ext, 3 * feature), jnp.bfloat16),
             pltpu.VMEM((ext, feature), jnp.bfloat16),
         ],
-    )(at, tokens, low, high, left, right, w_qkv, w_proj)[0]
+    )(at, tokens, low, high, left, right, w_qkv, w_proj)
 
 
 def shifts(axis):
@@ -397,6 +401,7 @@
 
     left = lax.ppermute(strip(slice(tile_cols - margin, tile_cols)), "exp", forward)
     right = lax.ppermute(strip(slice(0, margin)), "exp", backward)
+    got, left, right = lax.optimization_barrier((got, left, right))
     at = jnp.stack(
         [
             lax.axis_index("rep"),
@@ -405,7 +410,7 @@
             jnp.int32(experts),
         ]
     ).astype(jnp.int32)
-    mixed = front(
+    mixed, *halves = front(
         at,
         tokens.reshape(tok_count, feature),
         low.reshape(-1, feature),
@@ -415,7 +420,7 @@
         w_qkv,
         w_proj,
     )
-    got_mixed = exchange(mixed)
+    got_halves = [exchange(half) for half in halves]
     slots_g, target = vmem_call(
         functools.partial(grad_slots_kernel, experts, capacity),
         [rows_of, ((2, tok_count), jnp.int32)],
@@ -424,8 +429,8 @@
         count=2,
     )(give, got)
     slot_g = dispatch(slots_g)
-    [slots_x] = vmem_call(token_slots_kernel, [rows_of], "token_slots", 400_000_000, count=3)(
-        target, mixed, got_mixed
+    [slots_x] = vmem_call(token_slots_kernel, [rows_of], "token_slots", 400_000_000, count=4)(
+        target, mixed, *got_halves
     )
     slot_x = dispatch(slots_x)
     grads, hidden, pre_grad = middle(weights, slot_x, slot_g)

time: 174 us -> 178 us (1.023)
  the two profiles are of different devices: /device:TPU:1 before, /device:TPU:6 now
where the time goes in v8:
time: 178 us; the launch traced here: 175 us
  starting transfers between devices  54 us (30%)
  waiting for transfers between devices  52.2 us (29%)
  Pallas kernels  24.9 us (14%)
  blocking collectives  22 us (12%)
  between operations  14.3 us (8%)
  local copies, waits for them, and re-layouts  5.83 us (3%)
  other arithmetic  1.96 us (1%)
    ppermute x5, waiting for transfers between devices, exchange(): return lax.ppermute(rows, ('rep', 'exp'), swap)  31.7 us
    all_to_all x3, starting transfers between devices, dispatch(): return lax.all_to_all(blocks, 'exp', 0, 0, tiled=True).reshape(-1, feature)  23.6 us
    all_to_all x1, blocking collectives, dispatch(): return lax.all_to_all(blocks, 'exp', 0, 0, tiled=True).reshape(-1, feature)  22 us
    all_to_all x3, waiting for transfers between devices, dispatch(): return lax.all_to_all(blocks, 'exp', 0, 0, tiled=True).reshape(-1, feature)  18.2 us
    ppermute x5, starting transfers between devices, exchange(): return lax.ppermute(rows, ('rep', 'exp'), swap)  14.2 us
    ppermute x1, starting transfers between devices, per_device(): lax.ppermute(strip(slice(tile_cols - margin, tile_cols)), 'exp', forward)  8.61 us
    pallas_call x1, Pallas kernels, middle(): pl.pallas_call(middle_kernel, grid=(CHUNKS,), in_specs=[pl.BlockSpec((ste...  7.89 us
    pallas_call x2, Pallas kernels, back(): pl.pallas_call(functools.partial(back_kernel, side), grid=(steps,), in_sp...  7.35 us
  transfers between devices with their start and end apart: 14, of which 8 were waited for; matrix products, arithmetic and copies ran while one was open for 1% of the time, Pallas kernels for 9%

profile of v8, /device:TPU:6, one launch (start us, length us, event | category | flops | bytes accessed | tf_op | source)
XLA Modules:
  0.0 175.1 jit_solution(8983031155592975274)
XLA Ops:
  7.2 0.0 copy-start.1
  7.2 0.0 all-gather.3.cloned.1.call-start
  7.2 1.7 pad_maximum_fusion
  9.0 0.0 all-gather.3.cloned.1.call-update
  9.0 0.9 fusion.1
  9.9 3.8 %collective-permute-start.1 = (bf16[4,16,512]{2,1,0:T(8,128)(2,1)S(1)}, bf16[4,16,512]{2,1,0:T(8,128)(2,1)S(1)}, u32[]{:S(2)}, u32[]{:S(2)}) collective-permute-start(bf16[4,16,512]{2,1,0:T(8,128)(2,1)S(1)} %get-tuple-element.40), channel_id=1, source_target_pairs={{0,32},{32,64},{64,96},{96,128},{128,160},{160,192},{192,224},{224... | collective-permute-start | bytes 196616 | tf_op jit(solution)/shard_map/ppermute | solution.py:389
  13.7 1.3 collective-permute-start.2
  15.0 0.8 reshape.81.gate_ref
  15.8 0.0 copy-start
  15.8 0.9 copy-done
  16.8 0.0 copy-start.3
  16.8 0.7 copy-done.3
  17.4 0.1 upstream.1.give_ref
  17.5 4.6 %collective-permute-start = (bf16[272,512]{1,0:T(8,128)(2,1)S(1)}, bf16[272,512]{1,0:T(8,128)(2,1)S(1)}, u32[]{:S(2)}, u32[]{:S(2)}) collective-permute-start(bf16[272,512]{1,0:T(8,128)(2,1)S(1)} %upstream.1.give_ref), channel_id=1, source_target_pairs={{0,32},{1,481},{2,34},{3,483},{4,36},{5,485},{6,38},{7,487},{8,40}... | collective-permute-start | bytes 835592 | tf_op jit(solution)/shard_map/ppermute | solution.py:375
  22.1 0.0 copy-done.1
  22.1 0.1 fusion
  22.2 0.0 collective-permute-done.1
  22.2 0.0 collective-permute-done.2
  22.2 0.1 pad_maximum_fusion.2
  22.4 0.1 pad_maximum_fusion.1
  22.5 0.0 copy-start.5
  22.5 8.6 %collective-permute-start.3 = (bf16[96,512]{1,0:T(8,128)(2,1)S(1)}, bf16[96,512]{1,0:T(8,128)(2,1)S(1)}, u32[]{:S(2)}, u32[]{:S(2)}) collective-permute-start(bf16[96,512]{1,0:T(8,128)(2,1)S(1)} %reshape.65), channel_id=1, source_target_pairs={{0,1},{1,2},{2,3},{3,4},{4,5},{5,6},{6,7},{7,8},{8,9},{9,10},{10,1... | collective-permute-start | bytes 294920 | tf_op jit(solution)/shard_map/ppermute | solution.py:402
  31.1 2.4 %collective-permute-start.4 = (bf16[96,512]{1,0:T(8,128)(2,1)S(1)}, bf16[96,512]{1,0:T(8,128)(2,1)S(1)}, u32[]{:S(2)}, u32[]{:S(2)}) collective-permute-start(bf16[96,512]{1,0:T(8,128)(2,1)S(1)} %reshape.66), channel_id=1, source_target_pairs={{1,0},{2,1},{3,2},{4,3},{5,4},{6,5},{7,6},{8,7},{9,8},{10,9},{11,1... | collective-permute-start | bytes 294920 | tf_op jit(solution)/shard_map/ppermute | solution.py:403
  33.5 0.4 collective-permute-done.3.left_ref
  33.8 1.8 %collective-permute-done.4.right_ref = bf16[96,512]{1,0:T(8,128)(2,1)S(1)} collective-permute-done((bf16[96,512]{1,0:T(8,128)(2,1)S(1)}, bf16[96,512]{1,0:T(8,128)(2,1)S(1)}, u32[]{:S(2)}, u32[]{:S(2)}) %collective-permute-start.4) | collective-permute-done | bytes 98336 | tf_op jit(solution)/shard_map/ppermute | solution.py:403
  35.7 0.0 collective-permute-done.got_ref
  35.7 1.6 grad_slots.1
  37.3 10.8 %all-to-all-start.1 = ((bf16[32,24,512]{2,1,0:T(8,128)(2,1)}), bf16[32,24,512]{2,1,0:T(8,128)(2,1)S(1)}, u32[]{:S(2)}, u32[]{:S(2)}) async-start(bf16[32,24,512]{2,1,0:T(8,128)(2,1)} %bitcast.10), calls=%async_computation.1 | async-start | bytes 1572864 | tf_op jit(solution)/shard_map/all_to_all | solution.py:379
  48.1 0.0 reduce-scatter.2.cloned.1.call-start
  48.1 0.1 pad_add_fusion.at_ref
  48.2 0.0 copy-done.5
  48.2 0.0 copy-start.4
  48.2 1.4 copy-done.4
  49.6 4.4 %front.1 = (bf16[256,512]{1,0:T(8,128)(2,1)S(1)}, bf16[128,512]{1,0:T(8,128)(2,1)S(1)}, bf16[128,512]{1,0:T(8,128)(2,1)S(1)}) custom-call(s32[4]{0:T(128)S(1)} %pad_add_fusion.at_ref, bf16[256,512]{1,0:T(8,128)(2,1)S(1)} %bitcast.24, bf16[64,512]{1,0:T(8,128)(2,1)S(1)} %bitcast.25, bf16[64,512]{1,0:T(8,128)(2,1)S(1)} %bitcast.26, ...), custom_call_target="tpu_custom_call" | custom-call | flops 4000000000 | bytes 3000000 | tf_op jit(solution)/shard_map/front/pallas_call | solution.py:333
  54.0 1.9 %collective-permute-start.5 = (bf16[128,512]{1,0:T(8,128)(2,1)S(1)}, bf16[128,512]{1,0:T(8,128)(2,1)S(1)}, u32[]{:S(2)}, u32[]{:S(2)}) collective-permute-start(bf16[128,512]{1,0:T(8,128)(2,1)S(1)} %get-tuple-element.26), channel_id=1, source_target_pairs={{0,32},{1,481},{2,34},{3,483},{4,36},{5,485},{6,38},{7,487},{8,40}... | collective-permute-start | bytes 393224 | tf_op jit(solution)/shard_map/ppermute | solution.py:375
  55.9 3.9 %collective-permute-start.6 = (bf16[128,512]{1,0:T(8,128)(2,1)S(1)}, bf16[128,512]{1,0:T(8,128)(2,1)S(1)}, u32[]{:S(2)}, u32[]{:S(2)}) collective-permute-start(bf16[128,512]{1,0:T(8,128)(2,1)S(1)} %get-tuple-element.27), channel_id=1, source_target_pairs={{0,32},{1,481},{2,34},{3,483},{4,36},{5,485},{6,38},{7,487},{8,40}... | collective-permute-start | bytes 393224 | tf_op jit(solution)/shard_map/ppermute | solution.py:375
  59.9 4.3 %collective-permute-done.5.first_ref = bf16[128,512]{1,0:T(8,128)(2,1)S(1)} collective-permute-done((bf16[128,512]{1,0:T(8,128)(2,1)S(1)}, bf16[128,512]{1,0:T(8,128)(2,1)S(1)}, u32[]{:S(2)}, u32[]{:S(2)}) %collective-permute-start.5) | collective-permute-done | bytes 131104 | tf_op jit(solution)/shard_map/ppermute | solution.py:375
  64.2 7.0 %collective-permute-done.6.second_ref = bf16[128,512]{1,0:T(8,128)(2,1)S(1)} collective-permute-done((bf16[128,512]{1,0:T(8,128)(2,1)S(1)}, bf16[128,512]{1,0:T(8,128)(2,1)S(1)}, u32[]{:S(2)}, u32[]{:S(2)}) %collective-permute-start.6) | collective-permute-done | bytes 131104 | tf_op jit(solution)/shard_map/ppermute | solution.py:375
  71.2 0.6 token_slots.1
  71.7 0.0 all-to-all-done.1
  71.8 0.0 copy-start.6
  71.8 22.0 %all_to_all.20 = bf16[32,24,512]{2,1,0:T(8,128)(2,1)} all-to-all(bf16[32,24,512]{2,1,0:T(8,128)(2,1)S(1)} %bitcast.22), channel_id=1, replica_groups=mesh['rep'=16,'exp'=32] {'exp'}, dimensions={0} | all-to-all | bytes 1572864 | tf_op jit(solution)/shard_map/all_to_all | solution.py:379
  93.8 0.0 all-gather.3.cloned.1.call-done
  93.8 0.0 copy-done.6
  93.8 7.9 %middle.1 = (bf16[8,256,512]{2,1,0:T(8,128)(2,1)}, bf16[1024,768]{1,0:T(8,128)(2,1)}, bf16[1024,768]{1,0:T(8,128)(2,1)}) custom-call(bf16[8,2,128,512]{3,2,1,0:T(8,128)(2,1)} %bitcast.28, bf16[768,512]{1,0:T(8,128)(2,1)} %bitcast.34, bf16[768,512]{1,0:T(8,128)(2,1)} %bitcast.33), custom_call_target="tpu_custom_call" | custom-call | flops 3221225472 | bytes 7340032 | tf_op jit(solution)/shard_map/middle/pallas_call | solution.py:156
  101.7 0.0 reduce-scatter.2.cloned.1.call-update
  101.7 3.7 %back.2 = bf16[768,512]{1,0:T(8,128)(2,1)} custom-call(bf16[8,2,128,512]{3,2,1,0:T(8,128)(2,1)} %bitcast.29, bf16[1024,768]{1,0:T(8,128)(2,1)} %get-tuple-element.29.act_ref), custom_call_target="tpu_custom_call" | custom-call | flops 805306368 | bytes 2621440 | tf_op jit(solution)/shard_map/back/pallas_call | solution.py:204
  105.4 6.4 %all-to-all-start.2 = ((bf16[32,24,512]{2,1,0:T(8,128)(2,1)}), bf16[32,24,512]{2,1,0:T(8,128)(2,1)S(1)}, u32[]{:S(2)}, u32[]{:S(2)}) async-start(bf16[32,24,512]{2,1,0:T(8,128)(2,1)} %bitcast.32), calls=%async_computation.2 | async-start | bytes 1572864 | tf_op jit(solution)/shard_map/all_to_all | solution.py:379
  111.8 3.6 %back.3 = bf16[768,512]{1,0:T(8,128)(2,1)} custom-call(bf16[8,2,128,512]{3,2,1,0:T(8,128)(2,1)} %bitcast.30, bf16[1024,768]{1,0:T(8,128)(2,1)} %get-tuple-element.30.act_ref), custom_call_target="tpu_custom_call" | custom-call | flops 805306368 | bytes 2621440 | tf_op jit(solution)/shard_map/back/pallas_call | solution.py:204
  115.4 8.4 %all-to-all-done.2 = bf16[32,24,512]{2,1,0:T(8,128)(2,1)S(1)} async-done(((bf16[32,24,512]{2,1,0:T(8,128)(2,1)}), bf16[32,24,512]{2,1,0:T(8,128)(2,1)S(1)}, u32[]{:S(2)}, u32[]{:S(2)}) %all-to-all-start.2) | async-done | bytes 786464 | tf_op jit(solution)/shard_map/all_to_all | solution.py:379
  123.9 6.4 %all-to-all-start.3 = ((bf16[32,24,512]{2,1,0:T(8,128)(2,1)}), bf16[32,24,512]{2,1,0:T(8,128)(2,1)S(1)}, u32[]{:S(2)}, u32[]{:S(2)}) async-start(bf16[32,24,512]{2,1,0:T(8,128)(2,1)} %bitcast.31), calls=%async_computation.3 | async-start | bytes 1572864 | tf_op jit(solution)/shard_map/all_to_all | solution.py:379
  130.3 0.4 back_rows.2
  130.7 1.9 %collective-permute-start.7 = (bf16[256,512]{1,0:T(8,128)(2,1)S(1)}, bf16[256,512]{1,0:T(8,128)(2,1)S(1)}, u32[]{:S(2)}, u32[]{:S(2)}) collective-permute-start(bf16[256,512]{1,0:T(8,128)(2,1)S(1)} %back_rows.2), channel_id=1, source_target_pairs={{0,32},{1,481},{2,34},{3,483},{4,36},{5,485},{6,38},{7,487},{8,40}... | collective-permute-start | bytes 786440 | tf_op jit(solution)/shard_map/ppermute | solution.py:375
  132.6 9.7 %all-to-all-done.3 = bf16[32,24,512]{2,1,0:T(8,128)(2,1)S(1)} async-done(((bf16[32,24,512]{2,1,0:T(8,128)(2,1)}), bf16[32,24,512]{2,1,0:T(8,128)(2,1)S(1)}, u32[]{:S(2)}, u32[]{:S(2)}) %all-to-all-start.3) | async-done | bytes 786464 | tf_op jit(solution)/shard_map/all_to_all | solution.py:379
  142.3 8.6 %collective-permute-done.7.got_out_ref = bf16[256,512]{1,0:T(8,128)(2,1)S(1)} collective-permute-done((bf16[256,512]{1,0:T(8,128)(2,1)S(1)}, bf16[256,512]{1,0:T(8,128)(2,1)S(1)}, u32[]{:S(2)}, u32[]{:S(2)}) %collective-permute-start.7) | collective-permute-done | bytes 262176 | tf_op jit(solution)/shard_map/ppermute | solution.py:375
  150.9 0.4 back_rows.3
  151.3 1.9 %collective-permute-start.8 = (bf16[256,512]{1,0:T(8,128)(2,1)S(1)}, bf16[256,512]{1,0:T(8,128)(2,1)S(1)}, u32[]{:S(2)}, u32[]{:S(2)}) collective-permute-start(bf16[256,512]{1,0:T(8,128)(2,1)S(1)} %back_rows.3), channel_id=1, source_target_pairs={{0,32},{1,481},{2,34},{3,483},{4,36},{5,485},{6,38},{7,487},{8,40}... | collective-permute-start | bytes 786440 | tf_op jit(solution)/shard_map/ppermute | solution.py:375
  153.2 11.9 %collective-permute-done.8.got_in_ref = bf16[256,512]{1,0:T(8,128)(2,1)S(1)} collective-permute-done((bf16[256,512]{1,0:T(8,128)(2,1)S(1)}, bf16[256,512]{1,0:T(8,128)(2,1)S(1)}, u32[]{:S(2)}, u32[]{:S(2)}) %collective-permute-start.8) | collective-permute-done | bytes 262176 | tf_op jit(solution)/shard_map/ppermute | solution.py:375
  165.1 1.4 combine.1
  166.5 0.0 reduce-scatter.2.cloned.1.call-done.sum_ref
  166.5 0.0 copy-start.2
  166.5 0.9 copy-done.2
  167.5 0.8 gradients.1
  (4 shorter events, 0.1 us)
Async XLA Ops:
  7.2 14.9 %copy-start.1 = (bf16[16,16,512]{2,1,0:T(8,128)(2,1)S(1)}, bf16[16,16,512]{2,1,0:T(8,128)(2,1)}, u32[]{:S(2)}) copy-start(bf16[16,16,512]{2,1,0:T(8,128)(2,1)} %param.8) | copy-start | bytes 786436
  7.2 86.6 %all-gather.3.cloned.1.call-start = ((), (), s32[]{:S(2)}) async-start(), calls=%async_computation.6 | async-start | bytes 2359296 | tf_op jit(solution)/shard_map/all_gather | solution.py:381
  9.9 12.3 %collective-permute-start.1 = (bf16[4,16,512]{2,1,0:T(8,128)(2,1)S(1)}, bf16[4,16,512]{2,1,0:T(8,128)(2,1)S(1)}, u32[]{:S(2)}, u32[]{:S(2)}) collective-permute-start(bf16[4,16,512]{2,1,0:T(8,128)(2,1)S(1)} %get-tuple-element.40), channel_id=1, source_target_pairs={{0,32},{32,64},{64,96},{96,128},{128,160},{160,192},{192,224},{224... | collective-permute-start | bytes 196616 | tf_op jit(solution)/shard_map/ppermute | solution.py:389
  13.7 8.5 %collective-permute-start.2 = (bf16[4,16,512]{2,1,0:T(8,128)(2,1)S(1)}, bf16[4,16,512]{2,1,0:T(8,128)(2,1)S(1)}, u32[]{:S(2)}, u32[]{:S(2)}) collective-permute-start(bf16[4,16,512]{2,1,0:T(8,128)(2,1)S(1)} %get-tuple-element.41), channel_id=1, source_target_pairs={{32,0},{64,32},{96,64},{128,96},{160,128},{192,160},{224,192},{256... | collective-permute-start | bytes 196616 | tf_op jit(solution)/shard_map/ppermute | solution.py:390
  15.8 1.0 copy-start
  16.8 0.7 copy-start.3
  17.5 18.1 %collective-permute-start = (bf16[272,512]{1,0:T(8,128)(2,1)S(1)}, bf16[272,512]{1,0:T(8,128)(2,1)S(1)}, u32[]{:S(2)}, u32[]{:S(2)}) collective-permute-start(bf16[272,512]{1,0:T(8,128)(2,1)S(1)} %upstream.1.give_ref), channel_id=1, source_target_pairs={{0,32},{1,481},{2,34},{3,483},{4,36},{5,485},{6,38},{7,487},{8,40}... | collective-permute-start | bytes 835592 | tf_op jit(solution)/shard_map/ppermute | solution.py:375
  22.5 25.7 %copy-start.5 = (bf16[512,512]{1,0:T(8,128)(2,1)S(1)}, bf16[512,512]{1,0:T(8,128)(2,1)}, u32[]{:S(2)}) copy-start(bf16[512,512]{1,0:T(8,128)(2,1)} %wproj_ref.1) | copy-start | bytes 1572868
  22.5 11.3 %collective-permute-start.3 = (bf16[96,512]{1,0:T(8,128)(2,1)S(1)}, bf16[96,512]{1,0:T(8,128)(2,1)S(1)}, u32[]{:S(2)}, u32[]{:S(2)}) collective-permute-start(bf16[96,512]{1,0:T(8,128)(2,1)S(1)} %reshape.65), channel_id=1, source_target_pairs={{0,1},{1,2},{2,3},{3,4},{4,5},{5,6},{6,7},{7,8},{8,9},{9,10},{10,1... | collective-permute-start | bytes 294920 | tf_op jit(solution)/shard_map/ppermute | solution.py:402
  31.1 4.6 %collective-permute-start.4 = (bf16[96,512]{1,0:T(8,128)(2,1)S(1)}, bf16[96,512]{1,0:T(8,128)(2,1)S(1)}, u32[]{:S(2)}, u32[]{:S(2)}) collective-permute-start(bf16[96,512]{1,0:T(8,128)(2,1)S(1)} %reshape.66), channel_id=1, source_target_pairs={{1,0},{2,1},{3,2},{4,3},{5,4},{6,5},{7,6},{8,7},{9,8},{10,9},{11,1... | collective-permute-start | bytes 294920 | tf_op jit(solution)/shard_map/ppermute | solution.py:403
  37.3 34.5 %all-to-all-start.1 = ((bf16[32,24,512]{2,1,0:T(8,128)(2,1)}), bf16[32,24,512]{2,1,0:T(8,128)(2,1)S(1)}, u32[]{:S(2)}, u32[]{:S(2)}) async-start(bf16[32,24,512]{2,1,0:T(8,128)(2,1)} %bitcast.10), calls=%async_computation.1 | async-start | bytes 1572864 | tf_op jit(solution)/shard_map/all_to_all | solution.py:379
  48.1 118.4 %reduce-scatter.2.cloned.1.call-start = ((), (), s32[]{:S(2)}) async-start(), calls=%async_computation.5 | async-start | bytes 2359296 | tf_op jit(solution)/shard_map/reduce_scatter | solution.py:437
  48.2 1.4 copy-start.4
  54.0 10.2 %collective-permute-start.5 = (bf16[128,512]{1,0:T(8,128)(2,1)S(1)}, bf16[128,512]{1,0:T(8,128)(2,1)S(1)}, u32[]{:S(2)}, u32[]{:S(2)}) collective-permute-start(bf16[128,512]{1,0:T(8,128)(2,1)S(1)} %get-tuple-element.26), channel_id=1, source_target_pairs={{0,32},{1,481},{2,34},{3,483},{4,36},{5,485},{6,38},{7,487},{8,40}... | collective-permute-start | bytes 393224 | tf_op jit(solution)/shard_map/ppermute | solution.py:375
  55.9 15.2 %collective-permute-start.6 = (bf16[128,512]{1,0:T(8,128)(2,1)S(1)}, bf16[128,512]{1,0:T(8,128)(2,1)S(1)}, u32[]{:S(2)}, u32[]{:S(2)}) collective-permute-start(bf16[128,512]{1,0:T(8,128)(2,1)S(1)} %get-tuple-element.27), channel_id=1, source_target_pairs={{0,32},{1,481},{2,34},{3,483},{4,36},{5,485},{6,38},{7,487},{8,40}... | collective-permute-start | bytes 393224 | tf_op jit(solution)/shard_map/ppermute | solution.py:375
  71.8 22.0 %copy-start.6 = (bf16[32,24,512]{2,1,0:T(8,128)(2,1)}, bf16[32,24,512]{2,1,0:T(8,128)(2,1)S(1)}, u32[]{:S(2)}) copy-start(bf16[32,24,512]{2,1,0:T(8,128)(2,1)S(1)} %all-to-all-done.1) | copy-start | bytes 2359300
  105.4 18.5 %all-to-all-start.2 = ((bf16[32,24,512]{2,1,0:T(8,128)(2,1)}), bf16[32,24,512]{2,1,0:T(8,128)(2,1)S(1)}, u32[]{:S(2)}, u32[]{:S(2)}) async-start(bf16[32,24,512]{2,1,0:T(8,128)(2,1)} %bitcast.32), calls=%async_computation.2 | async-start | bytes 1572864 | tf_op jit(solution)/shard_map/all_to_all | solution.py:379
  123.9 18.5 %all-to-all-start.3 = ((bf16[32,24,512]{2,1,0:T(8,128)(2,1)}), bf16[32,24,512]{2,1,0:T(8,128)(2,1)S(1)}, u32[]{:S(2)}, u32[]{:S(2)}) async-start(bf16[32,24,512]{2,1,0:T(8,128)(2,1)} %bitcast.31), calls=%async_computation.3 | async-start | bytes 1572864 | tf_op jit(solution)/shard_map/all_to_all | solution.py:379
  130.7 20.2 %collective-permute-start.7 = (bf16[256,512]{1,0:T(8,128)(2,1)S(1)}, bf16[256,512]{1,0:T(8,128)(2,1)S(1)}, u32[]{:S(2)}, u32[]{:S(2)}) collective-permute-start(bf16[256,512]{1,0:T(8,128)(2,1)S(1)} %back_rows.2), channel_id=1, source_target_pairs={{0,32},{1,481},{2,34},{3,483},{4,36},{5,485},{6,38},{7,487},{8,40}... | collective-permute-start | bytes 786440 | tf_op jit(solution)/shard_map/ppermute | solution.py:375
  151.3 13.8 %collective-permute-start.8 = (bf16[256,512]{1,0:T(8,128)(2,1)S(1)}, bf16[256,512]{1,0:T(8,128)(2,1)S(1)}, u32[]{:S(2)}, u32[]{:S(2)}) collective-permute-start(bf16[256,512]{1,0:T(8,128)(2,1)S(1)} %back_rows.3), channel_id=1, source_target_pairs={{0,32},{1,481},{2,34},{3,483},{4,36},{5,485},{6,38},{7,487},{8,40}... | collective-permute-start | bytes 786440 | tf_op jit(solution)/shard_map/ppermute | solution.py:375
  166.5 0.9 copy-start.2
Sparse Core Ops, SparseCore 0:
  10.7 70.8 all-gather.2
  101.8 64.6 reduce-scatter.1

commit v9 on v6

--- a/solution.py
+++ b/solution.py
@@ -374,13 +374,6 @@
         blocks = rows.reshape(experts, -1, feature)
         return lax.all_to_all(blocks, "exp", 0, 0, tiled=True).reshape(-1, feature)
 
-    weights = lax.all_gather(
-        jnp.concatenate([w_up, w_down], axis=0),
-        "rep",
-        axis=0,
-        tiled=False,
-        axis_index_groups=groups,
-    )
     forward, backward = shifts("rep")
     low = lax.ppermute(tokens[tile_rows - margin :], "rep", forward)
     high = lax.ppermute(tokens[:margin], "rep", backward)
@@ -389,6 +382,14 @@
         upstream_kernel, [((tok_count + EXTRA, feature), bf16)], "upstream", 1_000_000, count=3
     )(route.reshape(1, tok_count), gate_rows, cotangent.reshape(tok_count, feature))
     got = exchange(give)
+    w_up, w_down, give = lax.optimization_barrier((w_up, w_down, give))
+    weights = lax.all_gather(
+        jnp.concatenate([w_up, w_down], axis=0),
+        "rep",
+        axis=0,
+        tiled=False,
+        axis_index_groups=groups,
+    )
     forward, backward = shifts("exp")
 
     def strip(cols):
@@ -416,6 +417,7 @@
         w_proj,
     )
     got_mixed = exchange(mixed)
+    got, mixed = lax.optimization_barrier((got, mixed))
     slots_g, target = vmem_call(
         functools.partial(grad_slots_kernel, experts, capacity),
         [rows_of, ((2, tok_count), jnp.int32)],

time: 174 us -> 181 us (1.040)
  the two profiles are of different devices: /device:TPU:1 before, /device:TPU:6 now
where the time goes in v9:
time: 181 us; the launch traced here: 178 us
  waiting for transfers between devices  53.4 us (30%)
  starting transfers between devices  51.6 us (29%)
  blocking collectives  23.8 us (13%)
  Pallas kernels  20.6 us (11%)
  between operations  14.3 us (8%)
  local copies, waits for them, and re-layouts  12.3 us (7%)
  other arithmetic  2.07 us (1%)
    ppermute x4, waiting for transfers between devices, exchange(): return lax.ppermute(rows, ('rep', 'exp'), swap)  30.7 us
    all_to_all x1, blocking collectives, dispatch(): return lax.all_to_all(blocks, 'exp', 0, 0, tiled=True).reshape(-1, feature)  23.8 us
    all_to_all x3, starting transfers between devices, dispatch(): return lax.all_to_all(blocks, 'exp', 0, 0, tiled=True).reshape(-1, feature)  23.6 us
    all_to_all x3, waiting for transfers between devices, dispatch(): return lax.all_to_all(blocks, 'exp', 0, 0, tiled=True).reshape(-1, feature)  17.9 us
    ppermute x4, starting transfers between devices, exchange(): return lax.ppermute(rows, ('rep', 'exp'), swap)  11.9 us
    unnamed x28, local copies, waits for them, and re-layouts  10.5 us
    ppermute x1, starting transfers between devices, per_device(): lax.ppermute(strip(slice(tile_cols - margin, tile_cols)), 'exp', forward)  7.91 us
    pallas_call x1, Pallas kernels, middle(): pl.pallas_call(middle_kernel, grid=(CHUNKS,), in_specs=[pl.BlockSpec((ste...  7.9 us
  transfers between devices with their start and end apart: 13, of which 10 were waited for; matrix products, arithmetic and copies ran while one was open for 1% of the time, Pallas kernels for 7%

profile of v9, /device:TPU:6, one launch (start us, length us, event | category | flops | bytes accessed | tf_op | source)
XLA Modules:
  0.0 178.1 jit_solution(13511890072624238662)
XLA Ops:
  7.2 0.0 all-gather.3.cloned.1.call-start
  7.2 0.8 reshape.81.gate_ref
  8.0 0.0 copy-start.5
  8.0 0.9 copy-done.5
  9.0 0.7 copy-done.8
  9.7 0.1 upstream.1.give_ref
  9.8 1.8 %pad_maximum_fusion = bf16[2,128,512]{2,1,0:T(8,128)(2,1)} fusion(bf16[1,128,512]{2,1,0:T(8,128)(2,1)} %param.15, bf16[1,128,512]{2,1,0:T(8,128)(2,1)} %param.14), kind=kLoop, calls=%fused_computation | loop fusion | flops 131072 | bytes 524288 | tf_op jit(solution)/shard_map/concatenate | solution.py:387
  11.6 0.0 all-gather.3.cloned.1.call-update
  11.6 3.8 %collective-permute-start = (bf16[272,512]{1,0:T(8,128)(2,1)S(1)}, bf16[272,512]{1,0:T(8,128)(2,1)S(1)}, u32[]{:S(2)}, u32[]{:S(2)}) collective-permute-start(bf16[272,512]{1,0:T(8,128)(2,1)S(1)} %upstream.1.give_ref), channel_id=1, source_target_pairs={{0,32},{1,481},{2,34},{3,483},{4,36},{5,485},{6,38},{7,487},{8,40}... | collective-permute-start | bytes 835592 | tf_op jit(solution)/shard_map/ppermute | solution.py:371
  15.5 0.9 fusion.1
  16.3 1.3 collective-permute-start.2
  17.6 4.5 %collective-permute-start.1 = (bf16[4,16,512]{2,1,0:T(8,128)(2,1)S(1)}, bf16[4,16,512]{2,1,0:T(8,128)(2,1)S(1)}, u32[]{:S(2)}, u32[]{:S(2)}) collective-permute-start(bf16[4,16,512]{2,1,0:T(8,128)(2,1)S(1)} %get-tuple-element.39), channel_id=1, source_target_pairs={{0,32},{32,64},{64,96},{96,128},{128,160},{160,192},{192,224},{224... | collective-permute-start | bytes 196616 | tf_op jit(solution)/shard_map/ppermute | solution.py:378
  22.2 0.0 copy-done.6
  22.2 0.1 fusion
  22.3 0.2 collective-permute-done.2
  22.5 1.6 collective-permute-done.1
  24.1 0.1 pad_maximum_fusion.2
  24.2 0.1 pad_maximum_fusion.1
  24.3 7.9 %collective-permute-start.3 = (bf16[96,512]{1,0:T(8,128)(2,1)S(1)}, bf16[96,512]{1,0:T(8,128)(2,1)S(1)}, u32[]{:S(2)}, u32[]{:S(2)}) collective-permute-start(bf16[96,512]{1,0:T(8,128)(2,1)S(1)} %reshape.68), channel_id=1, source_target_pairs={{0,1},{1,2},{2,3},{3,4},{4,5},{5,6},{6,7},{7,8},{8,9},{9,10},{10,1... | collective-permute-start | bytes 294920 | tf_op jit(solution)/shard_map/ppermute | solution.py:399
  32.3 2.4 %collective-permute-start.4 = (bf16[96,512]{1,0:T(8,128)(2,1)S(1)}, bf16[96,512]{1,0:T(8,128)(2,1)S(1)}, u32[]{:S(2)}, u32[]{:S(2)}) collective-permute-start(bf16[96,512]{1,0:T(8,128)(2,1)S(1)} %reshape.69), channel_id=1, source_target_pairs={{1,0},{2,1},{3,2},{4,3},{5,4},{6,5},{7,6},{8,7},{9,8},{10,9},{11,1... | collective-permute-start | bytes 294920 | tf_op jit(solution)/shard_map/ppermute | solution.py:400
  34.6 0.1 pad_add_fusion.at_ref
  34.7 0.3 collective-permute-done.3.left_ref
  35.0 1.8 %collective-permute-done.4.right_ref = bf16[96,512]{1,0:T(8,128)(2,1)S(1)} collective-permute-done((bf16[96,512]{1,0:T(8,128)(2,1)S(1)}, bf16[96,512]{1,0:T(8,128)(2,1)S(1)}, u32[]{:S(2)}, u32[]{:S(2)}) %collective-permute-start.4) | collective-permute-done | bytes 98336 | tf_op jit(solution)/shard_map/ppermute | solution.py:400
  36.8 0.0 copy-done.9
  36.8 0.0 copy-done.10
  36.8 4.4 %front.1.mixed_ref = bf16[256,512]{1,0:T(8,128)(2,1)S(1)} custom-call(s32[4]{0:T(128)S(1)} %pad_add_fusion.at_ref, bf16[256,512]{1,0:T(8,128)(2,1)S(1)} %bitcast.29, bf16[64,512]{1,0:T(8,128)(2,1)S(1)} %bitcast.31, bf16[64,512]{1,0:T(8,128)(2,1)S(1)} %bitcast.30, bf16[96,512]{1,0:T(8,128)(2,1)S(1)} %collective-permute-done.3.left_ref, ...), custom_call_target="tpu_custom_call" | custom-call | flops 4000000000 | bytes 3000000 | tf_op jit(solution)/shard_map/front/pallas_call | solution.py:329
  41.2 0.0 collective-permute-done.got_ref
  41.2 0.0 copy-start.11
  41.2 0.7 copy-done.11
  41.9 1.0 copy-done.12
  42.9 1.6 grad_slots.1
  44.5 10.8 %all-to-all-start.1 = ((bf16[32,24,512]{2,1,0:T(8,128)(2,1)}), bf16[32,24,512]{2,1,0:T(8,128)(2,1)S(1)}, u32[]{:S(2)}, u32[]{:S(2)}) async-start(bf16[32,24,512]{2,1,0:T(8,128)(2,1)} %bitcast.10), calls=%async_computation.1 | async-start | bytes 1572864 | tf_op jit(solution)/shard_map/all_to_all | solution.py:375
  55.3 0.0 reduce-scatter.2.cloned.1.call-start
  55.3 4.0 %collective-permute-start.5 = (bf16[256,512]{1,0:T(8,128)(2,1)S(1)}, bf16[256,512]{1,0:T(8,128)(2,1)S(1)}, u32[]{:S(2)}, u32[]{:S(2)}) collective-permute-start(bf16[256,512]{1,0:T(8,128)(2,1)S(1)} %front.1.mixed_ref), channel_id=1, source_target_pairs={{0,32},{1,481},{2,34},{3,483},{4,36},{5,485},{6,38},{7,487},{8,40}... | collective-permute-start | bytes 786440 | tf_op jit(solution)/shard_map/ppermute | solution.py:371
  59.3 13.8 %collective-permute-done.5.got_ref = bf16[256,512]{1,0:T(8,128)(2,1)S(1)} collective-permute-done((bf16[256,512]{1,0:T(8,128)(2,1)S(1)}, bf16[256,512]{1,0:T(8,128)(2,1)S(1)}, u32[]{:S(2)}, u32[]{:S(2)}) %collective-permute-start.5) | collective-permute-done | bytes 262176 | tf_op jit(solution)/shard_map/ppermute | solution.py:371
  73.1 0.6 token_slots.1
  73.7 0.0 all-to-all-done.1
  73.7 0.0 copy-start.13
  73.7 23.8 %all_to_all.20 = bf16[32,24,512]{2,1,0:T(8,128)(2,1)} all-to-all(bf16[32,24,512]{2,1,0:T(8,128)(2,1)S(1)} %bitcast.27), channel_id=1, replica_groups=mesh['rep'=16,'exp'=32] {'exp'}, dimensions={0} | all-to-all | bytes 1572864 | tf_op jit(solution)/shard_map/all_to_all | solution.py:375
  97.5 7.9 %middle.1 = (bf16[8,256,512]{2,1,0:T(8,128)(2,1)}, bf16[1024,768]{1,0:T(8,128)(2,1)}, bf16[1024,768]{1,0:T(8,128)(2,1)}) custom-call(bf16[8,2,128,512]{3,2,1,0:T(8,128)(2,1)} %bitcast.18, bf16[768,512]{1,0:T(8,128)(2,1)} %bitcast.34, bf16[768,512]{1,0:T(8,128)(2,1)} %bitcast.33), custom_call_target="tpu_custom_call" | custom-call | flops 3221225472 | bytes 7340032 | tf_op jit(solution)/shard_map/middle/pallas_call | solution.py:155
  105.4 0.0 reduce-scatter.2.cloned.1.call-update
  105.4 1.6 copy-done
  107.0 1.4 copy-done.4
  108.4 1.5 back.2
  110.0 0.0 copy-start.2
  110.0 0.9 copy-done.2
  110.8 6.4 %all-to-all-start.2 = ((bf16[32,24,512]{2,1,0:T(8,128)(2,1)}), bf16[32,24,512]{2,1,0:T(8,128)(2,1)S(1)}, u32[]{:S(2)}, u32[]{:S(2)}) async-start(bf16[32,24,512]{2,1,0:T(8,128)(2,1)} %bitcast.26), calls=%async_computation.2 | async-start | bytes 1572864 | tf_op jit(solution)/shard_map/all_to_all | solution.py:375
  117.2 0.0 copy-start.3
  117.3 1.5 copy-done.3
  118.7 1.5 back.3
  120.3 0.9 copy-done.1
  121.2 8.2 %all-to-all-done.2 = bf16[32,24,512]{2,1,0:T(8,128)(2,1)S(1)} async-done(((bf16[32,24,512]{2,1,0:T(8,128)(2,1)}), bf16[32,24,512]{2,1,0:T(8,128)(2,1)S(1)}, u32[]{:S(2)}, u32[]{:S(2)}) %all-to-all-start.2) | async-done | bytes 786464 | tf_op jit(solution)/shard_map/all_to_all | solution.py:375
  129.3 6.4 %all-to-all-start.3 = ((bf16[32,24,512]{2,1,0:T(8,128)(2,1)}), bf16[32,24,512]{2,1,0:T(8,128)(2,1)S(1)}, u32[]{:S(2)}, u32[]{:S(2)}) async-start(bf16[32,24,512]{2,1,0:T(8,128)(2,1)} %bitcast.25), calls=%async_computation.3 | async-start | bytes 1572864 | tf_op jit(solution)/shard_map/all_to_all | solution.py:375
  135.7 0.4 back_rows.2
  136.1 1.9 %collective-permute-start.6 = (bf16[256,512]{1,0:T(8,128)(2,1)S(1)}, bf16[256,512]{1,0:T(8,128)(2,1)S(1)}, u32[]{:S(2)}, u32[]{:S(2)}) collective-permute-start(bf16[256,512]{1,0:T(8,128)(2,1)S(1)} %back_rows.2), channel_id=1, source_target_pairs={{0,32},{1,481},{2,34},{3,483},{4,36},{5,485},{6,38},{7,487},{8,40}... | collective-permute-start | bytes 786440 | tf_op jit(solution)/shard_map/ppermute | solution.py:371
  138.1 9.7 %all-to-all-done.3 = bf16[32,24,512]{2,1,0:T(8,128)(2,1)S(1)} async-done(((bf16[32,24,512]{2,1,0:T(8,128)(2,1)}), bf16[32,24,512]{2,1,0:T(8,128)(2,1)S(1)}, u32[]{:S(2)}, u32[]{:S(2)}) %all-to-all-start.3) | async-done | bytes 786464 | tf_op jit(solution)/shard_map/all_to_all | solution.py:375
  147.8 6.0 %collective-permute-done.6.got_out_ref = bf16[256,512]{1,0:T(8,128)(2,1)S(1)} collective-permute-done((bf16[256,512]{1,0:T(8,128)(2,1)S(1)}, bf16[256,512]{1,0:T(8,128)(2,1)S(1)}, u32[]{:S(2)}, u32[]{:S(2)}) %collective-permute-start.6) | collective-permute-done | bytes 262176 | tf_op jit(solution)/shard_map/ppermute | solution.py:371
  153.8 0.4 back_rows.3
  154.2 2.2 %collective-permute-start.7 = (bf16[256,512]{1,0:T(8,128)(2,1)S(1)}, bf16[256,512]{1,0:T(8,128)(2,1)S(1)}, u32[]{:S(2)}, u32[]{:S(2)}) collective-permute-start(bf16[256,512]{1,0:T(8,128)(2,1)S(1)} %back_rows.3), channel_id=1, source_target_pairs={{0,32},{1,481},{2,34},{3,483},{4,36},{5,485},{6,38},{7,487},{8,40}... | collective-permute-start | bytes 786440 | tf_op jit(solution)/shard_map/ppermute | solution.py:371
  156.4 10.8 %collective-permute-done.7.got_in_ref = bf16[256,512]{1,0:T(8,128)(2,1)S(1)} collective-permute-done((bf16[256,512]{1,0:T(8,128)(2,1)S(1)}, bf16[256,512]{1,0:T(8,128)(2,1)S(1)}, u32[]{:S(2)}, u32[]{:S(2)}) %collective-permute-start.7) | collective-permute-done | bytes 262176 | tf_op jit(solution)/shard_map/ppermute | solution.py:371
  167.2 1.3 combine.1
  168.6 0.9 reduce-scatter.2.cloned.1.call-done.sum_ref
  169.5 0.9 copy-done.7
  170.4 0.8 gradients.1
  (15 shorter events, 0.1 us)
Async XLA Ops:
  7.2 90.3 %all-gather.3.cloned.1.call-start = ((), (), s32[]{:S(2)}) async-start(), calls=%async_computation.6 | async-start | bytes 2359296 | tf_op jit(solution)/shard_map/all_gather | solution.py:386
  8.0 1.0 copy-start.5
  9.0 0.7 copy-start.8
  9.6 12.6 %copy-start.6 = (bf16[16,16,512]{2,1,0:T(8,128)(2,1)S(1)}, bf16[16,16,512]{2,1,0:T(8,128)(2,1)}, u32[]{:S(2)}) copy-start(bf16[16,16,512]{2,1,0:T(8,128)(2,1)} %param.8) | copy-start | bytes 786436
  9.6 27.2 %copy-start.9 = (bf16[512,1536]{1,0:T(8,128)(2,1)S(1)}, bf16[512,1536]{1,0:T(8,128)(2,1)}, u32[]{:S(2)}) copy-start(bf16[512,1536]{1,0:T(8,128)(2,1)} %wqkv_ref.1) | copy-start | bytes 4718596
  9.6 27.2 %copy-start.10 = (bf16[512,512]{1,0:T(8,128)(2,1)S(1)}, bf16[512,512]{1,0:T(8,128)(2,1)}, u32[]{:S(2)}) copy-start(bf16[512,512]{1,0:T(8,128)(2,1)} %wproj_ref.1) | copy-start | bytes 1572868
  11.6 29.6 %collective-permute-start = (bf16[272,512]{1,0:T(8,128)(2,1)S(1)}, bf16[272,512]{1,0:T(8,128)(2,1)S(1)}, u32[]{:S(2)}, u32[]{:S(2)}) collective-permute-start(bf16[272,512]{1,0:T(8,128)(2,1)S(1)} %upstream.1.give_ref), channel_id=1, source_target_pairs={{0,32},{1,481},{2,34},{3,483},{4,36},{5,485},{6,38},{7,487},{8,40}... | collective-permute-start | bytes 835592 | tf_op jit(solution)/shard_map/ppermute | solution.py:371
  16.3 6.2 %collective-permute-start.2 = (bf16[4,16,512]{2,1,0:T(8,128)(2,1)S(1)}, bf16[4,16,512]{2,1,0:T(8,128)(2,1)S(1)}, u32[]{:S(2)}, u32[]{:S(2)}) collective-permute-start(bf16[4,16,512]{2,1,0:T(8,128)(2,1)S(1)} %get-tuple-element.38), channel_id=1, source_target_pairs={{32,0},{64,32},{96,64},{128,96},{160,128},{192,160},{224,192},{256... | collective-permute-start | bytes 196616 | tf_op jit(solution)/shard_map/ppermute | solution.py:379
  17.6 6.4 %collective-permute-start.1 = (bf16[4,16,512]{2,1,0:T(8,128)(2,1)S(1)}, bf16[4,16,512]{2,1,0:T(8,128)(2,1)S(1)}, u32[]{:S(2)}, u32[]{:S(2)}) collective-permute-start(bf16[4,16,512]{2,1,0:T(8,128)(2,1)S(1)} %get-tuple-element.39), channel_id=1, source_target_pairs={{0,32},{32,64},{64,96},{96,128},{128,160},{160,192},{192,224},{224... | collective-permute-start | bytes 196616 | tf_op jit(solution)/shard_map/ppermute | solution.py:378
  24.3 10.6 %collective-permute-start.3 = (bf16[96,512]{1,0:T(8,128)(2,1)S(1)}, bf16[96,512]{1,0:T(8,128)(2,1)S(1)}, u32[]{:S(2)}, u32[]{:S(2)}) collective-permute-start(bf16[96,512]{1,0:T(8,128)(2,1)S(1)} %reshape.68), channel_id=1, source_target_pairs={{0,1},{1,2},{2,3},{3,4},{4,5},{5,6},{6,7},{7,8},{8,9},{9,10},{10,1... | collective-permute-start | bytes 294920 | tf_op jit(solution)/shard_map/ppermute | solution.py:399
  32.3 4.6 %collective-permute-start.4 = (bf16[96,512]{1,0:T(8,128)(2,1)S(1)}, bf16[96,512]{1,0:T(8,128)(2,1)S(1)}, u32[]{:S(2)}, u32[]{:S(2)}) collective-permute-start(bf16[96,512]{1,0:T(8,128)(2,1)S(1)} %reshape.69), channel_id=1, source_target_pairs={{1,0},{2,1},{3,2},{4,3},{5,4},{6,5},{7,6},{8,7},{9,8},{10,9},{11,1... | collective-permute-start | bytes 294920 | tf_op jit(solution)/shard_map/ppermute | solution.py:400
  41.2 0.7 copy-start.11
  41.9 1.0 copy-start.12
  44.5 29.2 %all-to-all-start.1 = ((bf16[32,24,512]{2,1,0:T(8,128)(2,1)}), bf16[32,24,512]{2,1,0:T(8,128)(2,1)S(1)}, u32[]{:S(2)}, u32[]{:S(2)}) async-start(bf16[32,24,512]{2,1,0:T(8,128)(2,1)} %bitcast.10), calls=%async_computation.1 | async-start | bytes 1572864 | tf_op jit(solution)/shard_map/all_to_all | solution.py:375
  55.3 114.2 %reduce-scatter.2.cloned.1.call-start = ((), (), s32[]{:S(2)}) async-start(), calls=%async_computation.5 | async-start | bytes 2359296 | tf_op jit(solution)/shard_map/reduce_scatter | solution.py:434
  55.3 17.8 %collective-permute-start.5 = (bf16[256,512]{1,0:T(8,128)(2,1)S(1)}, bf16[256,512]{1,0:T(8,128)(2,1)S(1)}, u32[]{:S(2)}, u32[]{:S(2)}) collective-permute-start(bf16[256,512]{1,0:T(8,128)(2,1)S(1)} %front.1.mixed_ref), channel_id=1, source_target_pairs={{0,32},{1,481},{2,34},{3,483},{4,36},{5,485},{6,38},{7,487},{8,40}... | collective-permute-start | bytes 786440 | tf_op jit(solution)/shard_map/ppermute | solution.py:371
  73.7 23.8 %copy-start.13 = (bf16[32,24,512]{2,1,0:T(8,128)(2,1)}, bf16[32,24,512]{2,1,0:T(8,128)(2,1)S(1)}, u32[]{:S(2)}) copy-start(bf16[32,24,512]{2,1,0:T(8,128)(2,1)S(1)} %all-to-all-done.1) | copy-start | bytes 2359300
  105.4 1.6 copy-start
  107.0 1.4 copy-start.4
  110.0 0.9 copy-start.2
  110.8 18.5 %all-to-all-start.2 = ((bf16[32,24,512]{2,1,0:T(8,128)(2,1)}), bf16[32,24,512]{2,1,0:T(8,128)(2,1)S(1)}, u32[]{:S(2)}, u32[]{:S(2)}) async-start(bf16[32,24,512]{2,1,0:T(8,128)(2,1)} %bitcast.26), calls=%async_computation.2 | async-start | bytes 1572864 | tf_op jit(solution)/shard_map/all_to_all | solution.py:375
  117.2 1.5 copy-start.3
  120.3 0.9 copy-start.1
  129.3 18.5 %all-to-all-start.3 = ((bf16[32,24,512]{2,1,0:T(8,128)(2,1)}), bf16[32,24,512]{2,1,0:T(8,128)(2,1)S(1)}, u32[]{:S(2)}, u32[]{:S(2)}) async-start(bf16[32,24,512]{2,1,0:T(8,128)(2,1)} %bitcast.25), calls=%async_computation.3 | async-start | bytes 1572864 | tf_op jit(solution)/shard_map/all_to_all | solution.py:375
  136.1 17.7 %collective-permute-start.6 = (bf16[256,512]{1,0:T(8,128)(2,1)S(1)}, bf16[256,512]{1,0:T(8,128)(2,1)S(1)}, u32[]{:S(2)}, u32[]{:S(2)}) collective-permute-start(bf16[256,512]{1,0:T(8,128)(2,1)S(1)} %back_rows.2), channel_id=1, source_target_pairs={{0,32},{1,481},{2,34},{3,483},{4,36},{5,485},{6,38},{7,487},{8,40}... | collective-permute-start | bytes 786440 | tf_op jit(solution)/shard_map/ppermute | solution.py:371
  154.2 13.0 %collective-permute-start.7 = (bf16[256,512]{1,0:T(8,128)(2,1)S(1)}, bf16[256,512]{1,0:T(8,128)(2,1)S(1)}, u32[]{:S(2)}, u32[]{:S(2)}) collective-permute-start(bf16[256,512]{1,0:T(8,128)(2,1)S(1)} %back_rows.3), channel_id=1, source_target_pairs={{0,32},{1,481},{2,34},{3,483},{4,36},{5,485},{6,38},{7,487},{8,40}... | collective-permute-start | bytes 786440 | tf_op jit(solution)/shard_map/ppermute | solution.py:371
  169.5 0.9 copy-start.7
Sparse Core Ops, SparseCore 0:
  11.7 69.5 all-gather.2
  105.5 63.9 reduce-scatter.1
